TPU v7x, 32 devices: a whole 2x2x4 slice. The times are simulated.
32 devices in a mesh: rep: 2 (over x), fsdp: 16 (over z, y, core).
Axes of the slice: x: 2, y: 2, z: 4, core: 2. Of those that a mesh axis runs over, the one named last changes fastest.
Arguments:
- inputs: bfloat16 [2, 2048, 7168], P('rep', 'fsdp'), may hold values from -6 to 6
- cotangent: bfloat16 [2, 2048, 7168], P('rep', 'fsdp'), may hold values from -6 to 6
- weights: float32 [2, 2, 3584, 128], P('rep', None, 'fsdp'), may hold values from -6 to 6
- first_moment: float32 [2, 2, 3584, 128], P('rep', None, 'fsdp'), may hold values from -0.015625 to 0.015625
- second_moment: float32 [2, 2, 3584, 128], P('rep', None, 'fsdp'), may hold values from 1e-08 to 1e-05
- anchor: float32 [3584, 128], P('fsdp'), may hold values from -6 to 6
- momentum: float32 [3584, 128], P('fsdp'), may hold values from -4 to 4
- fragment: int32 [1], replicated, may hold values from 1 to 64
Outputs:
- new_weights: float32 [2, 2, 3584, 128], P('rep', None, 'fsdp')
- new_anchor: float32 [3584, 128], P('fsdp')
- new_momentum: float32 [3584, 128], P('fsdp')
All inputs are finite; a program needn't handle non-finite values.
Results may differ from a plain program's by a relative error of at most 0.0022.
Values may be sent and summed in bfloat16 or wider, within the bound.
No kernel may reach another device: no remote copies, remote signals or barrier semaphores. Data moves between devices by JAX's collectives and lax.ppermute only.
A program may use at most 64 MiB of HBM per device.

v0:
```python
import math

import jax
import jax.numpy as jnp
from jax import lax
from jax.sharding import PartitionSpec as P

norm_eps = 1e-05
beta_one = 0.9
beta_two = 0.95
adam_eps = 1e-08
decay_rate = 0.1
inner_rate = 0.05
outer_rate = 0.7
outer_beta = 0.9
mixing = 0.5


def layer_forward(hidden_in, w_in, w_out):
    inputs_f32 = hidden_in.astype(jnp.float32)
    inv_rms = lax.rsqrt(jnp.mean(inputs_f32 * inputs_f32, axis=-1, keepdims=True) + norm_eps)
    normed = (inputs_f32 * inv_rms).astype(jnp.bfloat16)
    in_scale = w_in.shape[1] ** (-0.5)
    out_scale = w_out.shape[0] ** (-0.5)
    pre_act = (
        lax.dot_general(normed, w_in, (((1,), (1,)), ((), ())), preferred_element_type=jnp.float32)
        * in_scale
    )
    activated = jax.nn.silu(pre_act).astype(jnp.bfloat16)
    layer_out = (
        inputs_f32 + jnp.dot(activated, w_out, preferred_element_type=jnp.float32) * out_scale
    ).astype(jnp.bfloat16)
    return (layer_out, (inputs_f32, inv_rms, normed, pre_act, activated))


def layer_backward(grad_out, w_in, w_out, saved, need_input):
    inputs_f32, inv_rms, normed, pre_act, activated = saved
    in_scale = w_in.shape[1] ** (-0.5)
    out_scale = w_out.shape[0] ** (-0.5)
    grad_w_out = (
        lax.dot_general(
            activated, grad_out, (((0,), (0,)), ((), ())), preferred_element_type=jnp.float32
        )
        * out_scale
    )
    grad_act = (
        lax.dot_general(
            grad_out, w_out, (((1,), (1,)), ((), ())), preferred_element_type=jnp.float32
        )
        * out_scale
    )
    sigmoid_pre = jax.nn.sigmoid(pre_act)
    grad_pre = (grad_act * sigmoid_pre * (1.0 + pre_act * (1.0 - sigmoid_pre))).astype(jnp.bfloat16)
    grad_w_in = (
        lax.dot_general(
            grad_pre, normed, (((0,), (0,)), ((), ())), preferred_element_type=jnp.float32
        )
        * in_scale
    )
    if not need_input:
        return (grad_w_in, grad_w_out, grad_out)
    grad_norm = jnp.dot(grad_pre, w_in, preferred_element_type=jnp.float32) * in_scale
    inner_sum = jnp.sum(grad_norm * inputs_f32, axis=-1, keepdims=True) / inputs_f32.shape[1]
    grad_in = (
        grad_out.astype(jnp.float32)
        + inv_rms * grad_norm
        - inputs_f32 * (inv_rms * inv_rms * inv_rms) * inner_sum
    )
    return (grad_w_in, grad_w_out, grad_in.astype(jnp.bfloat16))


def outer_step(total, base, velocity, replicas):
    mean_delta = total / replicas
    new_velocity = outer_beta * velocity + mean_delta
    new_global = base - outer_rate * (mean_delta + outer_beta * new_velocity)
    return (new_global, new_velocity)


def shards(inputs, cotangent, weights, first_moment, second_moment, anchor, momentum, fragment):
    tokens = inputs[0]
    upstream = cotangent[0]
    params = weights[0]
    layers = params.shape[0]
    model_width = tokens.shape[1]
    groups = lax.axis_size("fsdp")
    flat_rows = params.shape[1] * groups
    hidden = flat_rows * 128 // (2 * model_width)
    compact = params.astype(jnp.bfloat16)
    gathered_all = lax.all_gather(compact, "fsdp", axis=1, tiled=True).reshape(
        layers, 2, hidden, model_width
    )
    pairs = []
    saved_list = []
    current = tokens
    for layer_index in range(layers):
        weight_pair = gathered_all[layer_index]
        pairs.append(weight_pair)
        current, saved = layer_forward(current, weight_pair[0], weight_pair[1])
        saved_list.append(saved)
    partials = [None] * layers
    for layer_index in reversed(range(layers)):
        weight_pair = pairs[layer_index]
        grad_w_in, grad_w_out, upstream = layer_backward(
            upstream, weight_pair[0], weight_pair[1], saved_list[layer_index], layer_index > 0
        )
        term = jnp.stack([grad_w_in, grad_w_out]).reshape(flat_rows, 128)
        partials[layer_index] = term
    summed = lax.psum_scatter(jnp.stack(partials), "fsdp", scatter_dimension=1, tiled=True)
    gradient = summed / (tokens.shape[0] * groups)
    count = fragment[0]
    chosen = jnp.remainder(count, layers)
    count_real = count.astype(jnp.float32)
    correct_one = 1.0 - jnp.exp(count_real * math.log(beta_one))
    correct_two = 1.0 - jnp.exp(count_real * math.log(beta_two))
    moment_one = beta_one * first_moment[0] + (1.0 - beta_one) * gradient
    moment_two = beta_two * second_moment[0] + (1.0 - beta_two) * gradient * gradient
    updated = params - inner_rate * (
        moment_one / correct_one / (jnp.sqrt(moment_two / correct_two) + adam_eps)
        + decay_rate * params
    )
    pseudo = anchor - lax.dynamic_index_in_dim(params, chosen, 0, keepdims=False)
    replicas = lax.axis_size("rep")
    total = lax.psum(pseudo, "rep")
    new_global, new_velocity = outer_step(total, anchor, momentum, replicas)
    selector = (jnp.arange(layers, dtype=jnp.int32) == chosen)[:, None, None]
    merged = jnp.where(selector, mixing * updated + (1.0 - mixing) * new_global[None], updated)
    return (merged[None], new_global, new_velocity)


def solution(mesh):
    placed = (
        P("rep", "fsdp", None),
        P("rep", "fsdp", None),
        P("rep", None, "fsdp", None),
        P("rep", None, "fsdp", None),
        P("rep", None, "fsdp", None),
        P("fsdp", None),
        P("fsdp", None),
        P(),
    )
    return jax.shard_map(
        shards,
        mesh=mesh,
        in_specs=placed,
        out_specs=(P("rep", None, "fsdp", None), P("fsdp", None), P("fsdp", None)),
        check_vma=False,
    )
```

profile of v0, /device:TPU:0, one launch (start us, length us, event | category | flops | bytes accessed | tf_op | source)
XLA Modules:
  0.0 173.4 jit_solution(17458473633631358141)
XLA Ops:
  8.0 0.0 all-gather.2.cloned.1.call-start
  8.0 1.6 bitcast_convert_fusion
  9.6 0.0 all-gather.2.cloned.1.call-update
  9.7 0.0 all-reduce.2.cloned.1.call-start
  10.4 1.6 bitcast_subtract_fusion.1
  12.0 0.0 all-reduce.2.cloned.1.call-update
  12.0 0.0 reduce-scatter.2.cloned.1.call-start
  12.1 1.9 %fusion.9 = f32[128]{0:T(128)S(1)} fusion(bf16[1,128,7168]{2,1,0:T(8,128)(2,1)} %param.8), kind=kLoop, calls=%fused_computation.16 | loop fusion | flops 2752384 | bytes 1835520 | tf_op jit(solution)/shard_map/reduce_sum | solution.py:21
  14.0 41.0 %all-gather.2.cloned.1.call-done = bf16[2,3584,128]{2,1,0:T(8,128)(2,1)} async-done(((bf16[2,224,128]{2,1,0:T(8,128)(2,1)}), bf16[2,3584,128]{2,1,0:T(8,128)(2,1)}) %all-gather.2.cloned.1.call-update) | async-done | bytes 1835024 | tf_op jit(solution)/shard_map/all_gather | solution.py:89
  55.1 2.3 %fusion.54 = (bf16[1,1792,128]{2,1,0:T(8,128)(2,1)S(1)}, bf16[1,1792,128]{2,1,0:T(8,128)(2,1)}, bf16[1,1792,128]{2,1,0:T(8,128)(2,1)S(1)}, bf16[1,1792,128]{2,1,0:T(8,128)(2,1)S(1)}) fusion(bf16[2,3584,128]{2,1,0:T(8,128)(2,1)} %all-gather.2.cloned.1.call-done), kind=kLoop, calls=%fused_computation.78 | loop fusion | bytes 3670016 | tf_op jit(solution)/shard_map/slice | solution.py:104
  57.4 1.0 squeeze.36
  58.4 0.2 squeeze.37
  58.6 0.5 copy-done.1
  59.1 1.8 %fusion.21 = f32[128,32]{0,1:T(8,128)S(1)} fusion(bf16[32,7168]{1,0:T(8,128)(2,1)} %squeeze.36, bf16[1,128,7168]{2,1,0:T(8,128)(2,1)S(1)} %copy-done.1, f32[128]{0:T(128)S(1)} %add_rsqrt_fusion.1), kind=kOutput, calls=%fused_computation.33 | convolution fusion | flops 61476864 | bytes 2310656 | tf_op jit(solution)/shard_map/dot_general | solution.py:26
  60.9 2.7 %multiply_reduce_fusion.1 = (f32[128]{0:T(128)S(1)}, f32[128,7168]{1,0:T(8,128)}) fusion(bf16[32,7168]{1,0:T(8,128)(2,1)S(1)} %squeeze.37, f32[128,32]{0,1:T(8,128)S(1)} %fusion.21, bf16[1,128,7168]{2,1,0:T(8,128)(2,1)S(1)} %copy-done.1), kind=kOutput, calls=%fused_computation.23 | convolution fusion | flops 65163136 | bytes 5980672 | tf_op jit(solution)/shard_map/dot_general | solution.py:31
  63.6 1.2 squeeze.38
  64.8 1.0 squeeze.35
  65.8 3.0 %convolution_multiply_fusion.6 = f32[128,32]{0,1:T(8,128)S(1)} fusion(bf16[32,7168]{1,0:T(8,128)(2,1)S(1)} %squeeze.38, f32[128,7168]{1,0:T(8,128)} %get-tuple-element.13, f32[128]{0:T(128)S(1)} %get-tuple-element.7), kind=kOutput, calls=%fused_computation.40 | convolution fusion | flops 60559360 | bytes 4145664 | tf_op jit(solution)/shard_map/dot_general | solution.py:26
  68.7 0.0 copy-done.5
  68.7 2.2 %fusion.36 = bf16[128,32]{0,1:T(8,128)(2,1)S(1)} fusion(bf16[32,7168]{1,0:T(8,128)(2,1)S(1)} %copy-done.5, bf16[1,128,7168]{2,1,0:T(8,128)(2,1)} %param.9, f32[128,32]{0,1:T(8,128)S(1)} %convolution_multiply_fusion.6), kind=kOutput, calls=%fused_computation.42 | convolution fusion | flops 58761216 | bytes 2318336 | tf_op jit(solution)/shard_map/dot_general | solution.py:47
  71.0 0.0 copy-done
  71.0 0.0 copy-start.2
  71.0 0.7 multiply_reduce_fusion
  71.8 0.7 copy-done.2
  72.5 2.6 %subtract_convert_fusion = bf16[128,7168]{1,0:T(8,128)(2,1)} fusion(f32[128,7168]{1,0:T(8,128)S(1)} %copy-done, f32[128,7168]{1,0:T(8,128)S(1)} %get-tuple-element.15, bf16[1,128,7168]{2,1,0:T(8,128)(2,1)S(1)} %copy-done.2, f32[128]{0:T(128)S(1)} %get-tuple-element.17, f32[128]{0:T(128)S(1)} %get-tuple-element.16, f32[128]{0:T(128)S(1)} %get-tuple-element.6), kind=kLoop, calls=%fused_computation.20 | loop fusion | flops 6422528 | bytes 11011584 | tf_op jit(solution)/shard_map/convert_element_type | solution.py:69
  75.1 3.8 %fusion.3 = f32[1,32,7168]{2,1,0:T(8,128)} fusion(bf16[1,128,7168]{2,1,0:T(8,128)(2,1)S(1)} %copy-done.1, f32[128]{0:T(128)S(1)} %add_rsqrt_fusion.1, bf16[128,7168]{1,0:T(8,128)(2,1)} %subtract_convert_fusion, bf16[32,7168]{1,0:T(8,128)(2,1)S(1)} %squeeze.37, f32[128,32]{0,1:T(8,128)S(1)} %fusion.21), kind=kOutput, calls=%fused_computation.8 | convolution fusion | flops 120463360 | bytes 5063168 | tf_op jit(solution)/shard_map/dot_general | solution.py:55
  78.9 1.9 %fusion.4 = f32[1,32,7168]{2,1,0:T(8,128)S(1)} fusion(bf16[128,7168]{1,0:T(8,128)(2,1)} %subtract_convert_fusion, f32[128,32]{0,1:T(8,128)S(1)} %fusion.21), kind=kOutput, calls=%fused_computation.9 | convolution fusion | flops 58970112 | bytes 2768896 | tf_op jit(solution)/shard_map/dot_general | solution.py:41
  80.8 0.0 copy-start.3
  80.8 2.6 %fusion.5 = f32[1,32,7168]{2,1,0:T(8,128)S(1)} fusion(bf16[128,32]{0,1:T(8,128)(2,1)S(1)} %fusion.36, f32[128,7168]{1,0:T(8,128)} %get-tuple-element.13, f32[128]{0:T(128)S(1)} %get-tuple-element.7), kind=kOutput, calls=%fused_computation.10 | convolution fusion | flops 60784640 | bytes 4596224 | tf_op jit(solution)/shard_map/dot_general | solution.py:55
  83.4 0.0 copy-done.3
  83.4 0.0 copy-start.4
  83.4 1.3 fusion.6
  84.8 0.0 copy-done.4
  84.8 1.4 pad_maximum_fusion.1
  86.2 1.6 stack_reshape.6
  87.7 2.6 %pad_maximum_fusion.2 = f32[2,32,7168]{2,1,0:T(8,128)} fusion(f32[1,32,7168]{2,1,0:T(8,128)} %fusion.6, f32[1,32,7168]{2,1,0:T(8,128)S(1)} %fusion.5), kind=kLoop, calls=%fused_computation.27 | loop fusion | flops 458752 | bytes 3670016 | tf_op jit(solution)/shard_map/stack | solution.py:106
  90.3 2.7 %stack_reshape.7 = f32[1,3584,128]{2,1,0:T(8,128)} reshape(f32[2,32,7168]{2,1,0:T(8,128)} %pad_maximum_fusion.2) | data formatting | bytes 3670016 | tf_op jit(solution)/shard_map/stack;reshape | solution.py:108
  93.0 3.5 %pad_maximum_fusion = f32[2,3584,128]{2,1,0:T(8,128)} fusion(f32[1,3584,128]{2,1,0:T(8,128)} %stack_reshape.7, f32[1,3584,128]{2,1,0:T(8,128)S(1)} %stack_reshape.6), kind=kLoop, calls=%fused_computation.19 | loop fusion | flops 917504 | bytes 7340032 | tf_op jit(solution)/shard_map/stack | solution.py:108
  96.6 0.0 copy-start.9
  96.6 0.0 reduce-scatter.2.cloned.1.call-update
  96.7 0.0 all-reduce.2.cloned.1.call-done
  96.7 0.7 copy-done.7
  97.5 0.1 copy-done.10
  97.5 1.6 broadcast_multiply_fusion
  99.1 65.0 %reduce-scatter.2.cloned.1.call-done = f32[2,224,128]{2,1,0:T(8,128)} async-done(((f32[2,3584,128]{2,1,0:T(8,128)}), f32[2,224,128]{2,1,0:T(8,128)}) %reduce-scatter.2.cloned.1.call-update) | async-done | bytes 229392 | tf_op jit(solution)/shard_map/reduce_scatter | solution.py:108
  164.1 0.0 copy-done.6
  164.1 0.0 copy-done.8
  164.1 1.8 %select_bitcast_fusion = f32[1,2,224,128]{3,2,1,0:T(8,128)} fusion(f32[1,2,224,128]{3,2,1,0:T(8,128)S(1)} %copy-done.6, f32[2,224,128]{2,1,0:T(8,128)} %reduce-scatter.2.cloned.1.call-done, f32[1,2,224,128]{3,2,1,0:T(8,128)S(1)} %copy-done.8, f32[1,2,224,128]{3,2,1,0:T(8,128)S(1)} %copy-done.9, f32[224,128]{1,0:T(8,128)S(1)} %get-tuple-element.3, ...), kind=kLoop, calls=%fused_computation.54 | loop fusion | flops 1089536 | bytes 1261578 | tf_op jit(solution)/shard_map/broadcast_in_dim | solution.py:127
  (12 shorter events, 0.0 us)
Async XLA Ops:
  8.0 47.1 %all-gather.2.cloned.1.call-start = ((), (), s32[]{:S(2)}) async-start(), calls=%async_computation.1 | async-start | bytes 1949696 | tf_op jit(solution)/shard_map/all_gather | solution.py:89
  9.7 87.1 %all-reduce.2.cloned.1.call-start = ((), (), s32[]{:S(2)}) async-start(), calls=%async_computation.3 | async-start | bytes 229376 | tf_op jit(solution)/shard_map/psum | solution.py:123
  12.0 152.1 %reduce-scatter.2.cloned.1.call-start = ((), (), s32[]{:S(2)}) async-start(), calls=%async_computation.2 | async-start | bytes 3899392 | tf_op jit(solution)/shard_map/reduce_scatter | solution.py:108
  57.4 1.7 copy-start.1
  65.7 3.0 %copy-start.5 = (bf16[32,7168]{1,0:T(8,128)(2,1)S(1)}, bf16[32,7168]{1,0:T(8,128)(2,1)}, u32[]{:S(2)}) copy-start(bf16[32,7168]{1,0:T(8,128)(2,1)} %squeeze.35) | copy-start | bytes 1376260
  65.7 5.2 %copy-start = (f32[128,7168]{1,0:T(8,128)S(1)}, f32[128,7168]{1,0:T(8,128)}, u32[]{:S(2)}) copy-start(f32[128,7168]{1,0:T(8,128)} %get-tuple-element.13) | copy-start | bytes 11010052
  71.0 1.5 copy-start.2
  80.8 2.6 %copy-start.3 = (bf16[1,128,7168]{2,1,0:T(8,128)(2,1)S(1)}, bf16[1,128,7168]{2,1,0:T(8,128)(2,1)}, u32[]{:S(2)}) copy-start(bf16[1,128,7168]{2,1,0:T(8,128)(2,1)} %param.9) | copy-start | bytes 5505028
  83.4 1.3 copy-start.4
  96.6 0.9 copy-start.7
  96.6 1.0 copy-start.10
  96.6 67.5 %copy-start.6 = (f32[1,2,224,128]{3,2,1,0:T(8,128)S(1)}, f32[1,2,224,128]{3,2,1,0:T(8,128)}, u32[]{:S(2)}) copy-start(f32[1,2,224,128]{3,2,1,0:T(8,128)} %param.10) | copy-start | bytes 688132
  96.6 67.5 %copy-start.8 = (f32[1,2,224,128]{3,2,1,0:T(8,128)S(1)}, f32[1,2,224,128]{3,2,1,0:T(8,128)}, u32[]{:S(2)}) copy-start(f32[1,2,224,128]{3,2,1,0:T(8,128)} %param.12) | copy-start | bytes 688132
  96.6 67.5 %copy-start.9 = (f32[1,2,224,128]{3,2,1,0:T(8,128)S(1)}, f32[1,2,224,128]{3,2,1,0:T(8,128)}, u32[]{:S(2)}) copy-start(f32[1,2,224,128]{3,2,1,0:T(8,128)} %param.11) | copy-start | bytes 688132
Sparse Core Ops, SparseCore 0:
  11.7 43.3 all-gather.1
  96.7 67.3 reduce-scatter.1
Sparse Core Ops, SparseCore 1:
  13.1 23.6 all-reduce.1
where the time goes:
time: 174 us; the launch traced here: 173 us
  waiting for transfers between devices  106 us (61%)
  matrix products  20.1 us (12%)
  other arithmetic  18.7 us (11%)
  between operations  16.4 us (9%)
  local copies, waits for them, and re-layouts  12 us (7%)
    reduce_scatter x1, waiting for transfers between devices, shards(): lax.psum_scatter(jnp.stack(partials), 'fsdp', scatter_dimension=1, tiled=...  65 us
    all_gather x1, waiting for transfers between devices, shards(): lax.all_gather(compact, 'fsdp', axis=1, tiled=True)  41 us
    dot_general x2, matrix products, layer_backward(): lax.dot_general(grad_pre, normed, (((0,), (0,)), ((), ())), preferred_ele...  6.47 us
    dot_general x2, matrix products, layer_forward(): lax.dot_general(normed, w_in, (((1,), (1,)), ((), ())), preferred_element...  4.77 us
    another operation x2, local copies, waits for them, and re-layouts, shards(): jnp.stack(partials)  4.29 us
    another operation x2, other arithmetic, shards(): term = jnp.stack([grad_w_in, grad_w_out]).reshape(flat_rows, 128)  3.96 us
    another operation x1, other arithmetic, shards(): jnp.stack(partials)  3.54 us
  transfers between devices with their start and end apart: 3, of which 2 were waited for; matrix products, arithmetic and copies ran while one was open for 26% of the time, Pallas kernels for 0%

commit v1 on v0

v1 whole, which is shorter than its diff:
```python
import functools
import math

import jax
import jax.numpy as jnp
from jax import lax
from jax.experimental import pallas as pl
from jax.experimental.pallas import tpu as pltpu
from jax.sharding import PartitionSpec as P

norm_eps = 1e-05
beta_one = 0.9
beta_two = 0.95
adam_eps = 1e-08
decay_rate = 0.1
inner_rate = 0.05
outer_rate = 0.7
outer_beta = 0.9
mixing = 0.5
ROWS = 8


def swap(value, axis, mask):
    size = lax.axis_size(axis)
    return lax.ppermute(value, axis, [(i, i ^ mask) for i in range(size)])


def gather_blocks(own, axis, early):
    size = lax.axis_size(axis)
    tops = range(4, size, 4)
    have = {0: own}

    def take(k):
        have[k] = swap(have[k & (k - 1)], axis, k & -k)

    for k in tops:
        if k & (k - 1) == 0:
            take(k)
        if k == 4:
            take(2)
    take(1)
    for k in tops:
        if k in have:
            have[k], early = lax.optimization_barrier((have[k], early))
    for k in tops:
        if k not in have:
            take(k)
        take(k + 2)
    for k in range(3, size, 2):
        take(k)
    return [have[k] for k in range(size)], early


def add_f32(left, right):
    return left.astype(jnp.float32) + right.astype(jnp.float32)


def reduce_blocks(blocks, odd_sets, axis):
    size = lax.axis_size(axis)
    left = dict(blocks)
    for ks, terms in odd_sets:
        came = swap(terms, axis, 1)
        for place, k in enumerate(ks):
            left[k - 1] = add_f32(left[k - 1], came[place])
    bit = 2
    while bit < size:
        for k in sorted(left, reverse=True):
            if k & bit:
                part = left.pop(k)
                left[k ^ bit] = left[k ^ bit] + swap(part.astype(jnp.bfloat16), axis, bit).astype(jnp.float32)
        bit *= 2
    return left[0]


def output_sets(size):
    odd = list(range(size - 1, 0, -2))
    sends = [k for k in odd if k & 2]
    return [sends[:1], sends[1:], [k for k in odd if not k & 2], list(range(0, size, 2))]


def dot_nt(left, right):
    return lax.dot_general(left, right, (((1,), (1,)), ((), ())), preferred_element_type=jnp.float32)


def dot_nn(left, right):
    return jnp.dot(left, right, preferred_element_type=jnp.float32)


def adapter_kernel(n_pieces, places, units, width, *refs):
    upper_ref, normed0, h0, g2 = refs[:4]
    pieces = refs[4 : 4 + n_pieces]
    outs = refs[4 + n_pieces : -4]
    w_ref, h1, normed1, g1 = refs[-4:]
    tokens, model_width = h0.shape
    stacked = n_pieces * ROWS // 2
    hidden = stacked // 2
    in_scale = model_width ** (-0.5)
    out_scale = hidden ** (-0.5)
    steps = model_width // width
    upper = upper_ref[0]
    half = n_pieces // 2
    layer_of = (lax.broadcasted_iota(jnp.int32, (tokens, stacked), 1) % (2 * units)) // units
    zeros = jnp.zeros((tokens, stacked), jnp.float32)

    def cut(step):
        return pl.ds(pl.multiple_of(step * width, width), width)

    def first(step, carry):
        pre, grad = carry
        at = cut(step)
        for side in range(2):
            parts = [pieces[side * half + j][:, at].astype(jnp.float32) for j in range(half)]
            w_ref[side ^ upper, :, at] = jnp.concatenate(parts).astype(jnp.bfloat16)
        pre = pre + dot_nt(normed0[:, at], w_ref[0, :, at])
        grad = grad + dot_nt(g2[:, at], w_ref[1, :, at])
        return pre, grad

    pre0, grad_act1 = lax.fori_loop(0, steps, first, (zeros, zeros))
    pre0 = pre0 * in_scale
    sig0 = jax.nn.sigmoid(pre0)
    act0 = jnp.where(layer_of == 0, pre0 * sig0, 0.0)
    act0_low = act0.astype(jnp.bfloat16)

    def second(step, squares):
        at = cut(step)
        out = h0[:, at].astype(jnp.float32) + dot_nn(act0_low, w_ref[1, :, at]) * out_scale
        low = out.astype(jnp.bfloat16)
        h1[:, at] = low
        out = low.astype(jnp.float32)
        out = out * out
        for j in range(0, width, 128):
            squares = squares + out[:, j : j + 128]
        return squares

    squares = lax.fori_loop(0, steps, second, jnp.zeros((tokens, 128), jnp.float32))
    inv1 = lax.rsqrt(jnp.sum(squares, axis=1, keepdims=True) / model_width + norm_eps)

    def third(step, pre):
        at = cut(step)
        low = (h1[:, at].astype(jnp.float32) * inv1).astype(jnp.bfloat16)
        normed1[:, at] = low
        return pre + dot_nt(low, w_ref[0, :, at])

    pre1 = lax.fori_loop(0, steps, third, zeros) * in_scale
    sig1 = jax.nn.sigmoid(pre1)
    act1 = jnp.where(layer_of == 1, pre1 * sig1, 0.0)
    slope1 = sig1 * (1.0 + pre1 * (1.0 - sig1))
    gp1 = jnp.where(layer_of == 1, grad_act1 * out_scale * slope1, 0.0)
    gp1_low = gp1.astype(jnp.bfloat16)
    inner = jnp.sum(gp1_low.astype(jnp.float32) * pre1, axis=1, keepdims=True)
    coef = inv1 * inv1 * inner / model_width
    factor = inv1 * in_scale

    def fourth(step, grad):
        at = cut(step)
        value = (
            g2[:, at].astype(jnp.float32)
            + factor * dot_nn(gp1_low, w_ref[0, :, at])
            - coef * h1[:, at].astype(jnp.float32)
        )
        low = value.astype(jnp.bfloat16)
        g1[:, at] = low
        return grad + dot_nt(low, w_ref[1, :, at])

    grad_act0 = lax.fori_loop(0, steps, fourth, zeros)
    slope0 = sig0 * (1.0 + pre0 * (1.0 - sig0))
    gp0 = jnp.where(layer_of == 0, grad_act0 * out_scale * slope0, 0.0)
    act_t = jnp.concatenate([act0.T, act1.T], axis=1).astype(jnp.bfloat16)
    gp_t = jnp.concatenate([gp0.T, gp1.T], axis=1).astype(jnp.bfloat16)

    def fifth(step, carry):
        at = cut(step)
        grad_out = dot_nn(act_t, jnp.concatenate([g1[:, at], g2[:, at]])) * out_scale
        grad_in = dot_nn(gp_t, jnp.concatenate([normed0[:, at], normed1[:, at]])) * in_scale
        for side in range(2):
            term = jnp.where(upper == side, grad_in, grad_out)
            for j in range(half):
                k = side * half + j
                out, place = places[k]
                outs[out][place, :, at] = term[j * ROWS : (j + 1) * ROWS].astype(jnp.bfloat16)
        return carry

    lax.fori_loop(0, steps, fifth, 0)


def adapter_grads(upper, normed, tokens, upstream, pieces, units, sets):
    model_width = tokens.shape[1]
    n_pieces = len(pieces)
    width = 1792 if model_width % 1792 == 0 else 128
    stacked = n_pieces * ROWS // 2
    places = {k: (out, place) for out, ks in enumerate(sets) for place, k in enumerate(ks)}
    whole = pl.BlockSpec(memory_space=pltpu.VMEM)
    return pl.pallas_call(
        functools.partial(adapter_kernel, n_pieces, places, units, width),
        out_shape=[jax.ShapeDtypeStruct((len(ks), ROWS, model_width), jnp.bfloat16) for ks in sets],
        in_specs=[pl.BlockSpec(memory_space=pltpu.SMEM)] + [whole] * (3 + n_pieces),
        out_specs=[whole] * len(sets),
        scratch_shapes=[
            pltpu.VMEM((2, stacked, model_width), jnp.bfloat16),
            pltpu.VMEM(tokens.shape, jnp.bfloat16),
            pltpu.VMEM(tokens.shape, jnp.bfloat16),
            pltpu.VMEM(tokens.shape, jnp.bfloat16),
        ],
        compiler_params=pltpu.CompilerParams(vmem_limit_bytes=16 * 2**20),
    )(upper, normed, tokens, upstream, *pieces)


def shards(inputs, cotangent, weights, first_moment, second_moment, anchor, momentum, fragment):
    tokens = inputs[0]
    upstream = cotangent[0]
    params = weights[0]
    layers, rows = params.shape[0], params.shape[1]
    model_width = tokens.shape[1]
    groups = lax.axis_size("fsdp")
    units = rows * 128 // model_width
    upper = (lax.axis_index("fsdp") >= groups // 2).astype(jnp.int32).reshape(1)
    compact = params.astype(jnp.bfloat16).reshape(layers * units, model_width)
    inputs_f32 = tokens.astype(jnp.float32)
    inv_rms = lax.rsqrt(jnp.mean(inputs_f32 * inputs_f32, axis=-1, keepdims=True) + norm_eps)
    pieces, inv_rms = gather_blocks(compact, "fsdp", inv_rms)
    normed = (inputs_f32 * inv_rms).astype(jnp.bfloat16)
    per_piece = ROWS // (layers * units)
    if per_piece > 1:
        pieces = [jnp.concatenate(pieces[i : i + per_piece]) for i in range(0, groups, per_piece)]

    count = fragment[0]
    chosen = jnp.remainder(count, layers)
    replicas = lax.axis_size("rep")
    total = anchor - lax.dynamic_index_in_dim(params, chosen, 0, keepdims=False)
    step = 1
    while step < replicas:
        total = total + swap(total, "rep", step)
        step *= 2
    upper, total = lax.optimization_barrier((upper, total))

    sets = output_sets(groups)
    if per_piece == 1:
        outs = adapter_grads(upper, normed, tokens, upstream, pieces, units, sets)
    else:
        (both,) = adapter_grads(upper, normed, tokens, upstream, pieces, units, [list(range(len(pieces)))])
        both = both.reshape(groups, layers * units, model_width)
        outs = [jnp.stack([both[k] for k in ks]) for ks in sets]
    even = {k: outs[-1][place] for place, k in enumerate(sets[-1])}
    summed = reduce_blocks(even, list(zip(sets, outs))[:-1], "fsdp").reshape(layers, rows, 128)
    gradient = summed / (tokens.shape[0] * groups)
    count_real = count.astype(jnp.float32)
    correct_one = 1.0 - jnp.exp(count_real * math.log(beta_one))
    correct_two = 1.0 - jnp.exp(count_real * math.log(beta_two))
    moment_one = beta_one * first_moment[0] + (1.0 - beta_one) * gradient
    moment_two = beta_two * second_moment[0] + (1.0 - beta_two) * gradient * gradient
    updated = params - inner_rate * (
        moment_one / correct_one / (jnp.sqrt(moment_two / correct_two) + adam_eps)
        + decay_rate * params
    )
    mean_delta = total / replicas
    new_velocity = outer_beta * momentum + mean_delta
    new_global = anchor - outer_rate * (mean_delta + outer_beta * new_velocity)
    selector = (jnp.arange(layers, dtype=jnp.int32) == chosen)[:, None, None]
    merged = jnp.where(selector, mixing * updated + (1.0 - mixing) * new_global[None], updated)
    return (merged[None], new_global, new_velocity)


def solution(mesh):
    placed = (
        P("rep", "fsdp", None),
        P("rep", "fsdp", None),
        P("rep", None, "fsdp", None),
        P("rep", None, "fsdp", None),
        P("rep", None, "fsdp", None),
        P("fsdp", None),
        P("fsdp", None),
        P(),
    )
    return jax.shard_map(
        shards,
        mesh=mesh,
        in_specs=placed,
        out_specs=(P("rep", None, "fsdp", None), P("fsdp", None), P("fsdp", None)),
        check_vma=False,
    )
```

time: 174 us -> 63.4 us (0.36)
  waiting for transfers between devices: 106 us -> 22.4 us
  matrix products: 20.1 us -> 0 us
  starting transfers between devices: 0.12 us -> 19.2 us
  between operations: 16.4 us -> 1.65 us
  other arithmetic: 18.7 us -> 7.01 us
  Pallas kernels: 0 us -> 8.53 us
  local copies, waits for them, and re-layouts: 12 us -> 4.2 us
    reduce_scatter x1 -> x0, waiting for transfers between devices: 65 us -> none  [shards(): lax.psum_scatter(jnp.stack(partials), 'fsdp', scatter_dimension=1, tiled=...]
    all_gather x1 -> x0, waiting for transfers between devices: 41 us -> none  [shards(): lax.all_gather(compact, 'fsdp', axis=1, tiled=True)]
    ppermute x0 -> x26, waiting for transfers between devices: none -> 22.4 us  [swap(): return lax.ppermute(value, axis, [(i, i ^ mask) for i in range(size)])]
    dot_general x9 -> x0, matrix products: 20.1 us -> none  [the longest x2 6.47 us: layer_backward(): lax.dot_general(grad_pre, normed, (((0,), (0,)), ((), ())), preferred_ele...]
    ppermute x0 -> x26, starting transfers between devices: none -> 19.2 us  [swap(): return lax.ppermute(value, axis, [(i, i ^ mask) for i in range(size)])]
    pallas_call x0 -> x1, Pallas kernels: none -> 8.53 us  [adapter_grads(): pl.pallas_call(functools.partial(adapter_kernel, n_pieces, places, units,...]
    another operation x3 -> x0, other arithmetic: 7.49 us -> none  [the longest x2 3.96 us: shards(): term = jnp.stack([grad_w_in, grad_w_out]).reshape(flat_rows, 128)]
    another operation x2 -> x0, local copies, waits for them, and re-layouts: 4.29 us -> none  [shards(): jnp.stack(partials)]
  transfers between devices with their start and end apart: 3 -> 26, of which waited for: 2 -> 10; matrix products, arithmetic and copies ran while one was open for 26% -> 8% of each run, Pallas kernels for 0% -> 0%
where the time goes in v1:
time: 63.4 us; the launch traced here: 63 us
  waiting for transfers between devices  22.4 us (35%)
  starting transfers between devices  19.2 us (30%)
  Pallas kernels  8.53 us (13%)
  other arithmetic  7.01 us (11%)
  local copies, waits for them, and re-layouts  4.2 us (7%)
  between operations  1.65 us (3%)
    ppermute x26, waiting for transfers between devices, swap(): return lax.ppermute(value, axis, [(i, i ^ mask) for i in range(size)])  22.4 us
    ppermute x26, starting transfers between devices, swap(): return lax.ppermute(value, axis, [(i, i ^ mask) for i in range(size)])  19.2 us
    pallas_call x1, Pallas kernels, adapter_grads(): pl.pallas_call(functools.partial(adapter_kernel, n_pieces, places, units,...  8.53 us
    unnamed x32, local copies, waits for them, and re-layouts  4.06 us
    reduce_sum x1, other arithmetic, shards(): jnp.mean(inputs_f32 * inputs_f32, axis=-1, keepdims=True) + norm_eps  1.93 us
  transfers between devices with their start and end apart: 26, of which 10 were waited for; matrix products, arithmetic and copies ran while one was open for 8% of the time, Pallas kernels for 0%

profile of v1, /device:TPU:0, one launch (start us, length us, event | category | flops | bytes accessed | tf_op | source)
XLA Modules:
  0.0 63.0 jit_solution(17140596575040518267)
XLA Ops:
  0.6 1.1 %convert_element_type.136 = bf16[1,2,224,128]{3,2,1,0:T(8,128)(2,1)S(1)} convert(f32[1,2,224,128]{3,2,1,0:T(8,128)} %param.10) | non-fusion elementwise | flops 57344 | bytes 344064 | tf_op jit(solution)/shard_map/convert_element_type | solution.py:217
  1.8 3.1 %collective-permute-start.2 = (bf16[8,7168]{1,0:T(8,128)(2,1)S(1)}, bf16[8,7168]{1,0:T(8,128)(2,1)S(1)}, u32[]{:S(2)}, u32[]{:S(2)}) collective-permute-start(bf16[8,7168]{1,0:T(8,128)(2,1)S(1)} %convert_element_type.137.refs_4_), channel_id=1, source_target_pairs={{0,4},{1,5},{2,6},{3,7},{4,0},{5,1},{6,2},{7,3},{8,12},{9,13},{10,... | collective-permute-start | bytes 344072 | tf_op jit(solution)/shard_map/ppermute | solution.py:25
  4.9 2.6 %collective-permute-start.1 = (bf16[8,7168]{1,0:T(8,128)(2,1)S(1)}, bf16[8,7168]{1,0:T(8,128)(2,1)S(1)}, u32[]{:S(2)}, u32[]{:S(2)}) collective-permute-start(bf16[8,7168]{1,0:T(8,128)(2,1)S(1)} %convert_element_type.137.refs_4_), channel_id=1, source_target_pairs={{0,8},{1,9},{2,10},{3,11},{4,12},{5,13},{6,14},{7,15},{8,0},{9,1},... | collective-permute-start | bytes 344072 | tf_op jit(solution)/shard_map/ppermute | solution.py:25
  7.5 1.5 %collective-permute-start.4 = (bf16[8,7168]{1,0:T(8,128)(2,1)S(1)}, bf16[8,7168]{1,0:T(8,128)(2,1)S(1)}, u32[]{:S(2)}, u32[]{:S(2)}) collective-permute-start(bf16[8,7168]{1,0:T(8,128)(2,1)S(1)} %convert_element_type.137.refs_4_), channel_id=1, source_target_pairs={{0,2},{1,3},{2,0},{3,1},{4,6},{5,7},{6,4},{7,5},{8,10},{9,11},{10,... | collective-permute-start | bytes 344072 | tf_op jit(solution)/shard_map/ppermute | solution.py:25
  9.7 1.0 %bitcast_subtract_fusion = f32[224,128]{1,0:T(8,128)S(1)} fusion(f32[224,128]{1,0:T(8,128)} %param.13, f32[1,2,224,128]{3,2,1,0:T(8,128)} %param.10, s32[]{:T(128)S(6)} %select_n.17), kind=kLoop, calls=%fused_computation.24 | loop fusion | flops 28672 | bytes 344068 | tf_op jit(solution)/shard_map/sub | solution.py:229
  10.6 1.6 %collective-permute-start = (f32[224,128]{1,0:T(8,128)S(1)}, f32[224,128]{1,0:T(8,128)S(1)}, u32[]{:S(2)}, u32[]{:S(2)}) collective-permute-start(f32[224,128]{1,0:T(8,128)S(1)} %bitcast_subtract_fusion), channel_id=1, source_target_pairs={{0,16},{16,0},{1,17},{17,1},{2,18},{18,2},{3,19},{19,3},{4,20},{20... | collective-permute-start | bytes 344072 | tf_op jit(solution)/shard_map/ppermute | solution.py:25
  12.2 1.9 %fusion = f32[128]{0:T(128)S(1)} fusion(bf16[1,128,7168]{2,1,0:T(8,128)(2,1)} %param.8), kind=kLoop, calls=%fused_computation.2 | loop fusion | flops 2752384 | bytes 1835520 | tf_op jit(solution)/shard_map/reduce_sum | solution.py:219
  14.2 0.5 collective-permute-start.12
  14.7 0.5 collective-permute-start.10
  15.2 1.1 %collective-permute-done = f32[224,128]{1,0:T(8,128)S(1)} collective-permute-done((f32[224,128]{1,0:T(8,128)S(1)}, f32[224,128]{1,0:T(8,128)S(1)}, u32[]{:S(2)}, u32[]{:S(2)}) %collective-permute-start) | collective-permute-done | bytes 114720 | tf_op jit(solution)/shard_map/ppermute | solution.py:25
  16.3 0.5 collective-permute-start.7
  16.8 0.2 collective-permute-start.6
  17.0 2.5 %collective-permute-done.12.refs_16_ = bf16[8,7168]{1,0:T(8,128)(2,1)S(1)} collective-permute-done((bf16[8,7168]{1,0:T(8,128)(2,1)S(1)}, bf16[8,7168]{1,0:T(8,128)(2,1)S(1)}, u32[]{:S(2)}, u32[]{:S(2)}) %collective-permute-start.12) | collective-permute-done | bytes 114720 | tf_op jit(solution)/shard_map/ppermute | solution.py:25
  19.5 0.5 collective-permute-start.14
  20.0 0.5 collective-permute-start.13
  20.5 1.9 %collective-permute-done.7.refs_10_ = bf16[8,7168]{1,0:T(8,128)(2,1)S(1)} collective-permute-done((bf16[8,7168]{1,0:T(8,128)(2,1)S(1)}, bf16[8,7168]{1,0:T(8,128)(2,1)S(1)}, u32[]{:S(2)}, u32[]{:S(2)}) %collective-permute-start.7) | collective-permute-done | bytes 114720 | tf_op jit(solution)/shard_map/ppermute | solution.py:25
  22.4 0.5 collective-permute-start.8
  22.9 1.7 %collective-permute-done.14.refs_18_ = bf16[8,7168]{1,0:T(8,128)(2,1)S(1)} collective-permute-done((bf16[8,7168]{1,0:T(8,128)(2,1)S(1)}, bf16[8,7168]{1,0:T(8,128)(2,1)S(1)}, u32[]{:S(2)}, u32[]{:S(2)}) %collective-permute-start.14) | collective-permute-done | bytes 114720 | tf_op jit(solution)/shard_map/ppermute | solution.py:25
  24.6 0.4 fusion.1.refs_1_
  25.1 0.2 copy-done.8
  25.2 0.7 %add.123 = f32[224,128]{1,0:T(8,128)} add(f32[224,128]{1,0:T(8,128)S(1)} %bitcast_subtract_fusion, f32[224,128]{1,0:T(8,128)S(1)} %collective-permute-done) | non-fusion elementwise | flops 28672 | bytes 344064 | tf_op jit(solution)/shard_map/add | solution.py:232
  25.9 0.2 copy-done.1
  26.2 0.9 %copy-done.3 = bf16[8,7168]{1,0:T(8,128)(2,1)S(1)} copy-done((bf16[8,7168]{1,0:T(8,128)(2,1)S(1)}, bf16[8,7168]{1,0:T(8,128)(2,1)}, u32[]{:S(2)}) %copy-start.3) | copy-done | bytes 114712
  27.1 0.9 %copy-done.5 = bf16[8,7168]{1,0:T(8,128)(2,1)S(1)} copy-done((bf16[8,7168]{1,0:T(8,128)(2,1)S(1)}, bf16[8,7168]{1,0:T(8,128)(2,1)}, u32[]{:S(2)}) %copy-start.5) | copy-done | bytes 114712
  28.0 0.9 %copy-done.7 = bf16[8,7168]{1,0:T(8,128)(2,1)S(1)} copy-done((bf16[8,7168]{1,0:T(8,128)(2,1)S(1)}, bf16[8,7168]{1,0:T(8,128)(2,1)}, u32[]{:S(2)}) %copy-start.7) | copy-done | bytes 114712
  28.9 0.9 %copy-done.9 = bf16[8,7168]{1,0:T(8,128)(2,1)S(1)} copy-done((bf16[8,7168]{1,0:T(8,128)(2,1)S(1)}, bf16[8,7168]{1,0:T(8,128)(2,1)}, u32[]{:S(2)}) %copy-start.9) | copy-done | bytes 114712
  29.8 8.5 %shard_map.103 = (bf16[1,8,7168]{2,1,0:T(8,128)(2,1)S(1)}, bf16[3,8,7168]{2,1,0:T(8,128)(2,1)S(1)}, bf16[4,8,7168]{2,1,0:T(8,128)(2,1)S(1)}, bf16[8,8,7168]{2,1,0:T(8,128)(2,1)S(1)}) custom-call(s32[1]{0:T(128)} %bitcast.1.refs_0_, bf16[128,7168]{1,0:T(8,128)(2,1)S(1)} %fusion.1.refs_1_, bf16[128,7168]{1,0:T(8,128)(2,1)S(1)} %bitcast.49, ...), custom_call_target="tpu_custom_call" | custom-call | tf_op jit(solution)/shard_map/pallas_call | solution.py:193
  38.3 0.6 collective-permute-start.17
  38.9 0.1 collective-permute-start.22
  39.0 0.4 collective-permute-start.16
  39.4 0.9 %collective-permute-done.22 = bf16[1,8,7168]{2,1,0:T(8,128)(2,1)S(1)} collective-permute-done((bf16[1,8,7168]{2,1,0:T(8,128)(2,1)S(1)}, bf16[1,8,7168]{2,1,0:T(8,128)(2,1)S(1)}, u32[]{:S(2)}, u32[]{:S(2)}) %collective-permute-start.22) | collective-permute-done | bytes 114720 | tf_op jit(solution)/shard_map/ppermute | solution.py:25
  40.3 0.1 fusion.8
  40.5 0.6 collective-permute-start.19
  41.0 1.5 %collective-permute-start.23 = (bf16[8,7168]{1,0:T(8,128)(2,1)S(1)}, bf16[8,7168]{1,0:T(8,128)(2,1)S(1)}, u32[]{:S(2)}, u32[]{:S(2)}) collective-permute-start(bf16[8,7168]{1,0:T(8,128)(2,1)S(1)} %get-tuple-element.33), channel_id=1, source_target_pairs={{0,2},{1,3},{2,0},{3,1},{4,6},{5,7},{6,4},{7,5},{8,10},{9,11},{10,... | collective-permute-start | bytes 344072 | tf_op jit(solution)/shard_map/ppermute | solution.py:25
  42.6 0.5 collective-permute-start.21
  43.1 3.4 %collective-permute-done.19 = bf16[8,7168]{1,0:T(8,128)(2,1)S(1)} collective-permute-done((bf16[8,7168]{1,0:T(8,128)(2,1)S(1)}, bf16[8,7168]{1,0:T(8,128)(2,1)S(1)}, u32[]{:S(2)}, u32[]{:S(2)}) %collective-permute-start.19) | collective-permute-done | bytes 114720 | tf_op jit(solution)/shard_map/ppermute | solution.py:25
  46.5 2.5 %collective-permute-done.23 = bf16[8,7168]{1,0:T(8,128)(2,1)S(1)} collective-permute-done((bf16[8,7168]{1,0:T(8,128)(2,1)S(1)}, bf16[8,7168]{1,0:T(8,128)(2,1)S(1)}, u32[]{:S(2)}, u32[]{:S(2)}) %collective-permute-start.23) | collective-permute-done | bytes 114720 | tf_op jit(solution)/shard_map/ppermute | solution.py:25
  49.0 0.1 fusion.5
  49.1 1.6 %collective-permute-start.24 = (bf16[8,7168]{1,0:T(8,128)(2,1)S(1)}, bf16[8,7168]{1,0:T(8,128)(2,1)S(1)}, u32[]{:S(2)}, u32[]{:S(2)}) collective-permute-start(bf16[8,7168]{1,0:T(8,128)(2,1)S(1)} %get-tuple-element.29), channel_id=1, source_target_pairs={{0,4},{1,5},{2,6},{3,7},{4,0},{5,1},{6,2},{7,3},{8,12},{9,13},{10,... | collective-permute-start | bytes 344072 | tf_op jit(solution)/shard_map/ppermute | solution.py:25
  50.8 0.6 collective-permute-start.18
  51.4 0.5 collective-permute-start.20
  51.9 3.0 %collective-permute-done.24 = bf16[8,7168]{1,0:T(8,128)(2,1)S(1)} collective-permute-done((bf16[8,7168]{1,0:T(8,128)(2,1)S(1)}, bf16[8,7168]{1,0:T(8,128)(2,1)S(1)}, u32[]{:S(2)}, u32[]{:S(2)}) %collective-permute-start.24) | collective-permute-done | bytes 114720 | tf_op jit(solution)/shard_map/ppermute | solution.py:25
  54.9 0.9 %collective-permute-start.25 = (bf16[8,7168]{1,0:T(8,128)(2,1)S(1)}, bf16[8,7168]{1,0:T(8,128)(2,1)S(1)}, u32[]{:S(2)}, u32[]{:S(2)}) collective-permute-start(bf16[8,7168]{1,0:T(8,128)(2,1)S(1)} %fusion.4), channel_id=1, source_target_pairs={{0,8},{1,9},{2,10},{3,11},{4,12},{5,13},{6,14},{7,15},{8,0},{9,1},... | collective-permute-start | bytes 344072 | tf_op jit(solution)/shard_map/ppermute | solution.py:25
  55.8 0.7 %broadcast_multiply_fusion.1 = (f32[224,128]{1,0:T(8,128)S(1)}, f32[224,128]{1,0:T(8,128)}, f32[224,128]{1,0:T(8,128)}) fusion(f32[224,128]{1,0:T(8,128)S(1)} %copy-done.11, f32[224,128]{1,0:T(8,128)S(1)} %copy-done.12, f32[224,128]{1,0:T(8,128)S(1)} %copy-done.15), kind=kLoop, calls=%fused_computation.28 | loop fusion | flops 229376 | bytes 688128 | tf_op jit(solution)/shard_map/mul | solution.py:259
  56.5 0.7 %collective-permute-done.20 = bf16[8,7168]{1,0:T(8,128)(2,1)S(1)} collective-permute-done((bf16[8,7168]{1,0:T(8,128)(2,1)S(1)}, bf16[8,7168]{1,0:T(8,128)(2,1)S(1)}, u32[]{:S(2)}, u32[]{:S(2)}) %collective-permute-start.20) | collective-permute-done | bytes 114720 | tf_op jit(solution)/shard_map/ppermute | solution.py:25
  57.2 4.7 %collective-permute-done.25 = bf16[8,7168]{1,0:T(8,128)(2,1)S(1)} collective-permute-done((bf16[8,7168]{1,0:T(8,128)(2,1)S(1)}, bf16[8,7168]{1,0:T(8,128)(2,1)S(1)}, u32[]{:S(2)}, u32[]{:S(2)}) %collective-permute-start.25) | collective-permute-done | bytes 114720 | tf_op jit(solution)/shard_map/ppermute | solution.py:25
  61.9 0.1 broadcast_multiply_fusion
  62.2 0.9 %add_select_fusion = f32[1,2,224,128]{3,2,1,0:T(8,128)} fusion(f32[1,2,224,128]{3,2,1,0:T(8,128)S(1)} %copy-done.10, f32[1,2,224,128]{3,2,1,0:T(8,128)S(1)} %mul.121, f32[1,2,224,128]{3,2,1,0:T(8,128)S(1)} %copy-done.13, f32[1,2,224,128]{3,2,1,0:T(8,128)S(1)} %mul.114, f32[1,2,224,128]{3,2,1,0:T(8,128)S(1)} %copy-done.14, ...), kind=kLoop, calls=%fused_computation.14 | loop fusion | flops 860160 | bytes 1490954 | tf_op jit(solution)/shard_map/jit(_where)/select_n | solution.py:259
  (53 shorter events, 0.3 us)
Async XLA Ops:
  0.6 24.0 %copy-start = (bf16[1,128,7168]{2,1,0:T(8,128)(2,1)S(1)}, bf16[1,128,7168]{2,1,0:T(8,128)(2,1)}, u32[]{:S(2)}) copy-start(bf16[1,128,7168]{2,1,0:T(8,128)(2,1)} %param.8) | copy-start | bytes 5505028
  1.8 12.4 %collective-permute-start.2 = (bf16[8,7168]{1,0:T(8,128)(2,1)S(1)}, bf16[8,7168]{1,0:T(8,128)(2,1)S(1)}, u32[]{:S(2)}, u32[]{:S(2)}) collective-permute-start(bf16[8,7168]{1,0:T(8,128)(2,1)S(1)} %convert_element_type.137.refs_4_), channel_id=1, source_target_pairs={{0,4},{1,5},{2,6},{3,7},{4,0},{5,1},{6,2},{7,3},{8,12},{9,13},{10,... | collective-permute-start | bytes 344072 | tf_op jit(solution)/shard_map/ppermute | solution.py:25
  4.9 9.3 %collective-permute-start.1 = (bf16[8,7168]{1,0:T(8,128)(2,1)S(1)}, bf16[8,7168]{1,0:T(8,128)(2,1)S(1)}, u32[]{:S(2)}, u32[]{:S(2)}) collective-permute-start(bf16[8,7168]{1,0:T(8,128)(2,1)S(1)} %convert_element_type.137.refs_4_), channel_id=1, source_target_pairs={{0,8},{1,9},{2,10},{3,11},{4,12},{5,13},{6,14},{7,15},{8,0},{9,1},... | collective-permute-start | bytes 344072 | tf_op jit(solution)/shard_map/ppermute | solution.py:25
  7.5 8.8 %collective-permute-start.4 = (bf16[8,7168]{1,0:T(8,128)(2,1)S(1)}, bf16[8,7168]{1,0:T(8,128)(2,1)S(1)}, u32[]{:S(2)}, u32[]{:S(2)}) collective-permute-start(bf16[8,7168]{1,0:T(8,128)(2,1)S(1)} %convert_element_type.137.refs_4_), channel_id=1, source_target_pairs={{0,2},{1,3},{2,0},{3,1},{4,6},{5,7},{6,4},{7,5},{8,10},{9,11},{10,... | collective-permute-start | bytes 344072 | tf_op jit(solution)/shard_map/ppermute | solution.py:25
  9.0 7.8 %collective-permute-start.3 = (bf16[8,7168]{1,0:T(8,128)(2,1)S(1)}, bf16[8,7168]{1,0:T(8,128)(2,1)S(1)}, u32[]{:S(2)}, u32[]{:S(2)}) collective-permute-start(bf16[8,7168]{1,0:T(8,128)(2,1)S(1)} %convert_element_type.137.refs_4_), channel_id=1, source_target_pairs={{0,1},{1,0},{2,3},{3,2},{4,5},{5,4},{6,7},{7,6},{8,9},{9,8},{10,11... | collective-permute-start | bytes 344072 | tf_op jit(solution)/shard_map/ppermute | solution.py:25
  10.6 5.6 %collective-permute-start = (f32[224,128]{1,0:T(8,128)S(1)}, f32[224,128]{1,0:T(8,128)S(1)}, u32[]{:S(2)}, u32[]{:S(2)}) collective-permute-start(f32[224,128]{1,0:T(8,128)S(1)} %bitcast_subtract_fusion), channel_id=1, source_target_pairs={{0,16},{16,0},{1,17},{17,1},{2,18},{18,2},{3,19},{19,3},{4,20},{20... | collective-permute-start | bytes 344072 | tf_op jit(solution)/shard_map/ppermute | solution.py:25
  14.2 5.3 %collective-permute-start.12 = (bf16[8,7168]{1,0:T(8,128)(2,1)S(1)}, bf16[8,7168]{1,0:T(8,128)(2,1)S(1)}, u32[]{:S(2)}, u32[]{:S(2)}) collective-permute-start(bf16[8,7168]{1,0:T(8,128)(2,1)S(1)} %collective-permute-done.1.refs_12_), channel_id=1, source_target_pairs={{0,4},{1,5},{2,6},{3,7},{4,0},{5,1},{6,2},{7,3},{8,12},{9,13},{10,... | collective-permute-start | bytes 344072 | tf_op jit(solution)/shard_map/ppermute | solution.py:25
  14.7 5.3 %collective-permute-start.10 = (bf16[8,7168]{1,0:T(8,128)(2,1)S(1)}, bf16[8,7168]{1,0:T(8,128)(2,1)S(1)}, u32[]{:S(2)}, u32[]{:S(2)}) collective-permute-start(bf16[8,7168]{1,0:T(8,128)(2,1)S(1)} %collective-permute-done.1.refs_12_), channel_id=1, source_target_pairs={{0,2},{1,3},{2,0},{3,1},{4,6},{5,7},{6,4},{7,5},{8,10},{9,11},{10,... | collective-permute-start | bytes 344072 | tf_op jit(solution)/shard_map/ppermute | solution.py:25
  16.3 3.8 %collective-permute-start.9 = (bf16[8,7168]{1,0:T(8,128)(2,1)S(1)}, bf16[8,7168]{1,0:T(8,128)(2,1)S(1)}, u32[]{:S(2)}, u32[]{:S(2)}) collective-permute-start(bf16[8,7168]{1,0:T(8,128)(2,1)S(1)} %collective-permute-done.1.refs_12_), channel_id=1, source_target_pairs={{0,1},{1,0},{2,3},{3,2},{4,5},{5,4},{6,7},{7,6},{8,9},{9,8},{10,11... | collective-permute-start | bytes 344072 | tf_op jit(solution)/shard_map/ppermute | solution.py:25
  16.3 6.1 %collective-permute-start.7 = (bf16[8,7168]{1,0:T(8,128)(2,1)S(1)}, bf16[8,7168]{1,0:T(8,128)(2,1)S(1)}, u32[]{:S(2)}, u32[]{:S(2)}) collective-permute-start(bf16[8,7168]{1,0:T(8,128)(2,1)S(1)} %collective-permute-done.2.refs_8_), channel_id=1, source_target_pairs={{0,2},{1,3},{2,0},{3,1},{4,6},{5,7},{6,4},{7,5},{8,10},{9,11},{10,... | collective-permute-start | bytes 344072 | tf_op jit(solution)/shard_map/ppermute | solution.py:25
  16.8 5.6 %collective-permute-start.6 = (bf16[8,7168]{1,0:T(8,128)(2,1)S(1)}, bf16[8,7168]{1,0:T(8,128)(2,1)S(1)}, u32[]{:S(2)}, u32[]{:S(2)}) collective-permute-start(bf16[8,7168]{1,0:T(8,128)(2,1)S(1)} %collective-permute-done.2.refs_8_), channel_id=1, source_target_pairs={{0,1},{1,0},{2,3},{3,2},{4,5},{5,4},{6,7},{7,6},{8,9},{9,8},{10,11... | collective-permute-start | bytes 344072 | tf_op jit(solution)/shard_map/ppermute | solution.py:25
  19.5 5.1 %collective-permute-start.14 = (bf16[8,7168]{1,0:T(8,128)(2,1)S(1)}, bf16[8,7168]{1,0:T(8,128)(2,1)S(1)}, u32[]{:S(2)}, u32[]{:S(2)}) collective-permute-start(bf16[8,7168]{1,0:T(8,128)(2,1)S(1)} %collective-permute-done.12.refs_16_), channel_id=1, source_target_pairs={{0,2},{1,3},{2,0},{3,1},{4,6},{5,7},{6,4},{7,5},{8,10},{9,11},{10,... | collective-permute-start | bytes 344072 | tf_op jit(solution)/shard_map/ppermute | solution.py:25
  20.0 5.9 %collective-permute-start.5 = (bf16[8,7168]{1,0:T(8,128)(2,1)S(1)}, bf16[8,7168]{1,0:T(8,128)(2,1)S(1)}, u32[]{:S(2)}, u32[]{:S(2)}) collective-permute-start(bf16[8,7168]{1,0:T(8,128)(2,1)S(1)} %collective-permute-done.4.refs_6_), channel_id=1, source_target_pairs={{0,1},{1,0},{2,3},{3,2},{4,5},{5,4},{6,7},{7,6},{8,9},{9,8},{10,11... | collective-permute-start | bytes 344072 | tf_op jit(solution)/shard_map/ppermute | solution.py:25
  20.0 5.0 %copy-start.2 = (bf16[8,7168]{1,0:T(8,128)(2,1)}, bf16[8,7168]{1,0:T(8,128)(2,1)S(1)}, u32[]{:S(2)}) copy-start(bf16[8,7168]{1,0:T(8,128)(2,1)S(1)} %collective-permute-done.9.refs_13_) | copy-start | bytes 344068
  20.0 5.9 %collective-permute-start.13 = (bf16[8,7168]{1,0:T(8,128)(2,1)S(1)}, bf16[8,7168]{1,0:T(8,128)(2,1)S(1)}, u32[]{:S(2)}, u32[]{:S(2)}) collective-permute-start(bf16[8,7168]{1,0:T(8,128)(2,1)S(1)} %collective-permute-done.12.refs_16_), channel_id=1, source_target_pairs={{0,1},{1,0},{2,3},{3,2},{4,5},{5,4},{6,7},{7,6},{8,9},{9,8},{10,11... | collective-permute-start | bytes 344072 | tf_op jit(solution)/shard_map/ppermute | solution.py:25
  22.4 2.6 %copy-start.4 = (bf16[8,7168]{1,0:T(8,128)(2,1)}, bf16[8,7168]{1,0:T(8,128)(2,1)S(1)}, u32[]{:S(2)}) copy-start(bf16[8,7168]{1,0:T(8,128)(2,1)S(1)} %collective-permute-done.7.refs_10_) | copy-start | bytes 344068
  22.4 3.5 %collective-permute-start.11 = (bf16[8,7168]{1,0:T(8,128)(2,1)S(1)}, bf16[8,7168]{1,0:T(8,128)(2,1)S(1)}, u32[]{:S(2)}, u32[]{:S(2)}) collective-permute-start(bf16[8,7168]{1,0:T(8,128)(2,1)S(1)} %collective-permute-done.10.refs_14_), channel_id=1, source_target_pairs={{0,1},{1,0},{2,3},{3,2},{4,5},{5,4},{6,7},{7,6},{8,9},{9,8},{10,11... | collective-permute-start | bytes 344072 | tf_op jit(solution)/shard_map/ppermute | solution.py:25
  22.4 2.6 %copy-start.6 = (bf16[8,7168]{1,0:T(8,128)(2,1)}, bf16[8,7168]{1,0:T(8,128)(2,1)S(1)}, u32[]{:S(2)}) copy-start(bf16[8,7168]{1,0:T(8,128)(2,1)S(1)} %collective-permute-done.6.refs_9_) | copy-start | bytes 344068
  22.4 3.5 %collective-permute-start.8 = (bf16[8,7168]{1,0:T(8,128)(2,1)S(1)}, bf16[8,7168]{1,0:T(8,128)(2,1)S(1)}, u32[]{:S(2)}, u32[]{:S(2)}) collective-permute-start(bf16[8,7168]{1,0:T(8,128)(2,1)S(1)} %collective-permute-done.7.refs_10_), channel_id=1, source_target_pairs={{0,1},{1,0},{2,3},{3,2},{4,5},{5,4},{6,7},{7,6},{8,9},{9,8},{10,11... | collective-permute-start | bytes 344072 | tf_op jit(solution)/shard_map/ppermute | solution.py:25
  24.6 0.6 %copy-start.8 = (bf16[8,7168]{1,0:T(8,128)(2,1)}, bf16[8,7168]{1,0:T(8,128)(2,1)S(1)}, u32[]{:S(2)}) copy-start(bf16[8,7168]{1,0:T(8,128)(2,1)S(1)} %collective-permute-done.14.refs_18_) | copy-start | bytes 344068
  24.6 1.3 %collective-permute-start.15 = (bf16[8,7168]{1,0:T(8,128)(2,1)S(1)}, bf16[8,7168]{1,0:T(8,128)(2,1)S(1)}, u32[]{:S(2)}, u32[]{:S(2)}) collective-permute-start(bf16[8,7168]{1,0:T(8,128)(2,1)S(1)} %collective-permute-done.14.refs_18_), channel_id=1, source_target_pairs={{0,1},{1,0},{2,3},{3,2},{4,5},{5,4},{6,7},{7,6},{8,9},{9,8},{10,11... | collective-permute-start | bytes 344072 | tf_op jit(solution)/shard_map/ppermute | solution.py:25
  24.6 1.5 %copy-start.1 = (bf16[1,128,7168]{2,1,0:T(8,128)(2,1)S(1)}, bf16[1,128,7168]{2,1,0:T(8,128)(2,1)}, u32[]{:S(2)}) copy-start(bf16[1,128,7168]{2,1,0:T(8,128)(2,1)} %param.9) | copy-start | bytes 5505028
  26.2 0.9 %copy-start.3 = (bf16[8,7168]{1,0:T(8,128)(2,1)S(1)}, bf16[8,7168]{1,0:T(8,128)(2,1)}, u32[]{:S(2)}) copy-start(bf16[8,7168]{1,0:T(8,128)(2,1)} %copy-done.2) | copy-start | bytes 344068
  27.1 0.9 %copy-start.5 = (bf16[8,7168]{1,0:T(8,128)(2,1)S(1)}, bf16[8,7168]{1,0:T(8,128)(2,1)}, u32[]{:S(2)}) copy-start(bf16[8,7168]{1,0:T(8,128)(2,1)} %copy-done.4) | copy-start | bytes 344068
  28.0 0.9 %copy-start.7 = (bf16[8,7168]{1,0:T(8,128)(2,1)S(1)}, bf16[8,7168]{1,0:T(8,128)(2,1)}, u32[]{:S(2)}) copy-start(bf16[8,7168]{1,0:T(8,128)(2,1)} %copy-done.6) | copy-start | bytes 344068
  28.9 0.9 %copy-start.9 = (bf16[8,7168]{1,0:T(8,128)(2,1)S(1)}, bf16[8,7168]{1,0:T(8,128)(2,1)}, u32[]{:S(2)}) copy-start(bf16[8,7168]{1,0:T(8,128)(2,1)} %copy-done.8) | copy-start | bytes 344068
  38.3 17.5 %copy-start.11 = (f32[224,128]{1,0:T(8,128)S(1)}, f32[224,128]{1,0:T(8,128)}, u32[]{:S(2)}) copy-start(f32[224,128]{1,0:T(8,128)} %param.13) | copy-start | bytes 344068
  38.3 17.5 %copy-start.12 = (f32[224,128]{1,0:T(8,128)S(1)}, f32[224,128]{1,0:T(8,128)}, u32[]{:S(2)}) copy-start(f32[224,128]{1,0:T(8,128)} %add.123) | copy-start | bytes 344068
  38.3 17.5 %copy-start.15 = (f32[224,128]{1,0:T(8,128)S(1)}, f32[224,128]{1,0:T(8,128)}, u32[]{:S(2)}) copy-start(f32[224,128]{1,0:T(8,128)} %param.14) | copy-start | bytes 344068
  38.3 2.0 %collective-permute-start.17 = (bf16[3,8,7168]{2,1,0:T(8,128)(2,1)S(1)}, bf16[3,8,7168]{2,1,0:T(8,128)(2,1)S(1)}, u32[]{:S(2)}, u32[]{:S(2)}) collective-permute-start(bf16[3,8,7168]{2,1,0:T(8,128)(2,1)S(1)} %get-tuple-element.20), channel_id=1, source_target_pairs={{0,1},{1,0},{2,3},{3,2},{4,5},{5,4},{6,7},{7,6},{8,9},{9,8},{10,11... | collective-permute-start | bytes 1032200 | tf_op jit(solution)/shard_map/ppermute | solution.py:25
  38.9 1.4 %collective-permute-start.22 = (bf16[1,8,7168]{2,1,0:T(8,128)(2,1)S(1)}, bf16[1,8,7168]{2,1,0:T(8,128)(2,1)S(1)}, u32[]{:S(2)}, u32[]{:S(2)}) collective-permute-start(bf16[1,8,7168]{2,1,0:T(8,128)(2,1)S(1)} %get-tuple-element.21), channel_id=1, source_target_pairs={{0,1},{1,0},{2,3},{3,2},{4,5},{5,4},{6,7},{7,6},{8,9},{9,8},{10,11... | collective-permute-start | bytes 344072 | tf_op jit(solution)/shard_map/ppermute | solution.py:25
  39.0 10.0 %collective-permute-start.16 = (bf16[4,8,7168]{2,1,0:T(8,128)(2,1)S(1)}, bf16[4,8,7168]{2,1,0:T(8,128)(2,1)S(1)}, u32[]{:S(2)}, u32[]{:S(2)}) collective-permute-start(bf16[4,8,7168]{2,1,0:T(8,128)(2,1)S(1)} %get-tuple-element.19), channel_id=1, source_target_pairs={{0,1},{1,0},{2,3},{3,2},{4,5},{5,4},{6,7},{7,6},{8,9},{9,8},{10,11... | collective-permute-start | bytes 1376264 | tf_op jit(solution)/shard_map/ppermute | solution.py:25
  40.5 6.0 %collective-permute-start.19 = (bf16[8,7168]{1,0:T(8,128)(2,1)S(1)}, bf16[8,7168]{1,0:T(8,128)(2,1)S(1)}, u32[]{:S(2)}, u32[]{:S(2)}) collective-permute-start(bf16[8,7168]{1,0:T(8,128)(2,1)S(1)} %get-tuple-element.32), channel_id=1, source_target_pairs={{0,2},{1,3},{2,0},{3,1},{4,6},{5,7},{6,4},{7,5},{8,10},{9,11},{10,... | collective-permute-start | bytes 344072 | tf_op jit(solution)/shard_map/ppermute | solution.py:25
  41.0 7.9 %collective-permute-start.23 = (bf16[8,7168]{1,0:T(8,128)(2,1)S(1)}, bf16[8,7168]{1,0:T(8,128)(2,1)S(1)}, u32[]{:S(2)}, u32[]{:S(2)}) collective-permute-start(bf16[8,7168]{1,0:T(8,128)(2,1)S(1)} %get-tuple-element.33), channel_id=1, source_target_pairs={{0,2},{1,3},{2,0},{3,1},{4,6},{5,7},{6,4},{7,5},{8,10},{9,11},{10,... | collective-permute-start | bytes 344072 | tf_op jit(solution)/shard_map/ppermute | solution.py:25
  42.6 9.3 %collective-permute-start.21 = (bf16[8,7168]{1,0:T(8,128)(2,1)S(1)}, bf16[8,7168]{1,0:T(8,128)(2,1)S(1)}, u32[]{:S(2)}, u32[]{:S(2)}) collective-permute-start(bf16[8,7168]{1,0:T(8,128)(2,1)S(1)} %get-tuple-element.31), channel_id=1, source_target_pairs={{0,2},{1,3},{2,0},{3,1},{4,6},{5,7},{6,4},{7,5},{8,10},{9,11},{10,... | collective-permute-start | bytes 344072 | tf_op jit(solution)/shard_map/ppermute | solution.py:25
  49.0 13.1 %copy-start.10 = (f32[1,2,224,128]{3,2,1,0:T(8,128)S(1)}, f32[1,2,224,128]{3,2,1,0:T(8,128)}, u32[]{:S(2)}) copy-start(f32[1,2,224,128]{3,2,1,0:T(8,128)} %param.10) | copy-start | bytes 688132
  49.1 13.1 %copy-start.13 = (f32[1,2,224,128]{3,2,1,0:T(8,128)S(1)}, f32[1,2,224,128]{3,2,1,0:T(8,128)}, u32[]{:S(2)}) copy-start(f32[1,2,224,128]{3,2,1,0:T(8,128)} %param.12) | copy-start | bytes 688132
  49.1 13.1 %copy-start.14 = (f32[1,2,224,128]{3,2,1,0:T(8,128)S(1)}, f32[1,2,224,128]{3,2,1,0:T(8,128)}, u32[]{:S(2)}) copy-start(f32[1,2,224,128]{3,2,1,0:T(8,128)} %param.11) | copy-start | bytes 688132
  49.1 5.8 %collective-permute-start.24 = (bf16[8,7168]{1,0:T(8,128)(2,1)S(1)}, bf16[8,7168]{1,0:T(8,128)(2,1)S(1)}, u32[]{:S(2)}, u32[]{:S(2)}) collective-permute-start(bf16[8,7168]{1,0:T(8,128)(2,1)S(1)} %get-tuple-element.29), channel_id=1, source_target_pairs={{0,4},{1,5},{2,6},{3,7},{4,0},{5,1},{6,2},{7,3},{8,12},{9,13},{10,... | collective-permute-start | bytes 344072 | tf_op jit(solution)/shard_map/ppermute | solution.py:25
  50.8 5.7 %collective-permute-start.18 = (bf16[8,7168]{1,0:T(8,128)(2,1)S(1)}, bf16[8,7168]{1,0:T(8,128)(2,1)S(1)}, u32[]{:S(2)}, u32[]{:S(2)}) collective-permute-start(bf16[8,7168]{1,0:T(8,128)(2,1)S(1)} %get-tuple-element.30), channel_id=1, source_target_pairs={{0,2},{1,3},{2,0},{3,1},{4,6},{5,7},{6,4},{7,5},{8,10},{9,11},{10,... | collective-permute-start | bytes 344072 | tf_op jit(solution)/shard_map/ppermute | solution.py:25
  51.4 5.9 %collective-permute-start.20 = (bf16[8,7168]{1,0:T(8,128)(2,1)S(1)}, bf16[8,7168]{1,0:T(8,128)(2,1)S(1)}, u32[]{:S(2)}, u32[]{:S(2)}) collective-permute-start(bf16[8,7168]{1,0:T(8,128)(2,1)S(1)} %get-tuple-element.28), channel_id=1, source_target_pairs={{0,4},{1,5},{2,6},{3,7},{4,0},{5,1},{6,2},{7,3},{8,12},{9,13},{10,... | collective-permute-start | bytes 344072 | tf_op jit(solution)/shard_map/ppermute | solution.py:25
  54.9 7.0 %collective-permute-start.25 = (bf16[8,7168]{1,0:T(8,128)(2,1)S(1)}, bf16[8,7168]{1,0:T(8,128)(2,1)S(1)}, u32[]{:S(2)}, u32[]{:S(2)}) collective-permute-start(bf16[8,7168]{1,0:T(8,128)(2,1)S(1)} %fusion.4), channel_id=1, source_target_pairs={{0,8},{1,9},{2,10},{3,11},{4,12},{5,13},{6,14},{7,15},{8,0},{9,1},... | collective-permute-start | bytes 344072 | tf_op jit(solution)/shard_map/ppermute | solution.py:25

commit v2 on v1

v2 whole, which is shorter than its diff:
```python
import functools
import math

import jax
import jax.numpy as jnp
from jax import lax
from jax.experimental import pallas as pl
from jax.experimental.pallas import tpu as pltpu
from jax.sharding import PartitionSpec as P

norm_eps = 1e-05
beta_one = 0.9
beta_two = 0.95
adam_eps = 1e-08
decay_rate = 0.1
inner_rate = 0.05
outer_rate = 0.7
outer_beta = 0.9
mixing = 0.5
ROWS = 8


def swap(value, axis, mask):
    size = lax.axis_size(axis)
    return lax.ppermute(value, axis, [(i, i ^ mask) for i in range(size)])


def after(value, *others):
    return lax.optimization_barrier((value, *others))[0]


def gather_blocks(own, axis, stage):
    size = lax.axis_size(axis)
    single = [k for k in range(4, size, 4) if k & (k - 1) == 0]
    others = [k for k in range(4, size, 4) if k & (k - 1)]
    own = own[None]
    have = {0: own}
    have[4] = swap(own, axis, 4)
    near = swap(own, axis, 2)
    for k in single[1:]:
        have[k] = swap(own, axis, k)
    done = stage((near, have[4]))
    for k in single[1:]:
        have[k] = after(have[k], done)
    for k in others:
        have[k] = swap(have[k & (k - 1)], axis, k & -k)
    first = jnp.concatenate([have[k] for k in single])
    second = jnp.concatenate([have[k] for k in others])
    far_first = swap(first, axis, 2)
    far_second = swap(second, axis, 2)
    sets = [
        ([0, 2] + single, jnp.concatenate([own, near, first])),
        (others + [k + 2 for k in single], jnp.concatenate([second, far_first])),
        ([k + 2 for k in others], far_second),
    ]
    crossed = [([k + 1 for k in ks], swap(blocks, axis, 1)) for ks, blocks in sets]
    return sets + crossed


def add_f32(left, right):
    return left.astype(jnp.float32) + right.astype(jnp.float32)


def reduce_blocks(blocks, odd_sets, axis):
    size = lax.axis_size(axis)
    left = dict(blocks)
    begun = None
    for ks, terms in odd_sets:
        came = swap(terms, axis, 1)
        if begun is not None:
            came = after(came, begun)
        for place, k in enumerate(ks):
            left[k - 1] = add_f32(left[k - 1], came[place])
        if begun is None:
            begun = left[ks[0] - 1] = left[ks[0] - 1].astype(jnp.bfloat16)

    def give(k, *earlier):
        part = after(left.pop(k).astype(jnp.bfloat16), *earlier)
        came = swap(part, axis, k & -k)
        left[k & (k - 1)] = left[k & (k - 1)] + came.astype(jnp.float32)
        return part

    earlier = ()
    for k in range(size - 4, -1, -4):
        give(k + 2, *earlier)
        if k:
            earlier = (give(k),)
    return left[0]


def output_sets(size):
    odd = list(range(size - 1, 0, -2))
    sends = [k for k in odd if k & 2]
    return [sends[:1], sends[1:], [k for k in odd if not k & 2], list(range(0, size, 2))]


def dot_nt(left, right):
    return lax.dot_general(left, right, (((1,), (1,)), ((), ())), preferred_element_type=jnp.float32)


def dot_nn(left, right, precision=None):
    return jnp.dot(left, right, preferred_element_type=jnp.float32, precision=precision)


def squares_of(value, total):
    value = value * value
    for j in range(0, value.shape[1], 128):
        total = total + value[:, j : j + 128]
    return total


def stage_kernel(h_ref, *refs):
    squares = refs[-1]
    width = 1024 if h_ref.shape[1] % 1024 == 0 else 128

    def step(at, total):
        cut = pl.ds(pl.multiple_of(at * width, width), width)
        return squares_of(h_ref[:, cut].astype(jnp.float32), total)

    squares[...] = lax.fori_loop(0, h_ref.shape[1] // width, step, jnp.zeros(squares.shape, jnp.float32))


def stage_tokens(tokens, early):
    return pl.pallas_call(
        stage_kernel,
        out_shape=jax.ShapeDtypeStruct((tokens.shape[0], 128), jnp.float32),
        in_specs=[pl.BlockSpec(memory_space=pltpu.VMEM)] + [pl.BlockSpec(memory_space=pl.ANY)] * len(early),
        out_specs=pl.BlockSpec(memory_space=pltpu.VMEM),
        compiler_params=pltpu.CompilerParams(vmem_limit_bytes=4 * 2**20),
    )(tokens, *early)


def adapter_kernel(n_arrays, sources, places, units, width, *refs):
    upper_ref, h0, g2, squares0 = refs[:4]
    arrays = refs[4 : 4 + n_arrays]
    outs = refs[4 + n_arrays : -2]
    n_pieces = len(sources)
    w_ref, h1 = refs[-2:]
    tokens, model_width = h0.shape
    stacked = n_pieces * ROWS // 2
    hidden = stacked // 2
    in_scale = model_width ** (-0.5)
    out_scale = hidden ** (-0.5)
    steps = model_width // width
    upper = upper_ref[0]
    half = n_pieces // 2
    w_in, w_out = pl.ds(0, stacked), pl.ds(stacked, stacked)
    layer_of = (lax.broadcasted_iota(jnp.int32, (tokens, stacked), 1) % (2 * units)) // units
    zeros = jnp.zeros((tokens, stacked), jnp.float32)
    no_squares = jnp.zeros((tokens, 128), jnp.float32)

    def cut(step):
        return pl.ds(pl.multiple_of(step * width, width), width)

    def inv_rms(squares):
        return lax.rsqrt(jnp.sum(squares, axis=1, keepdims=True) / model_width + norm_eps)

    def first(step, carry):
        pre, grad, cross = carry
        at = cut(step)
        for side in range(2):
            parts = []
            for k in range(side * half, side * half + half):
                array, place = sources[k]
                parts.append(arrays[array][place, :, at].astype(jnp.float32))
            rows = pl.ds(pl.multiple_of((side ^ upper) * stacked, stacked), stacked)
            w_ref[rows, at] = jnp.concatenate(parts).astype(jnp.bfloat16)
        pre = pre + dot_nt(h0[:, at], w_ref[w_in, at])
        grad = grad + dot_nt(g2[:, at], w_ref[w_out, at])
        cross = cross + dot_nt(w_ref[w_in, at], w_ref[w_out, at])
        return pre, grad, cross

    cross = jnp.zeros((stacked, stacked), jnp.float32)
    pre0, grad_act, cross = lax.fori_loop(0, steps, first, (zeros, zeros, cross))
    inv0 = inv_rms(squares0[...])
    pre0 = pre0 * (inv0 * in_scale)
    sig0 = jax.nn.sigmoid(pre0)
    act0 = jnp.where(layer_of == 0, pre0 * sig0, 0.0)
    act0_low = act0.astype(jnp.bfloat16)

    def second(step, carry):
        both, squares = carry
        at = cut(step)
        out = h0[:, at].astype(jnp.float32) + dot_nn(act0_low, w_ref[w_out, at]) * out_scale
        low = out.astype(jnp.bfloat16)
        h1[:, at] = low
        return both + dot_nt(low, w_ref[:, at]), squares_of(low.astype(jnp.float32), squares)

    both = jnp.zeros((tokens, 2 * stacked), jnp.float32)
    both, squares = lax.fori_loop(0, steps, second, (both, no_squares))
    inv1 = inv_rms(squares)
    pre1 = both[:, :stacked] * (inv1 * in_scale)
    sig1 = jax.nn.sigmoid(pre1)
    act1 = jnp.where(layer_of == 1, pre1 * sig1, 0.0)
    slope1 = sig1 * (1.0 + pre1 * (1.0 - sig1))
    gp1 = jnp.where(layer_of == 1, grad_act * out_scale * slope1, 0.0)
    gp1_low = gp1.astype(jnp.bfloat16)
    gp1 = gp1_low.astype(jnp.float32)
    coef = inv1 * inv1 * jnp.sum(gp1 * pre1, axis=1, keepdims=True) / model_width
    factor = inv1 * in_scale
    grad_act0 = (
        grad_act + factor * dot_nn(gp1, cross, lax.Precision.HIGHEST) - coef * both[:, stacked:]
    )
    slope0 = sig0 * (1.0 + pre0 * (1.0 - sig0))
    gp0 = jnp.where(layer_of == 0, grad_act0 * out_scale * slope0, 0.0)
    act_t = jnp.concatenate([act0.T, act1.T], axis=1).astype(jnp.bfloat16)
    gp_t = jnp.concatenate([(gp0 * inv0).T, (gp1 * inv1).T], axis=1).astype(jnp.bfloat16)

    def third(step, carry):
        at = cut(step)
        g1 = (
            g2[:, at].astype(jnp.float32)
            + factor * dot_nn(gp1_low, w_ref[w_in, at])
            - coef * h1[:, at].astype(jnp.float32)
        ).astype(jnp.bfloat16)
        grad_out = dot_nn(act_t, jnp.concatenate([g1, g2[:, at]]))
        grad_in = dot_nn(gp_t, jnp.concatenate([h0[:, at], h1[:, at]]))
        for side in range(2):
            term = jnp.where(upper == side, grad_in, grad_out)
            for j in range(half):
                out, place = places[side * half + j]
                outs[out][place, :, at] = term[j * ROWS : (j + 1) * ROWS].astype(jnp.bfloat16)
        return carry

    lax.fori_loop(0, steps, third, 0)


def places_of(sets):
    return {k: (at, place) for at, ks in enumerate(sets) for place, k in enumerate(ks)}


def adapter_grads(upper, tokens, upstream, squares, gathered, units, sets):
    model_width = tokens.shape[1]
    arrays = [array for _, array in gathered]
    sources = places_of([ks for ks, _ in gathered])
    places = places_of(sets)
    width = 1792 if model_width % 1792 == 0 else 128
    stacked = len(sources) * ROWS // 2
    whole = pl.BlockSpec(memory_space=pltpu.VMEM)
    return pl.pallas_call(
        functools.partial(adapter_kernel, len(arrays), sources, places, units, width),
        out_shape=[jax.ShapeDtypeStruct((len(ks), ROWS, model_width), jnp.bfloat16) for ks in sets],
        in_specs=[pl.BlockSpec(memory_space=pltpu.SMEM)] + [whole] * (3 + len(arrays)),
        out_specs=[whole] * len(sets),
        scratch_shapes=[
            pltpu.VMEM((2 * stacked, model_width), jnp.bfloat16),
            pltpu.VMEM(tokens.shape, jnp.bfloat16),
        ],
        compiler_params=pltpu.CompilerParams(vmem_limit_bytes=10 * 2**20),
    )(upper, tokens, upstream, squares, *arrays)


def shards(inputs, cotangent, weights, first_moment, second_moment, anchor, momentum, fragment):
    tokens = inputs[0]
    upstream = cotangent[0]
    params = weights[0]
    layers, rows = params.shape[0], params.shape[1]
    model_width = tokens.shape[1]
    groups = lax.axis_size("fsdp")
    units = rows * 128 // model_width
    hidden = units * groups // 2
    upper = (lax.axis_index("fsdp") >= groups // 2).astype(jnp.int32).reshape(1)
    compact = params.astype(jnp.bfloat16).reshape(layers * units, model_width)
    other = swap(params, "rep", 1)
    kept = []

    def stage(blocks):
        kept.append(stage_tokens(tokens, (*blocks, other)))
        return kept[0]

    gathered = gather_blocks(compact, "fsdp", stage)
    squares = kept[0]
    per_piece = ROWS // (layers * units)
    sets = output_sets(groups)
    if per_piece == 1:
        outs = adapter_grads(upper, tokens, upstream, squares, gathered, units, sets)
    else:
        blocks = {k: array[place] for ks, array in gathered for place, k in enumerate(ks)}
        blocks = jnp.stack([blocks[k] for k in range(groups)]).reshape(-1, ROWS, model_width)
        every = list(range(blocks.shape[0]))
        (both,) = adapter_grads(upper, tokens, upstream, squares, [(every, blocks)], units, [every])
        both = both.reshape(groups, layers * units, model_width)
        outs = [jnp.stack([both[k] for k in ks]) for ks in sets]
    even = {k: outs[-1][place] for place, k in enumerate(sets[-1])}
    summed = reduce_blocks(even, list(zip(sets, outs))[:-1], "fsdp").reshape(layers, rows, 128)
    scale = jnp.where(upper[0] == 1, hidden ** (-0.5), model_width ** (-0.5))
    gradient = summed * (scale / (tokens.shape[0] * groups))
    count = fragment[0]
    chosen = jnp.remainder(count, layers)

    def delta(values):
        return anchor - lax.dynamic_index_in_dim(values, chosen, 0, keepdims=False)

    replicas = lax.axis_size("rep")
    total = delta(params) + delta(other)
    step = 2
    while step < replicas:
        total = total + swap(total, "rep", step)
        step *= 2
    count_real = count.astype(jnp.float32)
    correct_one = 1.0 - jnp.exp(count_real * math.log(beta_one))
    correct_two = 1.0 - jnp.exp(count_real * math.log(beta_two))
    moment_one = beta_one * first_moment[0] + (1.0 - beta_one) * gradient
    moment_two = beta_two * second_moment[0] + (1.0 - beta_two) * gradient * gradient
    updated = params - inner_rate * (
        moment_one / correct_one / (jnp.sqrt(moment_two / correct_two) + adam_eps)
        + decay_rate * params
    )
    mean_delta = total / replicas
    new_velocity = outer_beta * momentum + mean_delta
    new_global = anchor - outer_rate * (mean_delta + outer_beta * new_velocity)
    selector = (jnp.arange(layers, dtype=jnp.int32) == chosen)[:, None, None]
    merged = jnp.where(selector, mixing * updated + (1.0 - mixing) * new_global[None], updated)
    return (merged[None], new_global, new_velocity)


def solution(mesh):
    placed = (
        P("rep", "fsdp", None),
        P("rep", "fsdp", None),
        P("rep", None, "fsdp", None),
        P("rep", None, "fsdp", None),
        P("rep", None, "fsdp", None),
        P("fsdp", None),
        P("fsdp", None),
        P(),
    )
    return jax.shard_map(
        shards,
        mesh=mesh,
        in_specs=placed,
        out_specs=(P("rep", None, "fsdp", None), P("fsdp", None), P("fsdp", None)),
        check_vma=False,
    )
```

time: 63.4 us -> 71.4 us (1.13)
  waiting for transfers between devices: 22.4 us -> 29.6 us
  local copies, waits for them, and re-layouts: 4.2 us -> 9.01 us
  other arithmetic: 7.01 us -> 2.98 us
    ppermute x26 -> x20, waiting for transfers between devices: 22.4 us -> 29.6 us  [swap(): return lax.ppermute(value, axis, [(i, i ^ mask) for i in range(size)])]
    unnamed x32 -> x40, local copies, waits for them, and re-layouts: 4.06 us -> 8.89 us
    reduce_sum x1 -> x0, other arithmetic: 1.93 us -> none  [shards(): jnp.mean(inputs_f32 * inputs_f32, axis=-1, keepdims=True) + norm_eps]
    sub x1 -> x0, other arithmetic: 0.97 us -> none  [shards(): total = anchor - lax.dynamic_index_in_dim(params, chosen, 0, keepdims=False)]
    pallas_call x1 -> x2, Pallas kernels: 8.53 us -> 8.65 us  [the longest x1 8.16 us: adapter_grads(): pl.pallas_call(functools.partial(adapter_kernel, len(arrays), sources, pl...]
    ppermute x26 -> x20, starting transfers between devices: 19.2 us -> 19.2 us  [swap(): return lax.ppermute(value, axis, [(i, i ^ mask) for i in range(size)])]
  transfers between devices with their start and end apart: 26 -> 20, of which waited for: 10 -> 13; matrix products, arithmetic and copies ran while one was open for 8% -> 1% of each run, Pallas kernels for 0% -> 1%
where the time goes in v2:
time: 71.4 us; the launch traced here: 71 us
  waiting for transfers between devices  29.6 us (41%)
  starting transfers between devices  19.2 us (27%)
  local copies, waits for them, and re-layouts  9.01 us (13%)
  Pallas kernels  8.65 us (12%)
  other arithmetic  2.98 us (4%)
  between operations  1.63 us (2%)
    ppermute x20, waiting for transfers between devices, swap(): return lax.ppermute(value, axis, [(i, i ^ mask) for i in range(size)])  29.6 us
    ppermute x20, starting transfers between devices, swap(): return lax.ppermute(value, axis, [(i, i ^ mask) for i in range(size)])  19.2 us
    unnamed x40, local copies, waits for them, and re-layouts  8.89 us
    pallas_call x1, Pallas kernels, adapter_grads(): pl.pallas_call(functools.partial(adapter_kernel, len(arrays), sources, pl...  8.16 us
  transfers between devices with their start and end apart: 20, of which 13 were waited for; matrix products, arithmetic and copies ran while one was open for 1% of the time, Pallas kernels for 1%

profile of v2, /device:TPU:0, one launch (start us, length us, event | category | flops | bytes accessed | tf_op | source)
XLA Modules:
  0.0 71.0 jit_solution(14145769433008897988)
XLA Ops:
  0.6 1.0 %convert_element_type.138 = bf16[1,2,224,128]{3,2,1,0:T(8,128)(2,1)S(1)} convert(f32[1,2,224,128]{3,2,1,0:T(8,128)} %param.10) | non-fusion elementwise | flops 57344 | bytes 344064 | tf_op jit(solution)/shard_map/convert_element_type | solution.py:263
  1.7 3.1 %collective-permute-start.1 = (bf16[1,8,7168]{2,1,0:T(8,128)(2,1)S(1)}, bf16[1,8,7168]{2,1,0:T(8,128)(2,1)S(1)}, u32[]{:S(2)}, u32[]{:S(2)}) collective-permute-start(bf16[1,8,7168]{2,1,0:T(8,128)(2,1)S(1)} %convert_element_type.139), channel_id=1, source_target_pairs={{0,4},{1,5},{2,6},{3,7},{4,0},{5,1},{6,2},{7,3},{8,12},{9,13},{10,... | collective-permute-start | bytes 344072 | tf_op jit(solution)/shard_map/ppermute | solution.py:25
  4.7 1.5 %collective-permute-start = (bf16[1,8,7168]{2,1,0:T(8,128)(2,1)S(1)}, bf16[1,8,7168]{2,1,0:T(8,128)(2,1)S(1)}, u32[]{:S(2)}, u32[]{:S(2)}) collective-permute-start(bf16[1,8,7168]{2,1,0:T(8,128)(2,1)S(1)} %convert_element_type.139), channel_id=1, source_target_pairs={{0,2},{1,3},{2,0},{3,1},{4,6},{5,7},{6,4},{7,5},{8,10},{9,11},{10,... | collective-permute-start | bytes 344072 | tf_op jit(solution)/shard_map/ppermute | solution.py:25
  6.3 2.6 %collective-permute-start.3 = (bf16[1,8,7168]{2,1,0:T(8,128)(2,1)S(1)}, bf16[1,8,7168]{2,1,0:T(8,128)(2,1)S(1)}, u32[]{:S(2)}, u32[]{:S(2)}) collective-permute-start(bf16[1,8,7168]{2,1,0:T(8,128)(2,1)S(1)} %convert_element_type.139), channel_id=1, source_target_pairs={{0,8},{1,9},{2,10},{3,11},{4,12},{5,13},{6,14},{7,15},{8,0},{9,1},... | collective-permute-start | bytes 344072 | tf_op jit(solution)/shard_map/ppermute | solution.py:25
  8.8 1.5 %collective-permute-start.2 = (f32[2,224,128]{2,1,0:T(8,128)}, f32[2,224,128]{2,1,0:T(8,128)S(1)}, u32[]{:S(2)}, u32[]{:S(2)}) collective-permute-start(f32[2,224,128]{2,1,0:T(8,128)} %bitcast.66), channel_id=1, source_target_pairs={{0,16},{16,0},{1,17},{17,1},{2,18},{18,2},{3,19},{19,3},{4,20},{20... | collective-permute-start | bytes 688136 | tf_op jit(solution)/shard_map/ppermute | solution.py:25
  10.4 5.2 %collective-permute-done.2.refs_2_ = f32[2,224,128]{2,1,0:T(8,128)S(1)} collective-permute-done((f32[2,224,128]{2,1,0:T(8,128)}, f32[2,224,128]{2,1,0:T(8,128)S(1)}, u32[]{:S(2)}, u32[]{:S(2)}) %collective-permute-start.2) | collective-permute-done | bytes 229408 | tf_op jit(solution)/shard_map/ppermute | solution.py:25
  15.6 1.6 %copy-done = bf16[1,128,7168]{2,1,0:T(8,128)(2,1)S(1)} copy-done((bf16[1,128,7168]{2,1,0:T(8,128)(2,1)S(1)}, bf16[1,128,7168]{2,1,0:T(8,128)(2,1)}, u32[]{:S(2)}) %copy-start) | copy-done | bytes 1835032
  17.2 0.5 shard_map.103.refs_3_
  17.7 0.5 collective-permute-start.4
  18.2 0.6 collective-permute-start.5
  18.8 0.1 collective-permute-start.7
  18.9 3.7 %collective-permute-done.4 = bf16[1,8,7168]{2,1,0:T(8,128)(2,1)S(1)} collective-permute-done((bf16[1,8,7168]{2,1,0:T(8,128)(2,1)S(1)}, bf16[1,8,7168]{2,1,0:T(8,128)(2,1)S(1)}, u32[]{:S(2)}, u32[]{:S(2)}) %collective-permute-start.4) | collective-permute-done | bytes 114720 | tf_op jit(solution)/shard_map/ppermute | solution.py:25
  22.5 1.8 %collective-permute-done.5 = bf16[2,8,7168]{2,1,0:T(8,128)(2,1)S(1)} collective-permute-done((bf16[2,8,7168]{2,1,0:T(8,128)(2,1)S(1)}, bf16[2,8,7168]{2,1,0:T(8,128)(2,1)S(1)}, u32[]{:S(2)}, u32[]{:S(2)}) %collective-permute-start.5) | collective-permute-done | bytes 229408 | tf_op jit(solution)/shard_map/ppermute | solution.py:25
  24.3 0.1 collective-permute-start.8
  24.4 0.6 collective-permute-start.6
  25.0 5.0 %collective-permute-done.6.refs_6_ = bf16[1,8,7168]{2,1,0:T(8,128)(2,1)S(1)} collective-permute-done((bf16[1,8,7168]{2,1,0:T(8,128)(2,1)S(1)}, bf16[1,8,7168]{2,1,0:T(8,128)(2,1)S(1)}, u32[]{:S(2)}, u32[]{:S(2)}) %collective-permute-start.6) | collective-permute-done | bytes 114720 | tf_op jit(solution)/shard_map/ppermute | solution.py:25
  30.0 0.6 copy-done.9
  30.6 0.7 collective-permute-done.9.refs_9_
  31.3 0.6 copy-done.11
  31.9 0.8 %copy-done.5 = bf16[4,8,7168]{2,1,0:T(8,128)(2,1)} copy-done((bf16[4,8,7168]{2,1,0:T(8,128)(2,1)}, bf16[4,8,7168]{2,1,0:T(8,128)(2,1)S(1)}, u32[]{:S(2)}) %copy-start.5) | copy-done | bytes 458776
  32.7 1.5 %copy-done.2 = bf16[1,128,7168]{2,1,0:T(8,128)(2,1)S(1)} copy-done((bf16[1,128,7168]{2,1,0:T(8,128)(2,1)S(1)}, bf16[1,128,7168]{2,1,0:T(8,128)(2,1)}, u32[]{:S(2)}) %copy-start.2) | copy-done | bytes 1835032
  34.2 1.0 %copy-done.6 = bf16[4,8,7168]{2,1,0:T(8,128)(2,1)S(1)} copy-done((bf16[4,8,7168]{2,1,0:T(8,128)(2,1)S(1)}, bf16[4,8,7168]{2,1,0:T(8,128)(2,1)}, u32[]{:S(2)}) %copy-start.6) | copy-done | bytes 458776
  35.2 0.8 %copy-done.8 = f32[128,128]{1,0:T(8,128)S(1)} copy-done((f32[128,128]{1,0:T(8,128)S(1)}, f32[128,128]{1,0:T(8,128)}, u32[]{:S(2)}) %copy-start.8) | copy-done | bytes 65560
  36.1 0.9 %copy-done.10 = bf16[1,8,7168]{2,1,0:T(8,128)(2,1)S(1)} copy-done((bf16[1,8,7168]{2,1,0:T(8,128)(2,1)S(1)}, bf16[1,8,7168]{2,1,0:T(8,128)(2,1)}, u32[]{:S(2)}) %copy-start.10) | copy-done | bytes 114712
  37.0 0.9 %copy-done.12 = bf16[1,8,7168]{2,1,0:T(8,128)(2,1)S(1)} copy-done((bf16[1,8,7168]{2,1,0:T(8,128)(2,1)S(1)}, bf16[1,8,7168]{2,1,0:T(8,128)(2,1)}, u32[]{:S(2)}) %copy-start.12) | copy-done | bytes 114712
  37.9 8.2 %shard_map.104 = (bf16[1,8,7168]{2,1,0:T(8,128)(2,1)S(1)}, bf16[3,8,7168]{2,1,0:T(8,128)(2,1)S(1)}, bf16[4,8,7168]{2,1,0:T(8,128)(2,1)S(1)}, bf16[8,8,7168]{2,1,0:T(8,128)(2,1)S(1)}) custom-call(s32[1]{0:T(128)} %bitcast.1.refs_0_, bf16[128,7168]{1,0:T(8,128)(2,1)S(1)} %bitcast.64, bf16[128,7168]{1,0:T(8,128)(2,1)S(1)} %bitcast.65, ...), custom_call_target="tpu_custom_call" | custom-call | tf_op jit(solution)/shard_map/pallas_call | solution.py:240
  46.1 0.2 collective-permute-start.11
  46.3 0.4 collective-permute-start.10
  46.7 0.2 collective-permute-start.14
  46.8 0.7 collective-permute-done.11
  47.5 0.6 collective-permute-start.12
  48.1 0.5 collective-permute-done.14
  48.6 0.1 fusion.14
  48.8 4.0 %collective-permute-done.12 = bf16[8,7168]{1,0:T(8,128)(2,1)S(1)} collective-permute-done((bf16[8,7168]{1,0:T(8,128)(2,1)S(1)}, bf16[8,7168]{1,0:T(8,128)(2,1)S(1)}, u32[]{:S(2)}, u32[]{:S(2)}) %collective-permute-start.12) | collective-permute-done | bytes 114720 | tf_op jit(solution)/shard_map/ppermute | solution.py:25
  52.8 0.6 collective-permute-start.15
  53.4 1.6 %collective-permute-start.13 = (bf16[8,7168]{1,0:T(8,128)(2,1)S(1)}, bf16[8,7168]{1,0:T(8,128)(2,1)S(1)}, u32[]{:S(2)}, u32[]{:S(2)}) collective-permute-start(bf16[8,7168]{1,0:T(8,128)(2,1)S(1)} %fusion.7), channel_id=1, source_target_pairs={{0,4},{1,5},{2,6},{3,7},{4,0},{5,1},{6,2},{7,3},{8,12},{9,13},{10,... | collective-permute-start | bytes 344072 | tf_op jit(solution)/shard_map/ppermute | solution.py:25
  55.0 2.7 %collective-permute-done.15 = bf16[8,7168]{1,0:T(8,128)(2,1)S(1)} collective-permute-done((bf16[8,7168]{1,0:T(8,128)(2,1)S(1)}, bf16[8,7168]{1,0:T(8,128)(2,1)S(1)}, u32[]{:S(2)}, u32[]{:S(2)}) %collective-permute-start.15) | collective-permute-done | bytes 114720 | tf_op jit(solution)/shard_map/ppermute | solution.py:25
  57.7 0.5 collective-permute-done.13
  58.3 1.6 %collective-permute-start.17 = (bf16[8,7168]{1,0:T(8,128)(2,1)S(1)}, bf16[8,7168]{1,0:T(8,128)(2,1)S(1)}, u32[]{:S(2)}, u32[]{:S(2)}) collective-permute-start(bf16[8,7168]{1,0:T(8,128)(2,1)S(1)} %get-tuple-element.21), channel_id=1, source_target_pairs={{0,2},{1,3},{2,0},{3,1},{4,6},{5,7},{6,4},{7,5},{8,10},{9,11},{10,... | collective-permute-start | bytes 344072 | tf_op jit(solution)/shard_map/ppermute | solution.py:25
  60.6 0.4 collective-permute-start.16
  61.0 2.1 %collective-permute-done.17 = bf16[8,7168]{1,0:T(8,128)(2,1)S(1)} collective-permute-done((bf16[8,7168]{1,0:T(8,128)(2,1)S(1)}, bf16[8,7168]{1,0:T(8,128)(2,1)S(1)}, u32[]{:S(2)}, u32[]{:S(2)}) %collective-permute-start.17) | collective-permute-done | bytes 114720 | tf_op jit(solution)/shard_map/ppermute | solution.py:25
  63.2 2.0 %collective-permute-start.18 = (bf16[8,7168]{1,0:T(8,128)(2,1)S(1)}, bf16[8,7168]{1,0:T(8,128)(2,1)S(1)}, u32[]{:S(2)}, u32[]{:S(2)}) collective-permute-start(bf16[8,7168]{1,0:T(8,128)(2,1)S(1)} %fusion.6), channel_id=1, source_target_pairs={{0,4},{1,5},{2,6},{3,7},{4,0},{5,1},{6,2},{7,3},{8,12},{9,13},{10,... | collective-permute-start | bytes 344072 | tf_op jit(solution)/shard_map/ppermute | solution.py:25
  65.1 1.3 %collective-permute-start.19 = (bf16[8,7168]{1,0:T(8,128)(2,1)S(1)}, bf16[8,7168]{1,0:T(8,128)(2,1)S(1)}, u32[]{:S(2)}, u32[]{:S(2)}) collective-permute-start(bf16[8,7168]{1,0:T(8,128)(2,1)S(1)} %get-tuple-element.22), channel_id=1, source_target_pairs={{0,2},{1,3},{2,0},{3,1},{4,6},{5,7},{6,4},{7,5},{8,10},{9,11},{10,... | collective-permute-start | bytes 344072 | tf_op jit(solution)/shard_map/ppermute | solution.py:25
  66.4 0.7 %broadcast_multiply_fusion = (f32[224,128]{1,0:T(8,128)S(1)}, f32[224,128]{1,0:T(8,128)}, f32[224,128]{1,0:T(8,128)}) fusion(f32[224,128]{1,0:T(8,128)S(1)} %copy-done.16, f32[2,224,128]{2,1,0:T(8,128)S(1)} %copy-done.4, s32[]{:T(128)S(6)} %select_n.23, f32[1,2,224,128]{3,2,1,0:T(8,128)S(1)} %copy-done.13, f32[224,128]{1,0:T(8,128)S(1)} %copy-done.17), kind=kLoop, calls=%fused_computation.34 | loop fusion | flops 315392 | bytes 802820 | tf_op jit(solution)/shard_map/mul | solution.py:313
  67.2 0.6 collective-permute-done.16
  67.7 2.2 %collective-permute-done.19 = bf16[8,7168]{1,0:T(8,128)(2,1)S(1)} collective-permute-done((bf16[8,7168]{1,0:T(8,128)(2,1)S(1)}, bf16[8,7168]{1,0:T(8,128)(2,1)S(1)}, u32[]{:S(2)}, u32[]{:S(2)}) %collective-permute-start.19) | collective-permute-done | bytes 114720 | tf_op jit(solution)/shard_map/ppermute | solution.py:25
  69.9 0.1 fusion.12
  70.1 0.9 %add_select_fusion = f32[1,2,224,128]{3,2,1,0:T(8,128)} fusion(f32[1,2,224,128]{3,2,1,0:T(8,128)S(1)} %copy-done.13, f32[1,2,224,128]{3,2,1,0:T(8,128)S(1)} %mul.105, f32[1,2,224,128]{3,2,1,0:T(8,128)S(1)} %copy-done.14, f32[1,2,224,128]{3,2,1,0:T(8,128)S(1)} %copy-done.15, f32[224,128]{1,0:T(8,128)S(1)} %get-tuple-element.23, f32[]{:T(128)S(6)} %sub.20, ...), kind=kLoop, calls=%fused_computation.19 | loop fusion | flops 1032192 | bytes 1261578 | tf_op jit(solution)/shard_map/jit(_where)/select_n | solution.py:313
  (49 shorter events, 0.5 us)
Async XLA Ops:
  1.7 8.7 %collective-permute-start.1 = (bf16[1,8,7168]{2,1,0:T(8,128)(2,1)S(1)}, bf16[1,8,7168]{2,1,0:T(8,128)(2,1)S(1)}, u32[]{:S(2)}, u32[]{:S(2)}) collective-permute-start(bf16[1,8,7168]{2,1,0:T(8,128)(2,1)S(1)} %convert_element_type.139), channel_id=1, source_target_pairs={{0,4},{1,5},{2,6},{3,7},{4,0},{5,1},{6,2},{7,3},{8,12},{9,13},{10,... | collective-permute-start | bytes 344072 | tf_op jit(solution)/shard_map/ppermute | solution.py:25
  4.7 5.6 %collective-permute-start = (bf16[1,8,7168]{2,1,0:T(8,128)(2,1)S(1)}, bf16[1,8,7168]{2,1,0:T(8,128)(2,1)S(1)}, u32[]{:S(2)}, u32[]{:S(2)}) collective-permute-start(bf16[1,8,7168]{2,1,0:T(8,128)(2,1)S(1)} %convert_element_type.139), channel_id=1, source_target_pairs={{0,2},{1,3},{2,0},{3,1},{4,6},{5,7},{6,4},{7,5},{8,10},{9,11},{10,... | collective-permute-start | bytes 344072 | tf_op jit(solution)/shard_map/ppermute | solution.py:25
  6.3 11.4 %collective-permute-start.3 = (bf16[1,8,7168]{2,1,0:T(8,128)(2,1)S(1)}, bf16[1,8,7168]{2,1,0:T(8,128)(2,1)S(1)}, u32[]{:S(2)}, u32[]{:S(2)}) collective-permute-start(bf16[1,8,7168]{2,1,0:T(8,128)(2,1)S(1)} %convert_element_type.139), channel_id=1, source_target_pairs={{0,8},{1,9},{2,10},{3,11},{4,12},{5,13},{6,14},{7,15},{8,0},{9,1},... | collective-permute-start | bytes 344072 | tf_op jit(solution)/shard_map/ppermute | solution.py:25
  8.8 6.7 %collective-permute-start.2 = (f32[2,224,128]{2,1,0:T(8,128)}, f32[2,224,128]{2,1,0:T(8,128)S(1)}, u32[]{:S(2)}, u32[]{:S(2)}) collective-permute-start(f32[2,224,128]{2,1,0:T(8,128)} %bitcast.66), channel_id=1, source_target_pairs={{0,16},{16,0},{1,17},{17,1},{2,18},{18,2},{3,19},{19,3},{4,20},{20... | collective-permute-start | bytes 688136 | tf_op jit(solution)/shard_map/ppermute | solution.py:25
  15.6 8.7 %copy-start.3 = (f32[2,224,128]{2,1,0:T(8,128)}, f32[2,224,128]{2,1,0:T(8,128)S(1)}, u32[]{:S(2)}) copy-start(f32[2,224,128]{2,1,0:T(8,128)S(1)} %collective-permute-done.2.refs_2_) | copy-start | bytes 688132
  15.6 1.6 %copy-start = (bf16[1,128,7168]{2,1,0:T(8,128)(2,1)S(1)}, bf16[1,128,7168]{2,1,0:T(8,128)(2,1)}, u32[]{:S(2)}) copy-start(bf16[1,128,7168]{2,1,0:T(8,128)(2,1)} %param.8) | copy-start | bytes 5505028
  17.2 15.6 %copy-start.1 = (bf16[1,128,7168]{2,1,0:T(8,128)(2,1)S(1)}, bf16[1,128,7168]{2,1,0:T(8,128)(2,1)}, u32[]{:S(2)}) copy-start(bf16[1,128,7168]{2,1,0:T(8,128)(2,1)} %param.8) | copy-start | bytes 5505028
  17.6 1.1 %copy-start.7 = (f32[128,128]{1,0:T(8,128)}, f32[128,128]{1,0:T(8,128)S(1)}, u32[]{:S(2)}) copy-start(f32[128,128]{1,0:T(8,128)S(1)} %shard_map.103.refs_3_) | copy-start | bytes 196612
  17.7 4.9 %collective-permute-start.4 = (bf16[1,8,7168]{2,1,0:T(8,128)(2,1)S(1)}, bf16[1,8,7168]{2,1,0:T(8,128)(2,1)S(1)}, u32[]{:S(2)}, u32[]{:S(2)}) collective-permute-start(bf16[1,8,7168]{2,1,0:T(8,128)(2,1)S(1)} %collective-permute-done.3), channel_id=1, source_target_pairs={{0,4},{1,5},{2,6},{3,7},{4,0},{5,1},{6,2},{7,3},{8,12},{9,13},{10,... | collective-permute-start | bytes 344072 | tf_op jit(solution)/shard_map/ppermute | solution.py:25
  18.2 6.1 %collective-permute-start.5 = (bf16[2,8,7168]{2,1,0:T(8,128)(2,1)S(1)}, bf16[2,8,7168]{2,1,0:T(8,128)(2,1)S(1)}, u32[]{:S(2)}, u32[]{:S(2)}) collective-permute-start(bf16[2,8,7168]{2,1,0:T(8,128)(2,1)S(1)} %pad_maximum_fusion), channel_id=1, source_target_pairs={{0,2},{1,3},{2,0},{3,1},{4,6},{5,7},{6,4},{7,5},{8,10},{9,11},{10,... | collective-permute-start | bytes 688136 | tf_op jit(solution)/shard_map/ppermute | solution.py:25
  18.8 13.1 %collective-permute-start.7 = (bf16[4,8,7168]{2,1,0:T(8,128)(2,1)S(1)}, bf16[4,8,7168]{2,1,0:T(8,128)(2,1)S(1)}, u32[]{:S(2)}, u32[]{:S(2)}) collective-permute-start(bf16[4,8,7168]{2,1,0:T(8,128)(2,1)S(1)} %constant_dynamic-update-slice_fusion.refs_4_), channel_id=1, source_target_pairs={{0,1},{1,0},{2,3},{3,2},{4,5},{5,4},{6,7},{7,6},{8,9},{9,8},{10,11... | collective-permute-start | bytes 1376264 | tf_op jit(solution)/shard_map/ppermute | solution.py:25
  24.3 8.4 %collective-permute-start.8 = (bf16[3,8,7168]{2,1,0:T(8,128)(2,1)S(1)}, bf16[3,8,7168]{2,1,0:T(8,128)(2,1)}, u32[]{:S(2)}, u32[]{:S(2)}) collective-permute-start(bf16[3,8,7168]{2,1,0:T(8,128)(2,1)S(1)} %constant_dynamic-update-slice_fusion.4.refs_5_), channel_id=1, source_target_pairs={{0,1},{1,0},{2,3},{3,2},{4,5},{5,4},{6,7},{7,6},{8,9},{9,8},{10,11... | collective-permute-start | bytes 1032200 | tf_op jit(solution)/shard_map/ppermute | solution.py:25
  24.4 5.6 %collective-permute-start.6 = (bf16[1,8,7168]{2,1,0:T(8,128)(2,1)S(1)}, bf16[1,8,7168]{2,1,0:T(8,128)(2,1)S(1)}, u32[]{:S(2)}, u32[]{:S(2)}) collective-permute-start(bf16[1,8,7168]{2,1,0:T(8,128)(2,1)S(1)} %collective-permute-done.4), channel_id=1, source_target_pairs={{0,2},{1,3},{2,0},{3,1},{4,6},{5,7},{6,4},{7,5},{8,10},{9,11},{10,... | collective-permute-start | bytes 344072 | tf_op jit(solution)/shard_map/ppermute | solution.py:25
  30.0 1.3 %collective-permute-start.9 = (bf16[1,8,7168]{2,1,0:T(8,128)(2,1)S(1)}, bf16[1,8,7168]{2,1,0:T(8,128)(2,1)S(1)}, u32[]{:S(2)}, u32[]{:S(2)}) collective-permute-start(bf16[1,8,7168]{2,1,0:T(8,128)(2,1)S(1)} %collective-permute-done.6.refs_6_), channel_id=1, source_target_pairs={{0,1},{1,0},{2,3},{3,2},{4,5},{5,4},{6,7},{7,6},{8,9},{9,8},{10,11... | collective-permute-start | bytes 344072 | tf_op jit(solution)/shard_map/ppermute | solution.py:25
  30.0 0.6 copy-start.9
  31.3 0.6 copy-start.11
  31.9 0.8 %copy-start.5 = (bf16[4,8,7168]{2,1,0:T(8,128)(2,1)}, bf16[4,8,7168]{2,1,0:T(8,128)(2,1)S(1)}, u32[]{:S(2)}) copy-start(bf16[4,8,7168]{2,1,0:T(8,128)(2,1)S(1)} %collective-permute-done.7.refs_7_) | copy-start | bytes 1376260
  32.7 1.5 %copy-start.2 = (bf16[1,128,7168]{2,1,0:T(8,128)(2,1)S(1)}, bf16[1,128,7168]{2,1,0:T(8,128)(2,1)}, u32[]{:S(2)}) copy-start(bf16[1,128,7168]{2,1,0:T(8,128)(2,1)} %param.9) | copy-start | bytes 5505028
  34.2 1.0 %copy-start.6 = (bf16[4,8,7168]{2,1,0:T(8,128)(2,1)S(1)}, bf16[4,8,7168]{2,1,0:T(8,128)(2,1)}, u32[]{:S(2)}) copy-start(bf16[4,8,7168]{2,1,0:T(8,128)(2,1)} %copy-done.5) | copy-start | bytes 1376260
  35.2 0.8 %copy-start.8 = (f32[128,128]{1,0:T(8,128)S(1)}, f32[128,128]{1,0:T(8,128)}, u32[]{:S(2)}) copy-start(f32[128,128]{1,0:T(8,128)} %copy-done.7) | copy-start | bytes 196612
  36.1 0.9 %copy-start.10 = (bf16[1,8,7168]{2,1,0:T(8,128)(2,1)S(1)}, bf16[1,8,7168]{2,1,0:T(8,128)(2,1)}, u32[]{:S(2)}) copy-start(bf16[1,8,7168]{2,1,0:T(8,128)(2,1)} %copy-done.9) | copy-start | bytes 344068
  37.0 0.9 %copy-start.12 = (bf16[1,8,7168]{2,1,0:T(8,128)(2,1)S(1)}, bf16[1,8,7168]{2,1,0:T(8,128)(2,1)}, u32[]{:S(2)}) copy-start(bf16[1,8,7168]{2,1,0:T(8,128)(2,1)} %copy-done.11) | copy-start | bytes 344068
  46.0 20.4 %copy-start.4 = (f32[2,224,128]{2,1,0:T(8,128)S(1)}, f32[2,224,128]{2,1,0:T(8,128)}, u32[]{:S(2)}) copy-start(f32[2,224,128]{2,1,0:T(8,128)} %copy-done.3) | copy-start | bytes 688132
  46.1 20.4 %copy-start.13 = (f32[1,2,224,128]{3,2,1,0:T(8,128)S(1)}, f32[1,2,224,128]{3,2,1,0:T(8,128)}, u32[]{:S(2)}) copy-start(f32[1,2,224,128]{3,2,1,0:T(8,128)} %param.10) | copy-start | bytes 688132
  46.1 20.3 %copy-start.16 = (f32[224,128]{1,0:T(8,128)S(1)}, f32[224,128]{1,0:T(8,128)}, u32[]{:S(2)}) copy-start(f32[224,128]{1,0:T(8,128)} %param.13) | copy-start | bytes 344068
  46.1 20.3 %copy-start.17 = (f32[224,128]{1,0:T(8,128)S(1)}, f32[224,128]{1,0:T(8,128)}, u32[]{:S(2)}) copy-start(f32[224,128]{1,0:T(8,128)} %param.14) | copy-start | bytes 344068
  46.1 1.4 %collective-permute-start.11 = (bf16[1,8,7168]{2,1,0:T(8,128)(2,1)S(1)}, bf16[1,8,7168]{2,1,0:T(8,128)(2,1)S(1)}, u32[]{:S(2)}, u32[]{:S(2)}) collective-permute-start(bf16[1,8,7168]{2,1,0:T(8,128)(2,1)S(1)} %get-tuple-element.16), channel_id=1, source_target_pairs={{0,1},{1,0},{2,3},{3,2},{4,5},{5,4},{6,7},{7,6},{8,9},{9,8},{10,11... | collective-permute-start | bytes 344072 | tf_op jit(solution)/shard_map/ppermute | solution.py:25
  46.3 2.4 %collective-permute-start.10 = (bf16[4,8,7168]{2,1,0:T(8,128)(2,1)S(1)}, bf16[4,8,7168]{2,1,0:T(8,128)(2,1)S(1)}, u32[]{:S(2)}, u32[]{:S(2)}) collective-permute-start(bf16[4,8,7168]{2,1,0:T(8,128)(2,1)S(1)} %get-tuple-element.15), channel_id=1, source_target_pairs={{0,1},{1,0},{2,3},{3,2},{4,5},{5,4},{6,7},{7,6},{8,9},{9,8},{10,11... | collective-permute-start | bytes 1376264 | tf_op jit(solution)/shard_map/ppermute | solution.py:25
  46.7 2.0 %collective-permute-start.14 = (bf16[3,8,7168]{2,1,0:T(8,128)(2,1)S(1)}, bf16[3,8,7168]{2,1,0:T(8,128)(2,1)S(1)}, u32[]{:S(2)}, u32[]{:S(2)}) collective-permute-start(bf16[3,8,7168]{2,1,0:T(8,128)(2,1)S(1)} %get-tuple-element.18), channel_id=1, source_target_pairs={{0,1},{1,0},{2,3},{3,2},{4,5},{5,4},{6,7},{7,6},{8,9},{9,8},{10,11... | collective-permute-start | bytes 1032200 | tf_op jit(solution)/shard_map/ppermute | solution.py:25
  47.5 5.3 %collective-permute-start.12 = (bf16[8,7168]{1,0:T(8,128)(2,1)S(1)}, bf16[8,7168]{1,0:T(8,128)(2,1)S(1)}, u32[]{:S(2)}, u32[]{:S(2)}) collective-permute-start(bf16[8,7168]{1,0:T(8,128)(2,1)S(1)} %fusion.13), channel_id=1, source_target_pairs={{0,2},{1,3},{2,0},{3,1},{4,6},{5,7},{6,4},{7,5},{8,10},{9,11},{10,... | collective-permute-start | bytes 344072 | tf_op jit(solution)/shard_map/ppermute | solution.py:25
  48.7 21.4 %copy-start.14 = (f32[1,2,224,128]{3,2,1,0:T(8,128)S(1)}, f32[1,2,224,128]{3,2,1,0:T(8,128)}, u32[]{:S(2)}) copy-start(f32[1,2,224,128]{3,2,1,0:T(8,128)} %param.12) | copy-start | bytes 688132
  48.7 21.4 %copy-start.15 = (f32[1,2,224,128]{3,2,1,0:T(8,128)S(1)}, f32[1,2,224,128]{3,2,1,0:T(8,128)}, u32[]{:S(2)}) copy-start(f32[1,2,224,128]{3,2,1,0:T(8,128)} %param.11) | copy-start | bytes 688132
  52.8 4.9 %collective-permute-start.15 = (bf16[8,7168]{1,0:T(8,128)(2,1)S(1)}, bf16[8,7168]{1,0:T(8,128)(2,1)S(1)}, u32[]{:S(2)}, u32[]{:S(2)}) collective-permute-start(bf16[8,7168]{1,0:T(8,128)(2,1)S(1)} %get-tuple-element.20), channel_id=1, source_target_pairs={{0,2},{1,3},{2,0},{3,1},{4,6},{5,7},{6,4},{7,5},{8,10},{9,11},{10,... | collective-permute-start | bytes 344072 | tf_op jit(solution)/shard_map/ppermute | solution.py:25
  53.4 4.8 %collective-permute-start.13 = (bf16[8,7168]{1,0:T(8,128)(2,1)S(1)}, bf16[8,7168]{1,0:T(8,128)(2,1)S(1)}, u32[]{:S(2)}, u32[]{:S(2)}) collective-permute-start(bf16[8,7168]{1,0:T(8,128)(2,1)S(1)} %fusion.7), channel_id=1, source_target_pairs={{0,4},{1,5},{2,6},{3,7},{4,0},{5,1},{6,2},{7,3},{8,12},{9,13},{10,... | collective-permute-start | bytes 344072 | tf_op jit(solution)/shard_map/ppermute | solution.py:25
  58.3 4.9 %collective-permute-start.17 = (bf16[8,7168]{1,0:T(8,128)(2,1)S(1)}, bf16[8,7168]{1,0:T(8,128)(2,1)S(1)}, u32[]{:S(2)}, u32[]{:S(2)}) collective-permute-start(bf16[8,7168]{1,0:T(8,128)(2,1)S(1)} %get-tuple-element.21), channel_id=1, source_target_pairs={{0,2},{1,3},{2,0},{3,1},{4,6},{5,7},{6,4},{7,5},{8,10},{9,11},{10,... | collective-permute-start | bytes 344072 | tf_op jit(solution)/shard_map/ppermute | solution.py:25
  60.6 7.1 %collective-permute-start.16 = (bf16[8,7168]{1,0:T(8,128)(2,1)S(1)}, bf16[8,7168]{1,0:T(8,128)(2,1)S(1)}, u32[]{:S(2)}, u32[]{:S(2)}) collective-permute-start(bf16[8,7168]{1,0:T(8,128)(2,1)S(1)} %fusion.9), channel_id=1, source_target_pairs={{0,8},{1,9},{2,10},{3,11},{4,12},{5,13},{6,14},{7,15},{8,0},{9,1},... | collective-permute-start | bytes 344072 | tf_op jit(solution)/shard_map/ppermute | solution.py:25
  63.2 6.8 %collective-permute-start.18 = (bf16[8,7168]{1,0:T(8,128)(2,1)S(1)}, bf16[8,7168]{1,0:T(8,128)(2,1)S(1)}, u32[]{:S(2)}, u32[]{:S(2)}) collective-permute-start(bf16[8,7168]{1,0:T(8,128)(2,1)S(1)} %fusion.6), channel_id=1, source_target_pairs={{0,4},{1,5},{2,6},{3,7},{4,0},{5,1},{6,2},{7,3},{8,12},{9,13},{10,... | collective-permute-start | bytes 344072 | tf_op jit(solution)/shard_map/ppermute | solution.py:25
  65.1 4.8 %collective-permute-start.19 = (bf16[8,7168]{1,0:T(8,128)(2,1)S(1)}, bf16[8,7168]{1,0:T(8,128)(2,1)S(1)}, u32[]{:S(2)}, u32[]{:S(2)}) collective-permute-start(bf16[8,7168]{1,0:T(8,128)(2,1)S(1)} %get-tuple-element.22), channel_id=1, source_target_pairs={{0,2},{1,3},{2,0},{3,1},{4,6},{5,7},{6,4},{7,5},{8,10},{9,11},{10,... | collective-permute-start | bytes 344072 | tf_op jit(solution)/shard_map/ppermute | solution.py:25

commit v3 on v2

v3 whole, which is shorter than its diff:
```python
import functools
import math

import jax
import jax.numpy as jnp
from jax import lax
from jax.experimental import pallas as pl
from jax.experimental.pallas import tpu as pltpu
from jax.sharding import PartitionSpec as P

norm_eps = 1e-05
beta_one = 0.9
beta_two = 0.95
adam_eps = 1e-08
decay_rate = 0.1
inner_rate = 0.05
outer_rate = 0.7
outer_beta = 0.9
mixing = 0.5
ROWS = 8


def swap(value, axis, mask):
    size = lax.axis_size(axis)
    return lax.ppermute(value, axis, [(i, i ^ mask) for i in range(size)])


def after(value, *others):
    return lax.optimization_barrier((value, *others))[0]


def gather_blocks(own, axis, stage, late):
    size = lax.axis_size(axis)
    single = [k for k in range(4, size, 4) if k & (k - 1) == 0]
    others = [k for k in range(4, size, 4) if k & (k - 1)]
    own = own[None]
    have = {0: own}
    have[4] = swap(own, axis, 4)
    near = swap(own, axis, 2)
    for k in single[1:]:
        have[k] = swap(own, axis, k)
    done = stage((near, have[4]))
    for k in single[1:]:
        have[k] = after(have[k], done)
    for k in others:
        have[k] = swap(have[k & (k - 1)], axis, k & -k)
    first = jnp.concatenate([have[k] for k in single])
    second = jnp.concatenate([have[k] for k in others])
    far_first = swap(first, axis, 2)
    far_second = swap(second, axis, 2)
    sets = [
        ([0, 2] + single, after(jnp.concatenate([own, near, first]), late)),
        (others + [k + 2 for k in single], jnp.concatenate([second, far_first])),
        ([k + 2 for k in others], far_second),
    ]
    crossed = [([k + 1 for k in ks], swap(blocks, axis, 1)) for ks, blocks in sets]
    return sets + crossed


def add_f32(left, right):
    return left.astype(jnp.float32) + right.astype(jnp.float32)


def output_sets(size):
    tops = list(range(size - 4, -1, -4))
    half = len(tops) // 2
    parts = [[k + 2 for k in tops[:half]], [k + 2 for k in tops[half:]], tops]
    return [[k + 1 for k in ks] for ks in parts] + parts


def reduce_blocks(outs, axis):
    size = lax.axis_size(axis)
    tops = list(range(size - 4, -1, -4))
    half = len(tops) // 2
    came = [swap(odd, axis, 1) for odd in outs[:3]]
    sums = add_f32(outs[3], came[0]).astype(jnp.bfloat16)
    near = swap(sums, axis, 2)
    came[1] = after(came[1], sums)
    sums = add_f32(outs[4], came[1]).astype(jnp.bfloat16)
    rest = swap(after(sums, near), axis, 2)
    came[2] = after(came[2], sums)
    kept = add_f32(outs[5], came[2])
    left = {}
    for at, k in enumerate(tops):
        if at == half:
            rest = after(rest, part)
        arrived = near[at] if at < half else rest[at - half]
        left[k] = left.get(k, 0.0) + kept[at] + arrived.astype(jnp.float32)
        if k:
            part = left[k].astype(jnp.bfloat16)
            moved = swap(part, axis, k & -k).astype(jnp.float32)
            left[k & (k - 1)] = left.get(k & (k - 1), 0.0) + moved
    return left[0]


def dot(left, right, precision=None):
    return jnp.dot(left, right, preferred_element_type=jnp.float32, precision=precision)


def squares_of(value, total):
    value = value * value
    for j in range(0, value.shape[1], 128):
        total = total + value[:, j : j + 128]
    return total


def stage_kernel(h_ref, *refs):
    squares = refs[-1]
    width = 1024 if h_ref.shape[1] % 1024 == 0 else 128

    def step(at, total):
        cut = pl.ds(pl.multiple_of(at * width, width), width)
        return squares_of(h_ref[:, cut].astype(jnp.float32), total)

    squares[...] = lax.fori_loop(0, h_ref.shape[1] // width, step, jnp.zeros(squares.shape, jnp.float32))


def stage_tokens(tokens, early):
    return pl.pallas_call(
        stage_kernel,
        out_shape=jax.ShapeDtypeStruct((tokens.shape[0], 128), jnp.float32),
        in_specs=[pl.BlockSpec(memory_space=pltpu.VMEM)] + [pl.BlockSpec(memory_space=pl.ANY)] * len(early),
        out_specs=pl.BlockSpec(memory_space=pltpu.VMEM),
        compiler_params=pltpu.CompilerParams(vmem_limit_bytes=4 * 2**20),
    )(tokens, *early)


def adapter_kernel(n_arrays, sources, places, units, width, *refs):
    upper_ref, h0, g2, squares0 = refs[:4]
    arrays = refs[4 : 4 + n_arrays]
    outs = refs[4 + n_arrays : -3]
    w_ref, wt_ref, h1 = refs[-3:]
    n_pieces = len(sources)
    tokens, model_width = h0.shape
    stacked = n_pieces * ROWS // 2
    hidden = stacked // 2
    in_scale = model_width ** (-0.5)
    out_scale = hidden ** (-0.5)
    steps = model_width // 2 // width
    upper = upper_ref[0]
    half = n_pieces // 2
    w_in, w_out = pl.ds(0, stacked), pl.ds(stacked, stacked)
    layer_of = (lax.broadcasted_iota(jnp.int32, (tokens, stacked), 1) % (2 * units)) // units
    no_squares = jnp.zeros((tokens, 128), jnp.float32)

    def cut(step, side=0):
        return pl.ds(pl.multiple_of(side * (model_width // 2) + step * width, width), width)

    def inv_rms(squares):
        return lax.rsqrt(jnp.sum(squares, axis=1, keepdims=True) / model_width + norm_eps)

    def first(step, total):
        low = cut(step)
        for part in range(2):
            values = []
            for k in range(part * half, part * half + half):
                array, place = sources[k]
                values.append(arrays[array][place, :, low].astype(jnp.float32))
            rows = pl.ds(pl.multiple_of((part ^ upper) * stacked, stacked), stacked)
            for side in range(2):
                block = jnp.concatenate([v[side * ROWS : (side + 1) * ROWS] for v in values])
                w_ref[rows, cut(step, side)] = block.astype(jnp.bfloat16)
        for side in range(2):
            at = cut(step, side)
            turned = w_ref[:, at].T
            wt_ref[at, :] = turned
            total = total + dot(jnp.concatenate([h0[:, at], g2[:, at], w_ref[w_in, at]]), turned)
        return total

    total = jnp.zeros((2 * tokens + stacked, 2 * stacked), jnp.float32)
    total = lax.fori_loop(0, steps, first, total)
    pre0 = total[:tokens, :stacked]
    grad_act = total[tokens : 2 * tokens, stacked:]
    cross = total[2 * tokens :, stacked:]
    inv0 = inv_rms(squares0[...])
    pre0 = pre0 * (inv0 * in_scale)
    sig0 = jax.nn.sigmoid(pre0)
    act0 = jnp.where(layer_of == 0, pre0 * sig0, 0.0)
    act0_low = act0.astype(jnp.bfloat16)

    def second(step, carry):
        both, squares = carry
        for side in range(2):
            at = cut(step, side)
            out = h0[:, at].astype(jnp.float32) + dot(act0_low, w_ref[w_out, at]) * out_scale
            low = out.astype(jnp.bfloat16)
            h1[:, at] = low
            both = both + dot(low, wt_ref[at, :])
            squares = squares_of(low.astype(jnp.float32), squares)
        return both, squares

    both = jnp.zeros((tokens, 2 * stacked), jnp.float32)
    both, squares = lax.fori_loop(0, steps, second, (both, no_squares))
    inv1 = inv_rms(squares)
    pre1 = both[:, :stacked] * (inv1 * in_scale)
    sig1 = jax.nn.sigmoid(pre1)
    act1 = jnp.where(layer_of == 1, pre1 * sig1, 0.0)
    slope1 = sig1 * (1.0 + pre1 * (1.0 - sig1))
    gp1 = jnp.where(layer_of == 1, grad_act * out_scale * slope1, 0.0)
    gp1_low = gp1.astype(jnp.bfloat16)
    gp1 = gp1_low.astype(jnp.float32)
    coef = inv1 * inv1 * jnp.sum(gp1 * pre1, axis=1, keepdims=True) / model_width
    factor = inv1 * in_scale
    grad_act0 = grad_act + factor * dot(gp1, cross, lax.Precision.HIGHEST) - coef * both[:, stacked:]
    slope0 = sig0 * (1.0 + pre0 * (1.0 - sig0))
    gp0 = jnp.where(layer_of == 0, grad_act0 * out_scale * slope0, 0.0)
    act_t = jnp.concatenate([act0.T, act1.T], axis=1).astype(jnp.bfloat16)
    gp_t = jnp.concatenate([(gp0 * inv0).T, (gp1 * inv1).T], axis=1).astype(jnp.bfloat16)

    def third(step, carry):
        terms = []
        for side in range(2):
            at = cut(step, side)
            g1 = (
                g2[:, at].astype(jnp.float32)
                + factor * dot(gp1_low, w_ref[w_in, at])
                - coef * h1[:, at].astype(jnp.float32)
            ).astype(jnp.bfloat16)
            grad_out = dot(act_t, jnp.concatenate([g1, g2[:, at]]))
            grad_in = dot(gp_t, jnp.concatenate([h0[:, at], h1[:, at]]))
            terms.append([jnp.where(upper == part, grad_in, grad_out) for part in range(2)])
        for k in range(n_pieces):
            out, place = places[k]
            part, j = k // half, k % half
            rows = [terms[side][part][j * ROWS : (j + 1) * ROWS] for side in range(2)]
            outs[out][place, :, cut(step)] = jnp.concatenate(rows).astype(jnp.bfloat16)
        return carry

    lax.fori_loop(0, steps, third, 0)


def places_of(sets):
    return {k: (at, place) for at, ks in enumerate(sets) for place, k in enumerate(ks)}


def adapter_grads(upper, tokens, upstream, squares, gathered, units, sets):
    model_width = tokens.shape[1]
    arrays = [array for _, array in gathered]
    sources = places_of([ks for ks, _ in gathered])
    places = places_of(sets)
    width = 512 if model_width % 1024 == 0 else 128
    stacked = len(sources) * ROWS // 2
    whole = pl.BlockSpec(memory_space=pltpu.VMEM)
    shapes = [(len(ks), 2 * ROWS, model_width // 2) for ks in sets]
    return pl.pallas_call(
        functools.partial(adapter_kernel, len(arrays), sources, places, units, width),
        out_shape=[jax.ShapeDtypeStruct(shape, jnp.bfloat16) for shape in shapes],
        in_specs=[pl.BlockSpec(memory_space=pltpu.SMEM)] + [whole] * (3 + len(arrays)),
        out_specs=[whole] * len(sets),
        scratch_shapes=[
            pltpu.VMEM((2 * stacked, model_width), jnp.bfloat16),
            pltpu.VMEM((model_width, 2 * stacked), jnp.bfloat16),
            pltpu.VMEM(tokens.shape, jnp.bfloat16),
        ],
        compiler_params=pltpu.CompilerParams(vmem_limit_bytes=12 * 2**20),
    )(upper, tokens, upstream, squares, *arrays)


def shards(inputs, cotangent, weights, first_moment, second_moment, anchor, momentum, fragment):
    tokens = inputs[0]
    upstream = cotangent[0]
    params = weights[0]
    layers, rows = params.shape[0], params.shape[1]
    model_width = tokens.shape[1]
    groups = lax.axis_size("fsdp")
    replicas = lax.axis_size("rep")
    units = rows * 128 // model_width
    hidden = units * groups // 2
    piece = layers * units
    upper = (lax.axis_index("fsdp") >= groups // 2).astype(jnp.int32).reshape(1)
    count = fragment[0]
    chosen = jnp.remainder(count, layers)
    count_real = count.astype(jnp.float32)
    correct_one = 1.0 - jnp.exp(count_real * math.log(beta_one))
    correct_two = 1.0 - jnp.exp(count_real * math.log(beta_two))
    scale = jnp.where(upper[0] == 1, hidden ** (-0.5), model_width ** (-0.5))
    scale = scale / (tokens.shape[0] * groups)
    compact = params.astype(jnp.bfloat16).reshape(piece, 2, model_width // 2)
    compact = compact.transpose(1, 0, 2).reshape(2 * piece, model_width // 2)
    compact, upper, chosen, correct_one, correct_two, scale = lax.optimization_barrier(
        (compact, upper, chosen, correct_one, correct_two, scale)
    )
    other = swap(params, "rep", 1)
    kept = []

    def stage(blocks):
        kept.append(stage_tokens(tokens, blocks))
        return kept[0]

    gathered = gather_blocks(compact, "fsdp", stage, other)
    squares = kept[0]

    sets = output_sets(groups)
    if piece == ROWS:
        outs = adapter_grads(upper, tokens, upstream, squares, gathered, units, sets)
    else:
        merged = ROWS // piece
        blocks = {k: array[place] for ks, array in gathered for place, k in enumerate(ks)}
        blocks = jnp.stack([blocks[k] for k in range(groups)])
        blocks = blocks.reshape(groups // merged, merged, 2, piece, model_width // 2)
        blocks = blocks.transpose(0, 2, 1, 3, 4).reshape(groups // merged, 2 * ROWS, model_width // 2)
        every = list(range(groups // merged))
        (both,) = adapter_grads(upper, tokens, upstream, squares, [(every, blocks)], units, [every])
        both = both.reshape(groups // merged, 2, merged, piece, model_width // 2)
        both = both.transpose(0, 2, 1, 3, 4).reshape(groups, 2 * piece, model_width // 2)
        outs = [jnp.stack([both[k] for k in ks]) for ks in sets]
    summed = reduce_blocks(outs, "fsdp").reshape(2, piece, model_width // 2)
    summed = summed.transpose(1, 0, 2).reshape(layers, rows, 128)
    gradient = summed * scale

    def delta(values):
        return anchor - lax.dynamic_index_in_dim(values, chosen, 0, keepdims=False)

    total = delta(params) + delta(other)
    step = 2
    while step < replicas:
        total = total + swap(total, "rep", step)
        step *= 2
    moment_one = beta_one * first_moment[0] + (1.0 - beta_one) * gradient
    moment_two = beta_two * second_moment[0] + (1.0 - beta_two) * gradient * gradient
    updated = params - inner_rate * (
        moment_one / correct_one / (jnp.sqrt(moment_two / correct_two) + adam_eps)
        + decay_rate * params
    )
    mean_delta = total / replicas
    new_velocity = outer_beta * momentum + mean_delta
    new_global = anchor - outer_rate * (mean_delta + outer_beta * new_velocity)
    selector = (jnp.arange(layers, dtype=jnp.int32) == chosen)[:, None, None]
    merged = jnp.where(selector, mixing * updated + (1.0 - mixing) * new_global[None], updated)
    return (merged[None], new_global, new_velocity)


def solution(mesh):
    placed = (
        P("rep", "fsdp", None),
        P("rep", "fsdp", None),
        P("rep", None, "fsdp", None),
        P("rep", None, "fsdp", None),
        P("rep", None, "fsdp", None),
        P("fsdp", None),
        P("fsdp", None),
        P(),
    )
    return jax.shard_map(
        shards,
        mesh=mesh,
        in_specs=placed,
        out_specs=(P("rep", None, "fsdp", None), P("fsdp", None), P("fsdp", None)),
        check_vma=False,
    )
```

time: 71.4 us -> 64.5 us (0.903)
  local copies, waits for them, and re-layouts: 9.01 us -> 1.98 us
  Pallas kernels: 8.65 us -> 12.3 us
  starting transfers between devices: 19.2 us -> 16.1 us
    unnamed x40 -> x17, local copies, waits for them, and re-layouts: 8.89 us -> 1.55 us
    pallas_call x1, Pallas kernels: 8.16 us -> 11.8 us  [adapter_grads(): pl.pallas_call(functools.partial(adapter_kernel, len(arrays), sources, pl...]
    ppermute x20 -> x18, starting transfers between devices: 19.2 us -> 16.1 us  [swap(): return lax.ppermute(value, axis, [(i, i ^ mask) for i in range(size)])]
    ppermute x20 -> x18, waiting for transfers between devices: 29.6 us -> 29.3 us  [swap(): return lax.ppermute(value, axis, [(i, i ^ mask) for i in range(size)])]
  transfers between devices with their start and end apart: 20 -> 18, of which waited for: 13 -> 13; matrix products, arithmetic and copies ran while one was open for 1% -> 2% of each run, Pallas kernels for 1% -> 1%
where the time goes in v3:
time: 64.5 us; the launch traced here: 64.3 us
  waiting for transfers between devices  29.3 us (45%)
  starting transfers between devices  16.1 us (25%)
  Pallas kernels  12.3 us (19%)
  other arithmetic  3.03 us (5%)
  local copies, waits for them, and re-layouts  1.98 us (3%)
  between operations  1.57 us (2%)
    ppermute x18, waiting for transfers between devices, swap(): return lax.ppermute(value, axis, [(i, i ^ mask) for i in range(size)])  29.3 us
    ppermute x18, starting transfers between devices, swap(): return lax.ppermute(value, axis, [(i, i ^ mask) for i in range(size)])  16.1 us
    pallas_call x1, Pallas kernels, adapter_grads(): pl.pallas_call(functools.partial(adapter_kernel, len(arrays), sources, pl...  11.8 us
    unnamed x17, local copies, waits for them, and re-layouts  1.55 us
  transfers between devices with their start and end apart: 18, of which 13 were waited for; matrix products, arithmetic and copies ran while one was open for 2% of the time, Pallas kernels for 1%

profile of v3, /device:TPU:0, one launch (start us, length us, event | category | flops | bytes accessed | tf_op | source)
XLA Modules:
  0.0 64.3 jit_solution(12397590565928218402)
XLA Ops:
  1.4 1.0 %convert_element_type.81 = bf16[1,2,224,128]{3,2,1,0:T(8,128)(2,1)S(1)} convert(f32[1,2,224,128]{3,2,1,0:T(8,128)} %param.10) | non-fusion elementwise | flops 57344 | bytes 344064 | tf_op jit(solution)/shard_map/convert_element_type | solution.py:278
  2.4 3.1 %collective-permute-start.1 = (bf16[1,16,3584]{2,1,0:T(8,128)(2,1)S(1)}, bf16[1,16,3584]{2,1,0:T(8,128)(2,1)S(1)}, u32[]{:S(2)}, u32[]{:S(2)}) collective-permute-start(bf16[1,16,3584]{2,1,0:T(8,128)(2,1)S(1)} %bitcast.77), channel_id=1, source_target_pairs={{0,4},{1,5},{2,6},{3,7},{4,0},{5,1},{6,2},{7,3},{8,12},{9,13},{10,... | collective-permute-start | bytes 344072 | tf_op jit(solution)/shard_map/ppermute | solution.py:25
  5.5 1.5 %collective-permute-start = (bf16[1,16,3584]{2,1,0:T(8,128)(2,1)S(1)}, bf16[1,16,3584]{2,1,0:T(8,128)(2,1)S(1)}, u32[]{:S(2)}, u32[]{:S(2)}) collective-permute-start(bf16[1,16,3584]{2,1,0:T(8,128)(2,1)S(1)} %bitcast.78), channel_id=1, source_target_pairs={{0,2},{1,3},{2,0},{3,1},{4,6},{5,7},{6,4},{7,5},{8,10},{9,11},{10,... | collective-permute-start | bytes 344072 | tf_op jit(solution)/shard_map/ppermute | solution.py:25
  7.0 2.6 %collective-permute-start.2 = (bf16[1,16,3584]{2,1,0:T(8,128)(2,1)S(1)}, bf16[1,16,3584]{2,1,0:T(8,128)(2,1)S(1)}, u32[]{:S(2)}, u32[]{:S(2)}) collective-permute-start(bf16[1,16,3584]{2,1,0:T(8,128)(2,1)S(1)} %bitcast.79), channel_id=1, source_target_pairs={{0,8},{1,9},{2,10},{3,11},{4,12},{5,13},{6,14},{7,15},{8,0},{9,1},... | collective-permute-start | bytes 344072 | tf_op jit(solution)/shard_map/ppermute | solution.py:25
  9.6 1.5 %collective-permute-start.3 = (f32[2,224,128]{2,1,0:T(8,128)}, f32[2,224,128]{2,1,0:T(8,128)S(1)}, u32[]{:S(2)}, u32[]{:S(2)}) collective-permute-start(f32[2,224,128]{2,1,0:T(8,128)} %bitcast.76), channel_id=1, source_target_pairs={{0,16},{16,0},{1,17},{17,1},{2,18},{18,2},{3,19},{19,3},{4,20},{20... | collective-permute-start | bytes 688136 | tf_op jit(solution)/shard_map/ppermute | solution.py:25
  11.1 0.0 collective-permute-done.1.refs_1_
  11.1 0.0 collective-permute-done.refs_0_
  11.1 1.5 %copy-done = bf16[1,128,7168]{2,1,0:T(8,128)(2,1)S(1)} copy-done((bf16[1,128,7168]{2,1,0:T(8,128)(2,1)S(1)}, bf16[1,128,7168]{2,1,0:T(8,128)(2,1)}, u32[]{:S(2)}) %copy-start) | copy-done | bytes 1835032
  12.6 0.5 shard_map.103.refs_3_
  13.1 1.6 %collective-permute-done.2 = bf16[1,16,3584]{2,1,0:T(8,128)(2,1)S(1)} collective-permute-done((bf16[1,16,3584]{2,1,0:T(8,128)(2,1)S(1)}, bf16[1,16,3584]{2,1,0:T(8,128)(2,1)S(1)}, u32[]{:S(2)}, u32[]{:S(2)}) %collective-permute-start.2) | collective-permute-done | bytes 114720 | tf_op jit(solution)/shard_map/ppermute | solution.py:25
  14.7 0.9 %collective-permute-start.5 = (bf16[2,16,3584]{2,1,0:T(8,128)(2,1)S(1)}, bf16[2,16,3584]{2,1,0:T(8,128)(2,1)S(1)}, u32[]{:S(2)}, u32[]{:S(2)}) collective-permute-start(bf16[2,16,3584]{2,1,0:T(8,128)(2,1)S(1)} %pad_maximum_fusion.1), channel_id=1, source_target_pairs={{0,2},{1,3},{2,0},{3,1},{4,6},{5,7},{6,4},{7,5},{8,10},{9,11},{10,... | collective-permute-start | bytes 688136 | tf_op jit(solution)/shard_map/ppermute | solution.py:25
  15.6 0.1 pad_maximum_fusion.refs_4_
  15.6 0.7 %collective-permute-done.3 = f32[2,224,128]{2,1,0:T(8,128)S(1)} collective-permute-done((f32[2,224,128]{2,1,0:T(8,128)}, f32[2,224,128]{2,1,0:T(8,128)S(1)}, u32[]{:S(2)}, u32[]{:S(2)}) %collective-permute-start.3) | collective-permute-done | bytes 229408 | tf_op jit(solution)/shard_map/ppermute | solution.py:25
  16.3 3.1 %collective-permute-done.4 = bf16[1,16,3584]{2,1,0:T(8,128)(2,1)S(1)} collective-permute-done((bf16[1,16,3584]{2,1,0:T(8,128)(2,1)S(1)}, bf16[1,16,3584]{2,1,0:T(8,128)(2,1)S(1)}, u32[]{:S(2)}, u32[]{:S(2)}) %collective-permute-start.4) | collective-permute-done | bytes 114720 | tf_op jit(solution)/shard_map/ppermute | solution.py:25
  19.5 2.0 %collective-permute-done.5 = bf16[2,16,3584]{2,1,0:T(8,128)(2,1)S(1)} collective-permute-done((bf16[2,16,3584]{2,1,0:T(8,128)(2,1)S(1)}, bf16[2,16,3584]{2,1,0:T(8,128)(2,1)S(1)}, u32[]{:S(2)}, u32[]{:S(2)}) %collective-permute-start.5) | collective-permute-done | bytes 229408 | tf_op jit(solution)/shard_map/ppermute | solution.py:25
  21.5 0.1 collective-permute-start.8
  21.6 0.4 collective-permute-start.6
  21.9 5.2 %collective-permute-done.6.refs_6_ = bf16[1,16,3584]{2,1,0:T(8,128)(2,1)S(1)} collective-permute-done((bf16[1,16,3584]{2,1,0:T(8,128)(2,1)S(1)}, bf16[1,16,3584]{2,1,0:T(8,128)(2,1)S(1)}, u32[]{:S(2)}, u32[]{:S(2)}) %collective-permute-start.6) | collective-permute-done | bytes 114720 | tf_op jit(solution)/shard_map/ppermute | solution.py:25
  27.1 1.3 %collective-permute-done.9.refs_9_ = bf16[1,16,3584]{2,1,0:T(8,128)(2,1)S(1)} collective-permute-done((bf16[1,16,3584]{2,1,0:T(8,128)(2,1)S(1)}, bf16[1,16,3584]{2,1,0:T(8,128)(2,1)S(1)}, u32[]{:S(2)}, u32[]{:S(2)}) %collective-permute-start.9) | collective-permute-done | bytes 114720 | tf_op jit(solution)/shard_map/ppermute | solution.py:25
  28.5 11.8 %shard_map.104 = (bf16[2,16,3584]{2,1,0:T(8,128)(2,1)S(1)}, bf16[2,16,3584]{2,1,0:T(8,128)(2,1)S(1)}, bf16[4,16,3584]{2,1,0:T(8,128)(2,1)S(1)}, bf16[2,16,3584]{...) custom-call(s32[1]{0:T(128)} %bitcast.2.refs_0_, ...), custom_call_target="tpu_custom_call" | custom-call | tf_op jit(solution)/shard_map/pallas_call | solution.py:245
  40.3 0.2 collective-permute-start.12
  40.5 0.4 collective-permute-start.11
  40.9 0.1 collective-permute-start.10
  41.0 0.8 %collective-permute-done.12 = bf16[2,16,3584]{2,1,0:T(8,128)(2,1)S(1)} collective-permute-done((bf16[2,16,3584]{2,1,0:T(8,128)(2,1)S(1)}, bf16[2,16,3584]{2,1,0:T(8,128)(2,1)S(1)}, u32[]{:S(2)}, u32[]{:S(2)}) %collective-permute-start.12) | collective-permute-done | bytes 229408 | tf_op jit(solution)/shard_map/ppermute | solution.py:25
  41.8 0.1 add_convert_fusion.1
  41.9 0.4 collective-permute-start.13
  42.3 0.1 add_convert_fusion
  42.3 0.0 copy-start.3
  42.3 0.0 copy-start.6
  42.3 0.0 copy-start.7
  42.4 0.5 collective-permute-done.10
  42.8 0.1 convert_add_fusion
  42.9 6.7 %collective-permute-done.13 = bf16[2,16,3584]{2,1,0:T(8,128)(2,1)S(1)} collective-permute-done((bf16[2,16,3584]{2,1,0:T(8,128)(2,1)S(1)}, bf16[2,16,3584]{2,1,0:T(8,128)(2,1)S(1)}, u32[]{:S(2)}, u32[]{:S(2)}) %collective-permute-start.13) | collective-permute-done | bytes 229408 | tf_op jit(solution)/shard_map/ppermute | solution.py:25
  49.6 0.0 copy-start.4
  49.7 0.0 copy-start.5
  49.7 1.8 %collective-permute-start.14 = (bf16[16,3584]{1,0:T(8,128)(2,1)S(1)}, bf16[16,3584]{1,0:T(8,128)(2,1)S(1)}, u32[]{:S(2)}, u32[]{:S(2)}) collective-permute-start(bf16[16,3584]{1,0:T(8,128)(2,1)S(1)} %fusion.15), channel_id=1, source_target_pairs={{0,4},{1,5},{2,6},{3,7},{4,0},{5,1},{6,2},{7,3},{8,12},{9,13},{10,... | collective-permute-start | bytes 344072 | tf_op jit(solution)/shard_map/ppermute | solution.py:25
  51.5 0.3 collective-permute-start.16
  51.8 2.8 %collective-permute-done.14 = bf16[16,3584]{1,0:T(8,128)(2,1)S(1)} collective-permute-done((bf16[16,3584]{1,0:T(8,128)(2,1)S(1)}, bf16[16,3584]{1,0:T(8,128)(2,1)S(1)}, u32[]{:S(2)}, u32[]{:S(2)}) %collective-permute-start.14) | collective-permute-done | bytes 114720 | tf_op jit(solution)/shard_map/ppermute | solution.py:25
  54.6 2.5 %collective-permute-start.15 = (bf16[16,3584]{1,0:T(8,128)(2,1)S(1)}, bf16[16,3584]{1,0:T(8,128)(2,1)S(1)}, u32[]{:S(2)}, u32[]{:S(2)}) collective-permute-start(bf16[16,3584]{1,0:T(8,128)(2,1)S(1)} %fusion.13), channel_id=1, source_target_pairs={{0,8},{1,9},{2,10},{3,11},{4,12},{5,13},{6,14},{7,15},{8,0},{9,1},... | collective-permute-start | bytes 344072 | tf_op jit(solution)/shard_map/ppermute | solution.py:25
  57.1 0.9 %collective-permute-done.16 = bf16[2,16,3584]{2,1,0:T(8,128)(2,1)S(1)} collective-permute-done((bf16[2,16,3584]{2,1,0:T(8,128)(2,1)S(1)}, bf16[2,16,3584]{2,1,0:T(8,128)(2,1)S(1)}, u32[]{:S(2)}, u32[]{:S(2)}) %collective-permute-start.16) | collective-permute-done | bytes 229408 | tf_op jit(solution)/shard_map/ppermute | solution.py:25
  58.1 0.4 collective-permute-start.17
  58.5 0.7 %broadcast_multiply_fusion = (f32[224,128]{1,0:T(8,128)S(1)}, f32[224,128]{1,0:T(8,128)}, f32[224,128]{1,0:T(8,128)}) fusion(f32[224,128]{1,0:T(8,128)S(1)} %copy-done.6, f32[2,224,128]{2,1,0:T(8,128)S(1)} %collective-permute-done.3, s32[]{:T(128)S(6)} %select_n.23, f32[1,2,224,128]{3,2,1,0:T(8,128)S(1)} %copy-done.3, f32[224,128]{1,0:T(8,128)S(1)} %copy-done.7), kind=kLoop, calls=%fused_computation.36 | loop fusion | flops 315392 | bytes 802820 | tf_op jit(solution)/shard_map/mul | solution.py:329
  59.2 1.2 %collective-permute-done.15 = bf16[16,3584]{1,0:T(8,128)(2,1)S(1)} collective-permute-done((bf16[16,3584]{1,0:T(8,128)(2,1)S(1)}, bf16[16,3584]{1,0:T(8,128)(2,1)S(1)}, u32[]{:S(2)}, u32[]{:S(2)}) %collective-permute-start.15) | collective-permute-done | bytes 114720 | tf_op jit(solution)/shard_map/ppermute | solution.py:25
  60.4 2.5 %collective-permute-done.17 = bf16[16,3584]{1,0:T(8,128)(2,1)S(1)} collective-permute-done((bf16[16,3584]{1,0:T(8,128)(2,1)S(1)}, bf16[16,3584]{1,0:T(8,128)(2,1)S(1)}, u32[]{:S(2)}, u32[]{:S(2)}) %collective-permute-start.17) | collective-permute-done | bytes 114720 | tf_op jit(solution)/shard_map/ppermute | solution.py:25
  62.9 0.1 fusion.9
  63.0 0.2 copy.12
  63.2 0.2 mul.115
  63.4 0.9 %add_select_fusion = f32[1,2,224,128]{3,2,1,0:T(8,128)} fusion(f32[1,2,224,128]{3,2,1,0:T(8,128)S(1)} %copy-done.3, f32[1,2,224,128]{3,2,1,0:T(8,128)S(1)} %mul.115, f32[1,2,224,128]{3,2,1,0:T(8,128)S(1)} %copy-done.4, f32[1,2,224,128]{3,2,1,0:T(8,128)S(1)} %copy-done.5, f32[224,128]{1,0:T(8,128)S(1)} %get-tuple-element.39, f32[]{:T(128)S(6)} %sub.20, ...), kind=kLoop, calls=%fused_computation.25 | loop fusion | flops 1032192 | bytes 1261578 | tf_op jit(solution)/shard_map/jit(_where)/select_n | solution.py:329
  (25 shorter events, 0.2 us)
Async XLA Ops:
  2.4 8.7 %collective-permute-start.1 = (bf16[1,16,3584]{2,1,0:T(8,128)(2,1)S(1)}, bf16[1,16,3584]{2,1,0:T(8,128)(2,1)S(1)}, u32[]{:S(2)}, u32[]{:S(2)}) collective-permute-start(bf16[1,16,3584]{2,1,0:T(8,128)(2,1)S(1)} %bitcast.77), channel_id=1, source_target_pairs={{0,4},{1,5},{2,6},{3,7},{4,0},{5,1},{6,2},{7,3},{8,12},{9,13},{10,... | collective-permute-start | bytes 344072 | tf_op jit(solution)/shard_map/ppermute | solution.py:25
  5.5 5.6 %collective-permute-start = (bf16[1,16,3584]{2,1,0:T(8,128)(2,1)S(1)}, bf16[1,16,3584]{2,1,0:T(8,128)(2,1)S(1)}, u32[]{:S(2)}, u32[]{:S(2)}) collective-permute-start(bf16[1,16,3584]{2,1,0:T(8,128)(2,1)S(1)} %bitcast.78), channel_id=1, source_target_pairs={{0,2},{1,3},{2,0},{3,1},{4,6},{5,7},{6,4},{7,5},{8,10},{9,11},{10,... | collective-permute-start | bytes 344072 | tf_op jit(solution)/shard_map/ppermute | solution.py:25
  7.0 7.6 %collective-permute-start.2 = (bf16[1,16,3584]{2,1,0:T(8,128)(2,1)S(1)}, bf16[1,16,3584]{2,1,0:T(8,128)(2,1)S(1)}, u32[]{:S(2)}, u32[]{:S(2)}) collective-permute-start(bf16[1,16,3584]{2,1,0:T(8,128)(2,1)S(1)} %bitcast.79), channel_id=1, source_target_pairs={{0,8},{1,9},{2,10},{3,11},{4,12},{5,13},{6,14},{7,15},{8,0},{9,1},... | collective-permute-start | bytes 344072 | tf_op jit(solution)/shard_map/ppermute | solution.py:25
  9.6 6.7 %collective-permute-start.3 = (f32[2,224,128]{2,1,0:T(8,128)}, f32[2,224,128]{2,1,0:T(8,128)S(1)}, u32[]{:S(2)}, u32[]{:S(2)}) collective-permute-start(f32[2,224,128]{2,1,0:T(8,128)} %bitcast.76), channel_id=1, source_target_pairs={{0,16},{16,0},{1,17},{17,1},{2,18},{18,2},{3,19},{19,3},{4,20},{20... | collective-permute-start | bytes 688136 | tf_op jit(solution)/shard_map/ppermute | solution.py:25
  11.1 1.5 %copy-start = (bf16[1,128,7168]{2,1,0:T(8,128)(2,1)S(1)}, bf16[1,128,7168]{2,1,0:T(8,128)(2,1)}, u32[]{:S(2)}) copy-start(bf16[1,128,7168]{2,1,0:T(8,128)(2,1)} %param.8) | copy-start | bytes 5505028
  12.6 15.8 %copy-start.1 = (bf16[1,128,7168]{2,1,0:T(8,128)(2,1)S(1)}, bf16[1,128,7168]{2,1,0:T(8,128)(2,1)}, u32[]{:S(2)}) copy-start(bf16[1,128,7168]{2,1,0:T(8,128)(2,1)} %param.8) | copy-start | bytes 5505028
  12.6 15.8 %copy-start.2 = (bf16[1,128,7168]{2,1,0:T(8,128)(2,1)S(1)}, bf16[1,128,7168]{2,1,0:T(8,128)(2,1)}, u32[]{:S(2)}) copy-start(bf16[1,128,7168]{2,1,0:T(8,128)(2,1)} %param.9) | copy-start | bytes 5505028
  14.7 4.8 %collective-permute-start.4 = (bf16[1,16,3584]{2,1,0:T(8,128)(2,1)S(1)}, bf16[1,16,3584]{2,1,0:T(8,128)(2,1)S(1)}, u32[]{:S(2)}, u32[]{:S(2)}) collective-permute-start(bf16[1,16,3584]{2,1,0:T(8,128)(2,1)S(1)} %collective-permute-done.2), channel_id=1, source_target_pairs={{0,4},{1,5},{2,6},{3,7},{4,0},{5,1},{6,2},{7,3},{8,12},{9,13},{10,... | collective-permute-start | bytes 344072 | tf_op jit(solution)/shard_map/ppermute | solution.py:25
  14.7 6.8 %collective-permute-start.5 = (bf16[2,16,3584]{2,1,0:T(8,128)(2,1)S(1)}, bf16[2,16,3584]{2,1,0:T(8,128)(2,1)S(1)}, u32[]{:S(2)}, u32[]{:S(2)}) collective-permute-start(bf16[2,16,3584]{2,1,0:T(8,128)(2,1)S(1)} %pad_maximum_fusion.1), channel_id=1, source_target_pairs={{0,2},{1,3},{2,0},{3,1},{4,6},{5,7},{6,4},{7,5},{8,10},{9,11},{10,... | collective-permute-start | bytes 688136 | tf_op jit(solution)/shard_map/ppermute | solution.py:25
  16.3 12.1 %collective-permute-start.7 = (bf16[4,16,3584]{2,1,0:T(8,128)(2,1)S(1)}, bf16[4,16,3584]{2,1,0:T(8,128)(2,1)S(1)}, u32[]{:S(2)}, u32[]{:S(2)}) collective-permute-start(bf16[4,16,3584]{2,1,0:T(8,128)(2,1)S(1)} %pad_maximum_fusion.refs_4_), channel_id=1, source_target_pairs={{0,1},{1,0},{2,3},{3,2},{4,5},{5,4},{6,7},{7,6},{8,9},{9,8},{10,11... | collective-permute-start | bytes 1376264 | tf_op jit(solution)/shard_map/ppermute | solution.py:25
  21.5 7.0 %collective-permute-start.8 = (bf16[3,16,3584]{2,1,0:T(8,128)(2,1)S(1)}, bf16[3,16,3584]{2,1,0:T(8,128)(2,1)S(1)}, u32[]{:S(2)}, u32[]{:S(2)}) collective-permute-start(bf16[3,16,3584]{2,1,0:T(8,128)(2,1)S(1)} %constant_dynamic-update-slice_fusion.refs_5_), channel_id=1, source_target_pairs={{0,1},{1,0},{2,3},{3,2},{4,5},{5,4},{6,7},{7,6},{8,9},{9,8},{10,11... | collective-permute-start | bytes 1032200 | tf_op jit(solution)/shard_map/ppermute | solution.py:25
  21.6 5.6 %collective-permute-start.6 = (bf16[1,16,3584]{2,1,0:T(8,128)(2,1)S(1)}, bf16[1,16,3584]{2,1,0:T(8,128)(2,1)S(1)}, u32[]{:S(2)}, u32[]{:S(2)}) collective-permute-start(bf16[1,16,3584]{2,1,0:T(8,128)(2,1)S(1)} %collective-permute-done.4), channel_id=1, source_target_pairs={{0,2},{1,3},{2,0},{3,1},{4,6},{5,7},{6,4},{7,5},{8,10},{9,11},{10,... | collective-permute-start | bytes 344072 | tf_op jit(solution)/shard_map/ppermute | solution.py:25
  27.1 1.3 %collective-permute-start.9 = (bf16[1,16,3584]{2,1,0:T(8,128)(2,1)S(1)}, bf16[1,16,3584]{2,1,0:T(8,128)(2,1)S(1)}, u32[]{:S(2)}, u32[]{:S(2)}) collective-permute-start(bf16[1,16,3584]{2,1,0:T(8,128)(2,1)S(1)} %collective-permute-done.6.refs_6_), channel_id=1, source_target_pairs={{0,1},{1,0},{2,3},{3,2},{4,5},{5,4},{6,7},{7,6},{8,9},{9,8},{10,11... | collective-permute-start | bytes 344072 | tf_op jit(solution)/shard_map/ppermute | solution.py:25
  40.3 1.6 %collective-permute-start.12 = (bf16[2,16,3584]{2,1,0:T(8,128)(2,1)S(1)}, bf16[2,16,3584]{2,1,0:T(8,128)(2,1)S(1)}, u32[]{:S(2)}, u32[]{:S(2)}) collective-permute-start(bf16[2,16,3584]{2,1,0:T(8,128)(2,1)S(1)} %get-tuple-element.31), channel_id=1, source_target_pairs={{0,1},{1,0},{2,3},{3,2},{4,5},{5,4},{6,7},{7,6},{8,9},{9,8},{10,11... | collective-permute-start | bytes 688136 | tf_op jit(solution)/shard_map/ppermute | solution.py:25
  40.5 1.8 %collective-permute-start.11 = (bf16[2,16,3584]{2,1,0:T(8,128)(2,1)S(1)}, bf16[2,16,3584]{2,1,0:T(8,128)(2,1)S(1)}, u32[]{:S(2)}, u32[]{:S(2)}) collective-permute-start(bf16[2,16,3584]{2,1,0:T(8,128)(2,1)S(1)} %get-tuple-element.29), channel_id=1, source_target_pairs={{0,1},{1,0},{2,3},{3,2},{4,5},{5,4},{6,7},{7,6},{8,9},{9,8},{10,11... | collective-permute-start | bytes 688136 | tf_op jit(solution)/shard_map/ppermute | solution.py:25
  40.9 2.0 %collective-permute-start.10 = (bf16[4,16,3584]{2,1,0:T(8,128)(2,1)S(1)}, bf16[4,16,3584]{2,1,0:T(8,128)(2,1)S(1)}, u32[]{:S(2)}, u32[]{:S(2)}) collective-permute-start(bf16[4,16,3584]{2,1,0:T(8,128)(2,1)S(1)} %get-tuple-element.27), channel_id=1, source_target_pairs={{0,1},{1,0},{2,3},{3,2},{4,5},{5,4},{6,7},{7,6},{8,9},{9,8},{10,11... | collective-permute-start | bytes 1376264 | tf_op jit(solution)/shard_map/ppermute | solution.py:25
  41.9 7.7 %collective-permute-start.13 = (bf16[2,16,3584]{2,1,0:T(8,128)(2,1)S(1)}, bf16[2,16,3584]{2,1,0:T(8,128)(2,1)S(1)}, u32[]{:S(2)}, u32[]{:S(2)}) collective-permute-start(bf16[2,16,3584]{2,1,0:T(8,128)(2,1)S(1)} %add_convert_fusion.1), channel_id=1, source_target_pairs={{0,2},{1,3},{2,0},{3,1},{4,6},{5,7},{6,4},{7,5},{8,10},{9,11},{10,... | collective-permute-start | bytes 688136 | tf_op jit(solution)/shard_map/ppermute | solution.py:25
  42.3 16.2 %copy-start.3 = (f32[1,2,224,128]{3,2,1,0:T(8,128)S(1)}, f32[1,2,224,128]{3,2,1,0:T(8,128)}, u32[]{:S(2)}) copy-start(f32[1,2,224,128]{3,2,1,0:T(8,128)} %param.10) | copy-start | bytes 688132
  42.3 16.2 %copy-start.6 = (f32[224,128]{1,0:T(8,128)S(1)}, f32[224,128]{1,0:T(8,128)}, u32[]{:S(2)}) copy-start(f32[224,128]{1,0:T(8,128)} %param.13) | copy-start | bytes 344068
  42.3 16.2 %copy-start.7 = (f32[224,128]{1,0:T(8,128)S(1)}, f32[224,128]{1,0:T(8,128)}, u32[]{:S(2)}) copy-start(f32[224,128]{1,0:T(8,128)} %param.14) | copy-start | bytes 344068
  49.6 13.7 %copy-start.4 = (f32[1,2,224,128]{3,2,1,0:T(8,128)S(1)}, f32[1,2,224,128]{3,2,1,0:T(8,128)}, u32[]{:S(2)}) copy-start(f32[1,2,224,128]{3,2,1,0:T(8,128)} %param.12) | copy-start | bytes 688132
  49.7 13.7 %copy-start.5 = (f32[1,2,224,128]{3,2,1,0:T(8,128)S(1)}, f32[1,2,224,128]{3,2,1,0:T(8,128)}, u32[]{:S(2)}) copy-start(f32[1,2,224,128]{3,2,1,0:T(8,128)} %param.11) | copy-start | bytes 688132
  49.7 4.9 %collective-permute-start.14 = (bf16[16,3584]{1,0:T(8,128)(2,1)S(1)}, bf16[16,3584]{1,0:T(8,128)(2,1)S(1)}, u32[]{:S(2)}, u32[]{:S(2)}) collective-permute-start(bf16[16,3584]{1,0:T(8,128)(2,1)S(1)} %fusion.15), channel_id=1, source_target_pairs={{0,4},{1,5},{2,6},{3,7},{4,0},{5,1},{6,2},{7,3},{8,12},{9,13},{10,... | collective-permute-start | bytes 344072 | tf_op jit(solution)/shard_map/ppermute | solution.py:25
  51.5 6.5 %collective-permute-start.16 = (bf16[2,16,3584]{2,1,0:T(8,128)(2,1)S(1)}, bf16[2,16,3584]{2,1,0:T(8,128)(2,1)S(1)}, u32[]{:S(2)}, u32[]{:S(2)}) collective-permute-start(bf16[2,16,3584]{2,1,0:T(8,128)(2,1)S(1)} %add_convert_fusion), channel_id=1, source_target_pairs={{0,2},{1,3},{2,0},{3,1},{4,6},{5,7},{6,4},{7,5},{8,10},{9,11},{10,... | collective-permute-start | bytes 688136 | tf_op jit(solution)/shard_map/ppermute | solution.py:25
  54.6 5.9 %collective-permute-start.15 = (bf16[16,3584]{1,0:T(8,128)(2,1)S(1)}, bf16[16,3584]{1,0:T(8,128)(2,1)S(1)}, u32[]{:S(2)}, u32[]{:S(2)}) collective-permute-start(bf16[16,3584]{1,0:T(8,128)(2,1)S(1)} %fusion.13), channel_id=1, source_target_pairs={{0,8},{1,9},{2,10},{3,11},{4,12},{5,13},{6,14},{7,15},{8,0},{9,1},... | collective-permute-start | bytes 344072 | tf_op jit(solution)/shard_map/ppermute | solution.py:25
  58.1 4.9 %collective-permute-start.17 = (bf16[16,3584]{1,0:T(8,128)(2,1)S(1)}, bf16[16,3584]{1,0:T(8,128)(2,1)S(1)}, u32[]{:S(2)}, u32[]{:S(2)}) collective-permute-start(bf16[16,3584]{1,0:T(8,128)(2,1)S(1)} %fusion.16), channel_id=1, source_target_pairs={{0,4},{1,5},{2,6},{3,7},{4,0},{5,1},{6,2},{7,3},{8,12},{9,13},{10,... | collective-permute-start | bytes 344072 | tf_op jit(solution)/shard_map/ppermute | solution.py:25

commit v4 on v3

--- a/solution.py
+++ b/solution.py
@@ -35,23 +35,19 @@
     others = [k for k in range(4, size, 4) if k & (k - 1)]
     own = own[None]
     have = {0: own}
-    have[4] = swap(own, axis, 4)
+    for k in reversed(single):
+        have[k] = swap(own, axis, k)
     near = swap(own, axis, 2)
-    for k in single[1:]:
-        have[k] = swap(own, axis, k)
-    done = stage((near, have[4]))
-    for k in single[1:]:
-        have[k] = after(have[k], done)
     for k in others:
         have[k] = swap(have[k & (k - 1)], axis, k & -k)
     first = jnp.concatenate([have[k] for k in single])
     second = jnp.concatenate([have[k] for k in others])
     far_first = swap(first, axis, 2)
+    second = after(second, stage((have[single[-1]],)))
     far_second = swap(second, axis, 2)
     sets = [
         ([0, 2] + single, after(jnp.concatenate([own, near, first]), late)),
-        (others + [k + 2 for k in single], jnp.concatenate([second, far_first])),
-        ([k + 2 for k in others], far_second),
+        (others + [k + 2 for k in single + others], jnp.concatenate([second, far_first, far_second])),
     ]
     crossed = [([k + 1 for k in ks], swap(blocks, axis, 1)) for ks, blocks in sets]
     return sets + crossed
@@ -72,14 +68,15 @@
     size = lax.axis_size(axis)
     tops = list(range(size - 4, -1, -4))
     half = len(tops) // 2
-    came = [swap(odd, axis, 1) for odd in outs[:3]]
-    sums = add_f32(outs[3], came[0]).astype(jnp.bfloat16)
-    near = swap(sums, axis, 2)
-    came[1] = after(came[1], sums)
-    sums = add_f32(outs[4], came[1]).astype(jnp.bfloat16)
-    rest = swap(after(sums, near), axis, 2)
-    came[2] = after(came[2], sums)
-    kept = add_f32(outs[5], came[2])
+    came = swap(outs[0], axis, 1)
+    sums = add_f32(outs[3], came).astype(jnp.bfloat16)
+    near = [swap(sums[at], axis, 2) for at in range(half)]
+    odd, last_odd, sums = lax.optimization_barrier((outs[1], outs[2], sums))
+    came = swap(odd, axis, 1)
+    sums = add_f32(outs[4], came).astype(jnp.bfloat16)
+    rest = swap(sums, axis, 2)
+    near[0] = after(near[0], sums)
+    kept = add_f32(outs[5], swap(last_odd, axis, 1))
     left = {}
     for at, k in enumerate(tops):
         if at == half:
@@ -93,6 +90,10 @@
     return left[0]
 
 
+def dot_nt(left, right):
+    return lax.dot_general(left, right, (((1,), (1,)), ((), ())), preferred_element_type=jnp.float32)
+
+
 def dot(left, right, precision=None):
     return jnp.dot(left, right, preferred_element_type=jnp.float32, precision=precision)
 
@@ -128,8 +129,8 @@
 def adapter_kernel(n_arrays, sources, places, units, width, *refs):
     upper_ref, h0, g2, squares0 = refs[:4]
     arrays = refs[4 : 4 + n_arrays]
-    outs = refs[4 + n_arrays : -3]
-    w_ref, wt_ref, h1 = refs[-3:]
+    outs = refs[4 + n_arrays : -2]
+    w_ref, h1 = refs[-2:]
     n_pieces = len(sources)
     tokens, model_width = h0.shape
     stacked = n_pieces * ROWS // 2
@@ -162,9 +163,7 @@
                 w_ref[rows, cut(step, side)] = block.astype(jnp.bfloat16)
         for side in range(2):
             at = cut(step, side)
-            turned = w_ref[:, at].T
-            wt_ref[at, :] = turned
-            total = total + dot(jnp.concatenate([h0[:, at], g2[:, at], w_ref[w_in, at]]), turned)
+            total = total + dot_nt(jnp.concatenate([h0[:, at], g2[:, at], w_ref[w_in, at]]), w_ref[:, at])
         return total
 
     total = jnp.zeros((2 * tokens + stacked, 2 * stacked), jnp.float32)
@@ -185,7 +184,7 @@
             out = h0[:, at].astype(jnp.float32) + dot(act0_low, w_ref[w_out, at]) * out_scale
             low = out.astype(jnp.bfloat16)
             h1[:, at] = low
-            both = both + dot(low, wt_ref[at, :])
+            both = both + dot_nt(low, w_ref[:, at])
             squares = squares_of(low.astype(jnp.float32), squares)
         return both, squares
 
@@ -238,7 +237,7 @@
     arrays = [array for _, array in gathered]
     sources = places_of([ks for ks, _ in gathered])
     places = places_of(sets)
-    width = 512 if model_width % 1024 == 0 else 128
+    width = 1792 if model_width % 3584 == 0 else 128
     stacked = len(sources) * ROWS // 2
     whole = pl.BlockSpec(memory_space=pltpu.VMEM)
     shapes = [(len(ks), 2 * ROWS, model_width // 2) for ks in sets]
@@ -249,10 +248,9 @@
         out_specs=[whole] * len(sets),
         scratch_shapes=[
             pltpu.VMEM((2 * stacked, model_width), jnp.bfloat16),
-            pltpu.VMEM((model_width, 2 * stacked), jnp.bfloat16),
             pltpu.VMEM(tokens.shape, jnp.bfloat16),
         ],
-        compiler_params=pltpu.CompilerParams(vmem_limit_bytes=12 * 2**20),
+        compiler_params=pltpu.CompilerParams(vmem_limit_bytes=14 * 2**20),
     )(upper, tokens, upstream, squares, *arrays)
 
 

time: 64.5 us -> 54.4 us (0.84)
  waiting for transfers between devices: 29.3 us -> 22.1 us
  Pallas kernels: 12.3 us -> 7.01 us
  starting transfers between devices: 16.1 us -> 19.9 us
  local copies, waits for them, and re-layouts: 1.98 us -> 0.51 us
    ppermute x18, waiting for transfers between devices: 29.3 us -> 22.1 us  [swap(): return lax.ppermute(value, axis, [(i, i ^ mask) for i in range(size)])]
    pallas_call x1, Pallas kernels: 11.8 us -> 6.52 us  [adapter_grads(): pl.pallas_call(functools.partial(adapter_kernel, len(arrays), sources, pl...]
    ppermute x18, starting transfers between devices: 16.1 us -> 19.9 us  [swap(): return lax.ppermute(value, axis, [(i, i ^ mask) for i in range(size)])]
    unnamed x17 -> x16, local copies, waits for them, and re-layouts: 1.55 us -> 0.07 us
  transfers between devices with their start and end apart: 18 -> 18, of which waited for: 13 -> 10; matrix products, arithmetic and copies ran while one was open for 2% -> 2% of each run, Pallas kernels for 1% -> 1%
where the time goes in v4:
time: 54.4 us; the launch traced here: 54.2 us
  waiting for transfers between devices  22.1 us (41%)
  starting transfers between devices  19.9 us (37%)
  Pallas kernels  7.01 us (13%)
  other arithmetic  3.04 us (6%)
  between operations  1.74 us (3%)
    ppermute x18, waiting for transfers between devices, swap(): return lax.ppermute(value, axis, [(i, i ^ mask) for i in range(size)])  22.1 us
    ppermute x18, starting transfers between devices, swap(): return lax.ppermute(value, axis, [(i, i ^ mask) for i in range(size)])  19.9 us
    pallas_call x1, Pallas kernels, adapter_grads(): pl.pallas_call(functools.partial(adapter_kernel, len(arrays), sources, pl...  6.52 us
  transfers between devices with their start and end apart: 18, of which 10 were waited for; matrix products, arithmetic and copies ran while one was open for 2% of the time, Pallas kernels for 1%

profile of v4, /device:TPU:0, one launch (start us, length us, event | category | flops | bytes accessed | tf_op | source)
XLA Modules:
  0.0 54.2 jit_solution(13473429742447777722)
XLA Ops:
  1.5 1.0 %convert_element_type.74 = bf16[1,2,224,128]{3,2,1,0:T(8,128)(2,1)S(1)} convert(f32[1,2,224,128]{3,2,1,0:T(8,128)} %param.10) | non-fusion elementwise | flops 57344 | bytes 344064 | tf_op jit(solution)/shard_map/convert_element_type | solution.py:276
  2.6 4.1 %collective-permute-start = (bf16[1,16,3584]{2,1,0:T(8,128)(2,1)S(1)}, bf16[1,16,3584]{2,1,0:T(8,128)(2,1)S(1)}, u32[]{:S(2)}, u32[]{:S(2)}) collective-permute-start(bf16[1,16,3584]{2,1,0:T(8,128)(2,1)S(1)} %bitcast.80), channel_id=1, source_target_pairs={{0,8},{1,9},{2,10},{3,11},{4,12},{5,13},{6,14},{7,15},{8,0},{9,1},... | collective-permute-start | bytes 344072 | tf_op jit(solution)/shard_map/ppermute | solution.py:25
  6.7 1.6 %collective-permute-start.2 = (bf16[1,16,3584]{2,1,0:T(8,128)(2,1)S(1)}, bf16[1,16,3584]{2,1,0:T(8,128)(2,1)S(1)}, u32[]{:S(2)}, u32[]{:S(2)}) collective-permute-start(bf16[1,16,3584]{2,1,0:T(8,128)(2,1)S(1)} %bitcast.81), channel_id=1, source_target_pairs={{0,4},{1,5},{2,6},{3,7},{4,0},{5,1},{6,2},{7,3},{8,12},{9,13},{10,... | collective-permute-start | bytes 344072 | tf_op jit(solution)/shard_map/ppermute | solution.py:25
  8.2 1.5 %collective-permute-start.1 = (bf16[1,16,3584]{2,1,0:T(8,128)(2,1)S(1)}, bf16[1,16,3584]{2,1,0:T(8,128)(2,1)S(1)}, u32[]{:S(2)}, u32[]{:S(2)}) collective-permute-start(bf16[1,16,3584]{2,1,0:T(8,128)(2,1)S(1)} %bitcast.82), channel_id=1, source_target_pairs={{0,2},{1,3},{2,0},{3,1},{4,6},{5,7},{6,4},{7,5},{8,10},{9,11},{10,... | collective-permute-start | bytes 344072 | tf_op jit(solution)/shard_map/ppermute | solution.py:25
  9.8 1.5 %collective-permute-start.3 = (f32[2,224,128]{2,1,0:T(8,128)}, f32[2,224,128]{2,1,0:T(8,128)S(1)}, u32[]{:S(2)}, u32[]{:S(2)}) collective-permute-start(f32[2,224,128]{2,1,0:T(8,128)} %bitcast.79), channel_id=1, source_target_pairs={{0,16},{16,0},{1,17},{17,1},{2,18},{18,2},{3,19},{19,3},{4,20},{20... | collective-permute-start | bytes 688136 | tf_op jit(solution)/shard_map/ppermute | solution.py:25
  11.2 1.1 %collective-permute-done.refs_0_ = bf16[1,16,3584]{2,1,0:T(8,128)(2,1)S(1)} collective-permute-done((bf16[1,16,3584]{2,1,0:T(8,128)(2,1)S(1)}, bf16[1,16,3584]{2,1,0:T(8,128)(2,1)S(1)}, u32[]{:S(2)}, u32[]{:S(2)}) %collective-permute-start) | collective-permute-done | bytes 114720 | tf_op jit(solution)/shard_map/ppermute | solution.py:25
  12.4 0.2 collective-permute-done.2
  12.6 0.0 copy-start.1
  12.6 1.6 %collective-permute-start.5 = (bf16[2,16,3584]{2,1,0:T(8,128)(2,1)S(1)}, bf16[2,16,3584]{2,1,0:T(8,128)(2,1)S(1)}, u32[]{:S(2)}, u32[]{:S(2)}) collective-permute-start(bf16[2,16,3584]{2,1,0:T(8,128)(2,1)S(1)} %pad_maximum_fusion.1), channel_id=1, source_target_pairs={{0,2},{1,3},{2,0},{3,1},{4,6},{5,7},{6,4},{7,5},{8,10},{9,11},{10,... | collective-permute-start | bytes 688136 | tf_op jit(solution)/shard_map/ppermute | solution.py:25
  14.3 1.4 %collective-permute-start.4 = (bf16[1,16,3584]{2,1,0:T(8,128)(2,1)S(1)}, bf16[1,16,3584]{2,1,0:T(8,128)(2,1)S(1)}, u32[]{:S(2)}, u32[]{:S(2)}) collective-permute-start(bf16[1,16,3584]{2,1,0:T(8,128)(2,1)S(1)} %collective-permute-done.refs_0_), channel_id=1, source_target_pairs={{0,4},{1,5},{2,6},{3,7},{4,0},{5,1},{6,2},{7,3},{8,12},{9,13},{10,... | collective-permute-start | bytes 344072 | tf_op jit(solution)/shard_map/ppermute | solution.py:25
  15.6 0.0 collective-permute-done.1
  15.6 0.1 pad_maximum_fusion.refs_4_
  15.7 0.5 shard_map.103.refs_3_
  16.2 2.9 %collective-permute-done.4 = bf16[1,16,3584]{2,1,0:T(8,128)(2,1)S(1)} collective-permute-done((bf16[1,16,3584]{2,1,0:T(8,128)(2,1)S(1)}, bf16[1,16,3584]{2,1,0:T(8,128)(2,1)S(1)}, u32[]{:S(2)}, u32[]{:S(2)}) %collective-permute-start.4) | collective-permute-done | bytes 114720 | tf_op jit(solution)/shard_map/ppermute | solution.py:25
  19.1 0.5 collective-permute-start.6
  19.5 0.0 collective-permute-done.5
  19.6 4.3 %collective-permute-done.6 = bf16[1,16,3584]{2,1,0:T(8,128)(2,1)S(1)} collective-permute-done((bf16[1,16,3584]{2,1,0:T(8,128)(2,1)S(1)}, bf16[1,16,3584]{2,1,0:T(8,128)(2,1)S(1)}, u32[]{:S(2)}, u32[]{:S(2)}) %collective-permute-start.6) | collective-permute-done | bytes 114720 | tf_op jit(solution)/shard_map/ppermute | solution.py:25
  23.9 0.1 collective-permute-start.8
  23.9 0.0 collective-permute-done.7.refs_6_
  24.0 1.8 %collective-permute-done.8.refs_7_ = bf16[4,16,3584]{2,1,0:T(8,128)(2,1)S(1)} collective-permute-done((bf16[4,16,3584]{2,1,0:T(8,128)(2,1)S(1)}, bf16[4,16,3584]{2,1,0:T(8,128)(2,1)S(1)}, u32[]{:S(2)}, u32[]{:S(2)}) %collective-permute-start.8) | collective-permute-done | bytes 458784 | tf_op jit(solution)/shard_map/ppermute | solution.py:25
  25.8 6.5 %shard_map.104 = (bf16[2,16,3584]{2,1,0:T(8,128)(2,1)S(1)}, bf16[2,16,3584]{2,1,0:T(8,128)(2,1)S(1)}, bf16[4,16,3584]{2,1,0:T(8,128)(2,1)S(1)}, bf16[2,16,3584]{...) custom-call(s32[1]{0:T(128)} %bitcast.2.refs_0_, ...), custom_call_target="tpu_custom_call" | custom-call | tf_op jit(solution)/shard_map/pallas_call | solution.py:244
  32.3 0.2 collective-permute-start.9
  32.5 1.4 %collective-permute-done.9 = bf16[2,16,3584]{2,1,0:T(8,128)(2,1)S(1)} collective-permute-done((bf16[2,16,3584]{2,1,0:T(8,128)(2,1)S(1)}, bf16[2,16,3584]{2,1,0:T(8,128)(2,1)S(1)}, u32[]{:S(2)}, u32[]{:S(2)}) %collective-permute-start.9) | collective-permute-done | bytes 229408 | tf_op jit(solution)/shard_map/ppermute | solution.py:25
  33.8 0.1 add_convert_fusion.1
  33.9 0.2 collective-permute-start.12
  34.1 0.5 collective-permute-start.11
  34.6 0.1 collective-permute-start.10
  34.7 1.6 %collective-permute-start.14 = (bf16[16,3584]{1,0:T(8,128)(2,1)S(1)}, bf16[16,3584]{1,0:T(8,128)(2,1)S(1)}, u32[]{:S(2)}, u32[]{:S(2)}) collective-permute-start(bf16[16,3584]{1,0:T(8,128)(2,1)S(1)} %get-tuple-element.43), channel_id=1, source_target_pairs={{0,2},{1,3},{2,0},{3,1},{4,6},{5,7},{6,4},{7,5},{8,10},{9,11},{10,... | collective-permute-start | bytes 344072 | tf_op jit(solution)/shard_map/ppermute | solution.py:25
  36.3 0.1 add_convert_fusion
  36.4 0.0 copy-start.2
  36.4 0.0 copy-start.5
  36.4 0.0 copy-start.6
  36.4 3.8 %collective-permute-done.11 = bf16[16,3584]{1,0:T(8,128)(2,1)S(1)} collective-permute-done((bf16[16,3584]{1,0:T(8,128)(2,1)S(1)}, bf16[16,3584]{1,0:T(8,128)(2,1)S(1)}, u32[]{:S(2)}, u32[]{:S(2)}) %collective-permute-start.11) | collective-permute-done | bytes 114720 | tf_op jit(solution)/shard_map/ppermute | solution.py:25
  40.2 0.1 convert_add_fusion
  40.3 0.0 copy-start.3
  40.3 0.0 copy-start.4
  40.3 1.4 %collective-permute-start.13 = (bf16[16,3584]{1,0:T(8,128)(2,1)S(1)}, bf16[16,3584]{1,0:T(8,128)(2,1)S(1)}, u32[]{:S(2)}, u32[]{:S(2)}) collective-permute-start(bf16[16,3584]{1,0:T(8,128)(2,1)S(1)} %fusion.15), channel_id=1, source_target_pairs={{0,4},{1,5},{2,6},{3,7},{4,0},{5,1},{6,2},{7,3},{8,12},{9,13},{10,... | collective-permute-start | bytes 344072 | tf_op jit(solution)/shard_map/ppermute | solution.py:25
  41.7 0.5 collective-permute-start.16
  42.3 2.9 %collective-permute-done.13 = bf16[16,3584]{1,0:T(8,128)(2,1)S(1)} collective-permute-done((bf16[16,3584]{1,0:T(8,128)(2,1)S(1)}, bf16[16,3584]{1,0:T(8,128)(2,1)S(1)}, u32[]{:S(2)}, u32[]{:S(2)}) %collective-permute-start.13) | collective-permute-done | bytes 114720 | tf_op jit(solution)/shard_map/ppermute | solution.py:25
  45.2 2.0 %collective-permute-start.15 = (bf16[16,3584]{1,0:T(8,128)(2,1)S(1)}, bf16[16,3584]{1,0:T(8,128)(2,1)S(1)}, u32[]{:S(2)}, u32[]{:S(2)}) collective-permute-start(bf16[16,3584]{1,0:T(8,128)(2,1)S(1)} %fusion.13), channel_id=1, source_target_pairs={{0,8},{1,9},{2,10},{3,11},{4,12},{5,13},{6,14},{7,15},{8,0},{9,1},... | collective-permute-start | bytes 344072 | tf_op jit(solution)/shard_map/ppermute | solution.py:25
  47.2 0.7 %collective-permute-done.16 = bf16[2,16,3584]{2,1,0:T(8,128)(2,1)S(1)} collective-permute-done((bf16[2,16,3584]{2,1,0:T(8,128)(2,1)S(1)}, bf16[2,16,3584]{2,1,0:T(8,128)(2,1)S(1)}, u32[]{:S(2)}, u32[]{:S(2)}) %collective-permute-start.16) | collective-permute-done | bytes 229408 | tf_op jit(solution)/shard_map/ppermute | solution.py:25
  48.0 1.1 %collective-permute-start.17 = (bf16[16,3584]{1,0:T(8,128)(2,1)S(1)}, bf16[16,3584]{1,0:T(8,128)(2,1)S(1)}, u32[]{:S(2)}, u32[]{:S(2)}) collective-permute-start(bf16[16,3584]{1,0:T(8,128)(2,1)S(1)} %fusion.16), channel_id=1, source_target_pairs={{0,4},{1,5},{2,6},{3,7},{4,0},{5,1},{6,2},{7,3},{8,12},{9,13},{10,... | collective-permute-start | bytes 344072 | tf_op jit(solution)/shard_map/ppermute | solution.py:25
  49.1 0.7 %broadcast_multiply_fusion = (f32[224,128]{1,0:T(8,128)S(1)}, f32[224,128]{1,0:T(8,128)}, f32[224,128]{1,0:T(8,128)}) fusion(f32[224,128]{1,0:T(8,128)S(1)} %copy-done.5, f32[2,224,128]{2,1,0:T(8,128)S(1)} %collective-permute-done.3, s32[]{:T(128)S(6)} %select_n.23, f32[1,2,224,128]{3,2,1,0:T(8,128)S(1)} %copy-done.2, f32[224,128]{1,0:T(8,128)S(1)} %copy-done.6), kind=kLoop, calls=%fused_computation.37 | loop fusion | flops 315392 | bytes 802820 | tf_op jit(solution)/shard_map/mul | solution.py:327
  49.8 3.0 %collective-permute-done.17 = bf16[16,3584]{1,0:T(8,128)(2,1)S(1)} collective-permute-done((bf16[16,3584]{1,0:T(8,128)(2,1)S(1)}, bf16[16,3584]{1,0:T(8,128)(2,1)S(1)}, u32[]{:S(2)}, u32[]{:S(2)}) %collective-permute-start.17) | collective-permute-done | bytes 114720 | tf_op jit(solution)/shard_map/ppermute | solution.py:25
  52.9 0.1 fusion.9
  52.9 0.2 copy.12
  53.1 0.2 mul.115
  53.3 0.9 %add_select_fusion = f32[1,2,224,128]{3,2,1,0:T(8,128)} fusion(f32[1,2,224,128]{3,2,1,0:T(8,128)S(1)} %copy-done.2, f32[1,2,224,128]{3,2,1,0:T(8,128)S(1)} %mul.115, f32[1,2,224,128]{3,2,1,0:T(8,128)S(1)} %copy-done.3, f32[1,2,224,128]{3,2,1,0:T(8,128)S(1)} %copy-done.4, f32[224,128]{1,0:T(8,128)S(1)} %get-tuple-element.39, f32[]{:T(128)S(6)} %sub.20, ...), kind=kLoop, calls=%fused_computation.26 | loop fusion | flops 1032192 | bytes 1261578 | tf_op jit(solution)/shard_map/jit(_where)/select_n | solution.py:327
  (25 shorter events, 0.3 us)
Async XLA Ops:
  0.6 15.1 %copy-start = (bf16[1,128,7168]{2,1,0:T(8,128)(2,1)S(1)}, bf16[1,128,7168]{2,1,0:T(8,128)(2,1)}, u32[]{:S(2)}) copy-start(bf16[1,128,7168]{2,1,0:T(8,128)(2,1)} %param.8) | copy-start | bytes 5505028
  2.6 9.8 %collective-permute-start = (bf16[1,16,3584]{2,1,0:T(8,128)(2,1)S(1)}, bf16[1,16,3584]{2,1,0:T(8,128)(2,1)S(1)}, u32[]{:S(2)}, u32[]{:S(2)}) collective-permute-start(bf16[1,16,3584]{2,1,0:T(8,128)(2,1)S(1)} %bitcast.80), channel_id=1, source_target_pairs={{0,8},{1,9},{2,10},{3,11},{4,12},{5,13},{6,14},{7,15},{8,0},{9,1},... | collective-permute-start | bytes 344072 | tf_op jit(solution)/shard_map/ppermute | solution.py:25
  6.7 5.9 %collective-permute-start.2 = (bf16[1,16,3584]{2,1,0:T(8,128)(2,1)S(1)}, bf16[1,16,3584]{2,1,0:T(8,128)(2,1)S(1)}, u32[]{:S(2)}, u32[]{:S(2)}) collective-permute-start(bf16[1,16,3584]{2,1,0:T(8,128)(2,1)S(1)} %bitcast.81), channel_id=1, source_target_pairs={{0,4},{1,5},{2,6},{3,7},{4,0},{5,1},{6,2},{7,3},{8,12},{9,13},{10,... | collective-permute-start | bytes 344072 | tf_op jit(solution)/shard_map/ppermute | solution.py:25
  8.2 7.4 %collective-permute-start.1 = (bf16[1,16,3584]{2,1,0:T(8,128)(2,1)S(1)}, bf16[1,16,3584]{2,1,0:T(8,128)(2,1)S(1)}, u32[]{:S(2)}, u32[]{:S(2)}) collective-permute-start(bf16[1,16,3584]{2,1,0:T(8,128)(2,1)S(1)} %bitcast.82), channel_id=1, source_target_pairs={{0,2},{1,3},{2,0},{3,1},{4,6},{5,7},{6,4},{7,5},{8,10},{9,11},{10,... | collective-permute-start | bytes 344072 | tf_op jit(solution)/shard_map/ppermute | solution.py:25
  9.8 9.8 %collective-permute-start.3 = (f32[2,224,128]{2,1,0:T(8,128)}, f32[2,224,128]{2,1,0:T(8,128)S(1)}, u32[]{:S(2)}, u32[]{:S(2)}) collective-permute-start(f32[2,224,128]{2,1,0:T(8,128)} %bitcast.79), channel_id=1, source_target_pairs={{0,16},{16,0},{1,17},{17,1},{2,18},{18,2},{3,19},{19,3},{4,20},{20... | collective-permute-start | bytes 688136 | tf_op jit(solution)/shard_map/ppermute | solution.py:25
  12.6 13.1 %copy-start.1 = (bf16[1,128,7168]{2,1,0:T(8,128)(2,1)S(1)}, bf16[1,128,7168]{2,1,0:T(8,128)(2,1)}, u32[]{:S(2)}) copy-start(bf16[1,128,7168]{2,1,0:T(8,128)(2,1)} %param.9) | copy-start | bytes 5505028
  12.6 6.9 %collective-permute-start.5 = (bf16[2,16,3584]{2,1,0:T(8,128)(2,1)S(1)}, bf16[2,16,3584]{2,1,0:T(8,128)(2,1)S(1)}, u32[]{:S(2)}, u32[]{:S(2)}) collective-permute-start(bf16[2,16,3584]{2,1,0:T(8,128)(2,1)S(1)} %pad_maximum_fusion.1), channel_id=1, source_target_pairs={{0,2},{1,3},{2,0},{3,1},{4,6},{5,7},{6,4},{7,5},{8,10},{9,11},{10,... | collective-permute-start | bytes 688136 | tf_op jit(solution)/shard_map/ppermute | solution.py:25
  14.3 4.8 %collective-permute-start.4 = (bf16[1,16,3584]{2,1,0:T(8,128)(2,1)S(1)}, bf16[1,16,3584]{2,1,0:T(8,128)(2,1)S(1)}, u32[]{:S(2)}, u32[]{:S(2)}) collective-permute-start(bf16[1,16,3584]{2,1,0:T(8,128)(2,1)S(1)} %collective-permute-done.refs_0_), channel_id=1, source_target_pairs={{0,4},{1,5},{2,6},{3,7},{4,0},{5,1},{6,2},{7,3},{8,12},{9,13},{10,... | collective-permute-start | bytes 344072 | tf_op jit(solution)/shard_map/ppermute | solution.py:25
  19.1 4.8 %collective-permute-start.6 = (bf16[1,16,3584]{2,1,0:T(8,128)(2,1)S(1)}, bf16[1,16,3584]{2,1,0:T(8,128)(2,1)S(1)}, u32[]{:S(2)}, u32[]{:S(2)}) collective-permute-start(bf16[1,16,3584]{2,1,0:T(8,128)(2,1)S(1)} %collective-permute-done.4), channel_id=1, source_target_pairs={{0,2},{1,3},{2,0},{3,1},{4,6},{5,7},{6,4},{7,5},{8,10},{9,11},{10,... | collective-permute-start | bytes 344072 | tf_op jit(solution)/shard_map/ppermute | solution.py:25
  19.5 4.4 %collective-permute-start.7 = (bf16[4,16,3584]{2,1,0:T(8,128)(2,1)S(1)}, bf16[4,16,3584]{2,1,0:T(8,128)(2,1)S(1)}, u32[]{:S(2)}, u32[]{:S(2)}) collective-permute-start(bf16[4,16,3584]{2,1,0:T(8,128)(2,1)S(1)} %pad_maximum_fusion.refs_4_), channel_id=1, source_target_pairs={{0,1},{1,0},{2,3},{3,2},{4,5},{5,4},{6,7},{7,6},{8,9},{9,8},{10,11... | collective-permute-start | bytes 1376264 | tf_op jit(solution)/shard_map/ppermute | solution.py:25
  23.9 1.9 %collective-permute-start.8 = (bf16[4,16,3584]{2,1,0:T(8,128)(2,1)S(1)}, bf16[4,16,3584]{2,1,0:T(8,128)(2,1)S(1)}, u32[]{:S(2)}, u32[]{:S(2)}) collective-permute-start(bf16[4,16,3584]{2,1,0:T(8,128)(2,1)S(1)} %constant_dynamic-update-slice_fusion.refs_5_), channel_id=1, source_target_pairs={{0,1},{1,0},{2,3},{3,2},{4,5},{5,4},{6,7},{7,6},{8,9},{9,8},{10,11... | collective-permute-start | bytes 1376264 | tf_op jit(solution)/shard_map/ppermute | solution.py:25
  32.3 1.6 %collective-permute-start.9 = (bf16[2,16,3584]{2,1,0:T(8,128)(2,1)S(1)}, bf16[2,16,3584]{2,1,0:T(8,128)(2,1)S(1)}, u32[]{:S(2)}, u32[]{:S(2)}) collective-permute-start(bf16[2,16,3584]{2,1,0:T(8,128)(2,1)S(1)} %get-tuple-element.30), channel_id=1, source_target_pairs={{0,1},{1,0},{2,3},{3,2},{4,5},{5,4},{6,7},{7,6},{8,9},{9,8},{10,11... | collective-permute-start | bytes 688136 | tf_op jit(solution)/shard_map/ppermute | solution.py:25
  33.9 2.4 %collective-permute-start.12 = (bf16[2,16,3584]{2,1,0:T(8,128)(2,1)S(1)}, bf16[2,16,3584]{2,1,0:T(8,128)(2,1)S(1)}, u32[]{:S(2)}, u32[]{:S(2)}) collective-permute-start(bf16[2,16,3584]{2,1,0:T(8,128)(2,1)S(1)} %get-tuple-element.33), channel_id=1, source_target_pairs={{0,1},{1,0},{2,3},{3,2},{4,5},{5,4},{6,7},{7,6},{8,9},{9,8},{10,11... | collective-permute-start | bytes 688136 | tf_op jit(solution)/shard_map/ppermute | solution.py:25
  34.1 6.0 %collective-permute-start.11 = (bf16[16,3584]{1,0:T(8,128)(2,1)S(1)}, bf16[16,3584]{1,0:T(8,128)(2,1)S(1)}, u32[]{:S(2)}, u32[]{:S(2)}) collective-permute-start(bf16[16,3584]{1,0:T(8,128)(2,1)S(1)} %get-tuple-element.42), channel_id=1, source_target_pairs={{0,2},{1,3},{2,0},{3,1},{4,6},{5,7},{6,4},{7,5},{8,10},{9,11},{10,... | collective-permute-start | bytes 344072 | tf_op jit(solution)/shard_map/ppermute | solution.py:25
  34.6 5.5 %collective-permute-start.10 = (bf16[4,16,3584]{2,1,0:T(8,128)(2,1)S(1)}, bf16[4,16,3584]{2,1,0:T(8,128)(2,1)S(1)}, u32[]{:S(2)}, u32[]{:S(2)}) collective-permute-start(bf16[4,16,3584]{2,1,0:T(8,128)(2,1)S(1)} %get-tuple-element.31), channel_id=1, source_target_pairs={{0,1},{1,0},{2,3},{3,2},{4,5},{5,4},{6,7},{7,6},{8,9},{9,8},{10,11... | collective-permute-start | bytes 1376264 | tf_op jit(solution)/shard_map/ppermute | solution.py:25
  34.7 7.5 %collective-permute-start.14 = (bf16[16,3584]{1,0:T(8,128)(2,1)S(1)}, bf16[16,3584]{1,0:T(8,128)(2,1)S(1)}, u32[]{:S(2)}, u32[]{:S(2)}) collective-permute-start(bf16[16,3584]{1,0:T(8,128)(2,1)S(1)} %get-tuple-element.43), channel_id=1, source_target_pairs={{0,2},{1,3},{2,0},{3,1},{4,6},{5,7},{6,4},{7,5},{8,10},{9,11},{10,... | collective-permute-start | bytes 344072 | tf_op jit(solution)/shard_map/ppermute | solution.py:25
  36.4 12.7 %copy-start.2 = (f32[1,2,224,128]{3,2,1,0:T(8,128)S(1)}, f32[1,2,224,128]{3,2,1,0:T(8,128)}, u32[]{:S(2)}) copy-start(f32[1,2,224,128]{3,2,1,0:T(8,128)} %param.10) | copy-start | bytes 688132
  36.4 12.7 %copy-start.5 = (f32[224,128]{1,0:T(8,128)S(1)}, f32[224,128]{1,0:T(8,128)}, u32[]{:S(2)}) copy-start(f32[224,128]{1,0:T(8,128)} %param.13) | copy-start | bytes 344068
  36.4 12.7 %copy-start.6 = (f32[224,128]{1,0:T(8,128)S(1)}, f32[224,128]{1,0:T(8,128)}, u32[]{:S(2)}) copy-start(f32[224,128]{1,0:T(8,128)} %param.14) | copy-start | bytes 344068
  40.3 13.0 %copy-start.3 = (f32[1,2,224,128]{3,2,1,0:T(8,128)S(1)}, f32[1,2,224,128]{3,2,1,0:T(8,128)}, u32[]{:S(2)}) copy-start(f32[1,2,224,128]{3,2,1,0:T(8,128)} %param.12) | copy-start | bytes 688132
  40.3 13.0 %copy-start.4 = (f32[1,2,224,128]{3,2,1,0:T(8,128)S(1)}, f32[1,2,224,128]{3,2,1,0:T(8,128)}, u32[]{:S(2)}) copy-start(f32[1,2,224,128]{3,2,1,0:T(8,128)} %param.11) | copy-start | bytes 688132
  40.3 4.9 %collective-permute-start.13 = (bf16[16,3584]{1,0:T(8,128)(2,1)S(1)}, bf16[16,3584]{1,0:T(8,128)(2,1)S(1)}, u32[]{:S(2)}, u32[]{:S(2)}) collective-permute-start(bf16[16,3584]{1,0:T(8,128)(2,1)S(1)} %fusion.15), channel_id=1, source_target_pairs={{0,4},{1,5},{2,6},{3,7},{4,0},{5,1},{6,2},{7,3},{8,12},{9,13},{10,... | collective-permute-start | bytes 344072 | tf_op jit(solution)/shard_map/ppermute | solution.py:25
  41.7 6.2 %collective-permute-start.16 = (bf16[2,16,3584]{2,1,0:T(8,128)(2,1)S(1)}, bf16[2,16,3584]{2,1,0:T(8,128)(2,1)S(1)}, u32[]{:S(2)}, u32[]{:S(2)}) collective-permute-start(bf16[2,16,3584]{2,1,0:T(8,128)(2,1)S(1)} %add_convert_fusion), channel_id=1, source_target_pairs={{0,2},{1,3},{2,0},{3,1},{4,6},{5,7},{6,4},{7,5},{8,10},{9,11},{10,... | collective-permute-start | bytes 688136 | tf_op jit(solution)/shard_map/ppermute | solution.py:25
  45.2 7.7 %collective-permute-start.15 = (bf16[16,3584]{1,0:T(8,128)(2,1)S(1)}, bf16[16,3584]{1,0:T(8,128)(2,1)S(1)}, u32[]{:S(2)}, u32[]{:S(2)}) collective-permute-start(bf16[16,3584]{1,0:T(8,128)(2,1)S(1)} %fusion.13), channel_id=1, source_target_pairs={{0,8},{1,9},{2,10},{3,11},{4,12},{5,13},{6,14},{7,15},{8,0},{9,1},... | collective-permute-start | bytes 344072 | tf_op jit(solution)/shard_map/ppermute | solution.py:25
  48.0 4.9 %collective-permute-start.17 = (bf16[16,3584]{1,0:T(8,128)(2,1)S(1)}, bf16[16,3584]{1,0:T(8,128)(2,1)S(1)}, u32[]{:S(2)}, u32[]{:S(2)}) collective-permute-start(bf16[16,3584]{1,0:T(8,128)(2,1)S(1)} %fusion.16), channel_id=1, source_target_pairs={{0,4},{1,5},{2,6},{3,7},{4,0},{5,1},{6,2},{7,3},{8,12},{9,13},{10,... | collective-permute-start | bytes 344072 | tf_op jit(solution)/shard_map/ppermute | solution.py:25

commit v5 on v4

--- a/solution.py
+++ b/solution.py
@@ -59,35 +59,35 @@
 
 def output_sets(size):
     tops = list(range(size - 4, -1, -4))
-    half = len(tops) // 2
-    parts = [[k + 2 for k in tops[:half]], [k + 2 for k in tops[half:]], tops]
-    return [[k + 1 for k in ks] for ks in parts] + parts
-
-
-def reduce_blocks(outs, axis):
+    even = [k + 2 for k in tops] + tops
+    return [[k + 1 for k in even], even]
+
+
+def reduce_blocks(odd, even, axis):
     size = lax.axis_size(axis)
     tops = list(range(size - 4, -1, -4))
     half = len(tops) // 2
-    came = swap(outs[0], axis, 1)
-    sums = add_f32(outs[3], came).astype(jnp.bfloat16)
+    came = swap(odd, axis, 1)
+    sums = add_f32(even[: len(tops)], came[: len(tops)]).astype(jnp.bfloat16)
     near = [swap(sums[at], axis, 2) for at in range(half)]
-    odd, last_odd, sums = lax.optimization_barrier((outs[1], outs[2], sums))
-    came = swap(odd, axis, 1)
-    sums = add_f32(outs[4], came).astype(jnp.bfloat16)
-    rest = swap(sums, axis, 2)
-    near[0] = after(near[0], sums)
-    kept = add_f32(outs[5], swap(last_odd, axis, 1))
+    rest = swap(sums[half:], axis, 2)
+    came = after(came, sums)
+    kept = add_f32(even[len(tops) :], came[len(tops) :])
+    parts = []
     left = {}
     for at, k in enumerate(tops):
         if at == half:
             rest = after(rest, part)
         arrived = near[at] if at < half else rest[at - half]
-        left[k] = left.get(k, 0.0) + kept[at] + arrived.astype(jnp.float32)
         if k:
+            left[k] = left.get(k, 0.0) + kept[at] + arrived.astype(jnp.float32)
             part = left[k].astype(jnp.bfloat16)
-            moved = swap(part, axis, k & -k).astype(jnp.float32)
-            left[k & (k - 1)] = left.get(k & (k - 1), 0.0) + moved
-    return left[0]
+            moved = swap(part, axis, k & -k)
+            if k & (k - 1):
+                left[k & (k - 1)] = left.get(k & (k - 1), 0.0) + moved.astype(jnp.float32)
+            else:
+                parts.append(moved)
+    return [kept[-1], rest[-1]] + parts
 
 
 def dot_nt(left, right):
@@ -126,10 +126,14 @@
     )(tokens, *early)
 
 
+def in_upper_half():
+    return (lax.axis_index("fsdp") >= lax.axis_size("fsdp") // 2).astype(jnp.int32)
+
+
 def adapter_kernel(n_arrays, sources, places, units, width, *refs):
-    upper_ref, h0, g2, squares0 = refs[:4]
-    arrays = refs[4 : 4 + n_arrays]
-    outs = refs[4 + n_arrays : -2]
+    h0, g2, squares0 = refs[:3]
+    arrays = refs[3 : 3 + n_arrays]
+    outs = refs[3 + n_arrays : -2]
     w_ref, h1 = refs[-2:]
     n_pieces = len(sources)
     tokens, model_width = h0.shape
@@ -138,7 +142,7 @@
     in_scale = model_width ** (-0.5)
     out_scale = hidden ** (-0.5)
     steps = model_width // 2 // width
-    upper = upper_ref[0]
+    upper = in_upper_half()
     half = n_pieces // 2
     w_in, w_out = pl.ds(0, stacked), pl.ds(stacked, stacked)
     layer_of = (lax.broadcasted_iota(jnp.int32, (tokens, stacked), 1) % (2 * units)) // units
@@ -232,7 +236,7 @@
     return {k: (at, place) for at, ks in enumerate(sets) for place, k in enumerate(ks)}
 
 
-def adapter_grads(upper, tokens, upstream, squares, gathered, units, sets):
+def adapter_grads(tokens, upstream, squares, gathered, units, sets):
     model_width = tokens.shape[1]
     arrays = [array for _, array in gathered]
     sources = places_of([ks for ks, _ in gathered])
@@ -244,14 +248,84 @@
     return pl.pallas_call(
         functools.partial(adapter_kernel, len(arrays), sources, places, units, width),
         out_shape=[jax.ShapeDtypeStruct(shape, jnp.bfloat16) for shape in shapes],
-        in_specs=[pl.BlockSpec(memory_space=pltpu.SMEM)] + [whole] * (3 + len(arrays)),
+        in_specs=[whole] * (3 + len(arrays)),
         out_specs=[whole] * len(sets),
         scratch_shapes=[
             pltpu.VMEM((2 * stacked, model_width), jnp.bfloat16),
             pltpu.VMEM(tokens.shape, jnp.bfloat16),
         ],
         compiler_params=pltpu.CompilerParams(vmem_limit_bytes=14 * 2**20),
-    )(upper, tokens, upstream, squares, *arrays)
+    )(tokens, upstream, squares, *arrays)
+
+
+def delta_kernel(fragment, params, other, anchor, total):
+    chosen = lax.rem(fragment[0], params.shape[0])
+    total[...] = (anchor[...] - params[chosen]) + (anchor[...] - other[chosen])
+
+
+def fragment_delta(fragment, params, other, anchor):
+    whole = pl.BlockSpec(memory_space=pltpu.VMEM)
+    return pl.pallas_call(
+        delta_kernel,
+        out_shape=jax.ShapeDtypeStruct(anchor.shape, jnp.float32),
+        in_specs=[pl.BlockSpec(memory_space=pltpu.SMEM)] + [whole] * 3,
+        out_specs=whole,
+        compiler_params=pltpu.CompilerParams(vmem_limit_bytes=2 * 2**20),
+    )(fragment, params, other, anchor)
+
+
+def adam_kernel(n_parts, tokens, scales, *refs):
+    fragment, params, first_moment, second_moment, new_global = refs[:5]
+    parts = refs[5 : 5 + n_parts]
+    out, flat, merged, sem = refs[5 + n_parts :]
+    layers, rows, _ = params.shape
+    piece = parts[0].shape[0] // 2
+    tiles = parts[0].shape[1] // 128
+    scale = jnp.where(in_upper_half() == 1, scales[1] / tokens, scales[0] / tokens)
+    for tile in range(tiles):
+        at = pl.ds(tile * 128, 128)
+        total = parts[0][:, at].astype(jnp.float32)
+        for part in parts[1:]:
+            total = total + part[:, at].astype(jnp.float32)
+        total = total * scale
+        flat[pl.ds(tile, piece, stride=2 * tiles), :] = total[:piece]
+        flat[pl.ds(tiles + tile, piece, stride=2 * tiles), :] = total[piece:]
+    count = jnp.full((8, 128), fragment[0], jnp.int32).astype(jnp.float32)
+    correct_one = (1.0 - jnp.exp(count * math.log(beta_one)))[:1]
+    correct_two = (1.0 - jnp.exp(count * math.log(beta_two)))[:1]
+    chosen = lax.rem(fragment[0], layers)
+    copies = []
+    for layer in range(layers):
+        gradient = flat[pl.ds(layer * rows, rows), :]
+        moment_one = beta_one * first_moment[layer] + (1.0 - beta_one) * gradient
+        moment_two = beta_two * second_moment[layer] + (1.0 - beta_two) * gradient * gradient
+        updated = params[layer] - inner_rate * (
+            moment_one / correct_one / (jnp.sqrt(moment_two / correct_two) + adam_eps)
+            + decay_rate * params[layer]
+        )
+        mixed = mixing * updated + (1.0 - mixing) * new_global[...]
+        merged[layer] = jnp.where(chosen == layer, mixed, updated)
+        copies.append(pltpu.make_async_copy(merged.at[layer], out.at[layer], sem.at[layer]))
+        copies[-1].start()
+    for copy in copies:
+        copy.wait()
+
+
+def adam_step(fragment, params, first_moment, second_moment, new_global, parts, tokens, scales):
+    whole = pl.BlockSpec(memory_space=pltpu.VMEM)
+    layers, rows, lanes = params.shape
+    return pl.pallas_call(
+        functools.partial(adam_kernel, len(parts), tokens, scales),
+        out_shape=jax.ShapeDtypeStruct(params.shape, jnp.float32),
+        in_specs=[pl.BlockSpec(memory_space=pltpu.SMEM)] + [whole] * (4 + len(parts)),
+        out_specs=pl.BlockSpec(memory_space=pltpu.HBM),
+        scratch_shapes=[
+            pltpu.VMEM((layers * rows, lanes), jnp.float32),
+            pltpu.VMEM(params.shape, jnp.float32),
+            pltpu.SemaphoreType.DMA((layers,)),
+        ],
+        compiler_params=pltpu.CompilerParams(vmem_limit_bytes=4 * 2**20),
+    )(fragment, params, first_moment, second_moment, new_global, *parts)
 
 
 def shards(inputs, cotangent, weights, first_moment, second_moment, anchor, momentum, fragment):
@@ -265,19 +339,8 @@
     units = rows * 128 // model_width
     hidden = units * groups // 2
     piece = layers * units
-    upper = (lax.axis_index("fsdp") >= groups // 2).astype(jnp.int32).reshape(1)
-    count = fragment[0]
-    chosen = jnp.remainder(count, layers)
-    count_real = count.astype(jnp.float32)
-    correct_one = 1.0 - jnp.exp(count_real * math.log(beta_one))
-    correct_two = 1.0 - jnp.exp(count_real * math.log(beta_two))
-    scale = jnp.where(upper[0] == 1, hidden ** (-0.5), model_width ** (-0.5))
-    scale = scale / (tokens.shape[0] * groups)
     compact = params.astype(jnp.bfloat16).reshape(piece, 2, model_width // 2)
     compact = compact.transpose(1, 0, 2).reshape(2 * piece, model_width // 2)
-    compact, upper, chosen, correct_one, correct_two, scale = lax.optimization_barrier(
-        (compact, upper, chosen, correct_one, correct_two, scale)
-    )
     other = swap(params, "rep", 1)
     kept = []
 
@@ -290,7 +353,7 @@
 
     sets = output_sets(groups)
     if piece == ROWS:
-        outs = adapter_grads(upper, tokens, upstream, squares, gathered, units, sets)
+        odd, even = adapter_grads(tokens, upstream, squares, gathered, units, sets)
     else:
         merged = ROWS // piece
         blocks = {k: array[place] for ks, array in gathered for place, k in enumerate(ks)}
@@ -298,33 +361,24 @@
         blocks = blocks.reshape(groups // merged, merged, 2, piece, model_width // 2)
         blocks = blocks.transpose(0, 2, 1, 3, 4).reshape(groups // merged, 2 * ROWS, model_width // 2)
         every = list(range(groups // merged))
-        (both,) = adapter_grads(upper, tokens, upstream, squares, [(every, blocks)], units, [every])
+        (both,) = adapter_grads(tokens, upstream, squares, [(every, blocks)], units, [every])
         both = both.reshape(groups // merged, 2, merged, piece, model_width // 2)
         both = both.transpose(0, 2, 1, 3, 4).reshape(groups, 2 * piece, model_width // 2)
-        outs = [jnp.stack([both[k] for k in ks]) for ks in sets]
-    summed = reduce_blocks(outs, "fsdp").reshape(2, piece, model_width // 2)
-    summed = summed.transpose(1, 0, 2).reshape(layers, rows, 128)
-    gradient = summed * scale
-
-    def delta(values):
-        return anchor - lax.dynamic_index_in_dim(values, chosen, 0, keepdims=False)
-
-    total = delta(params) + delta(other)
+        odd, even = [jnp.stack([both[k] for k in ks]) for ks in sets]
+    parts = reduce_blocks(odd, even, "fsdp")
+
+    total = fragment_delta(fragment, params, other, anchor)
     step = 2
     while step < replicas:
         total = total + swap(total, "rep", step)
         step *= 2
-    moment_one = beta_one * first_moment[0] + (1.0 - beta_one) * gradient
-    moment_two = beta_two * second_moment[0] + (1.0 - beta_two) * gradient * gradient
-    updated = params - inner_rate * (
-        moment_one / correct_one / (jnp.sqrt(moment_two / correct_two) + adam_eps)
-        + decay_rate * params
-    )
-    mean_delta = total / replicas
+    mean_delta = after(total, parts[1]) / replicas
     new_velocity = outer_beta * momentum + mean_delta
     new_global = anchor - outer_rate * (mean_delta + outer_beta * new_velocity)
-    selector = (jnp.arange(layers, dtype=jnp.int32) == chosen)[:, None, None]
-    merged = jnp.where(selector, mixing * updated + (1.0 - mixing) * new_global[None], updated)
+    scales = (model_width ** (-0.5), hidden ** (-0.5))
+    merged = adam_step(
+        fragment, params, first_moment[0], second_moment[0], new_global, parts, tokens.shape[0] * groups, scales
+    )
     return (merged[None], new_global, new_velocity)
 
 

time: 54.4 us -> 55.1 us (1.013)
  waiting for transfers between devices: 22.1 us -> 25.7 us
  starting transfers between devices: 19.9 us -> 17.5 us
  Pallas kernels: 7.01 us -> 7.94 us
  other arithmetic: 3.04 us -> 2.15 us
    ppermute x18 -> x16, waiting for transfers between devices: 22.1 us -> 25.7 us  [swap(): return lax.ppermute(value, axis, [(i, i ^ mask) for i in range(size)])]
    ppermute x18 -> x16, starting transfers between devices: 19.9 us -> 17.5 us  [swap(): return lax.ppermute(value, axis, [(i, i ^ mask) for i in range(size)])]
    pallas_call x0 -> x2, Pallas kernels: none -> 0.99 us  [the longest x1 0.97 us: adam_step(): pl.pallas_call(functools.partial(adam_kernel, len(parts), tokens, scales)...]
    select_n x1 -> x0, other arithmetic: 0.9 us -> none  [shards(): jnp.where(selector, mixing * updated + (1.0 - mixing) * new_global[None],...]
    mul x2 -> x0, other arithmetic: 0.79 us -> none  [the longest x1 0.73 us: shards(): (1.0 - mixing) * new_global[None]]
    sub x0 -> x1, other arithmetic: none -> 0.68 us  [shards(): new_global = anchor - outer_rate * (mean_delta + outer_beta * new_velocity)]
  transfers between devices with their start and end apart: 18 -> 16, of which waited for: 10 -> 10; matrix products, arithmetic and copies ran while one was open for 2% -> 2% of each run, Pallas kernels for 1% -> 1%
where the time goes in v5:
time: 55.1 us; the launch traced here: 54.9 us
  waiting for transfers between devices  25.7 us (47%)
  starting transfers between devices  17.5 us (32%)
  Pallas kernels  7.94 us (14%)
  other arithmetic  2.15 us (4%)
  between operations  1.49 us (3%)
    ppermute x16, waiting for transfers between devices, swap(): return lax.ppermute(value, axis, [(i, i ^ mask) for i in range(size)])  25.7 us
    ppermute x16, starting transfers between devices, swap(): return lax.ppermute(value, axis, [(i, i ^ mask) for i in range(size)])  17.5 us
    pallas_call x1, Pallas kernels, adapter_grads(): pl.pallas_call(functools.partial(adapter_kernel, len(arrays), sources, pl...  6.47 us
  transfers between devices with their start and end apart: 16, of which 10 were waited for; matrix products, arithmetic and copies ran while one was open for 2% of the time, Pallas kernels for 1%

profile of v5, /device:TPU:0, one launch (start us, length us, event | category | flops | bytes accessed | tf_op | source)
XLA Modules:
  0.0 54.9 jit_solution(7637535607385135667)
XLA Ops:
  0.6 0.0 copy-start
  0.6 1.1 %convert_element_type.47 = bf16[1,2,224,128]{3,2,1,0:T(8,128)(2,1)S(1)} convert(f32[1,2,224,128]{3,2,1,0:T(8,128)} %param.10) | non-fusion elementwise | flops 57344 | bytes 344064 | tf_op jit(solution)/shard_map/convert_element_type | solution.py:342
  1.8 3.1 %collective-permute-start.3 = (bf16[1,16,3584]{2,1,0:T(8,128)(2,1)S(1)}, bf16[1,16,3584]{2,1,0:T(8,128)(2,1)S(1)}, u32[]{:S(2)}, u32[]{:S(2)}) collective-permute-start(bf16[1,16,3584]{2,1,0:T(8,128)(2,1)S(1)} %bitcast.45), channel_id=1, source_target_pairs={{0,4},{1,5},{2,6},{3,7},{4,0},{5,1},{6,2},{7,3},{8,12},{9,13},{10,... | collective-permute-start | bytes 344072 | tf_op jit(solution)/shard_map/ppermute | solution.py:25
  4.9 2.6 %collective-permute-start.1 = (bf16[1,16,3584]{2,1,0:T(8,128)(2,1)S(1)}, bf16[1,16,3584]{2,1,0:T(8,128)(2,1)S(1)}, u32[]{:S(2)}, u32[]{:S(2)}) collective-permute-start(bf16[1,16,3584]{2,1,0:T(8,128)(2,1)S(1)} %bitcast.46), channel_id=1, source_target_pairs={{0,8},{1,9},{2,10},{3,11},{4,12},{5,13},{6,14},{7,15},{8,0},{9,1},... | collective-permute-start | bytes 344072 | tf_op jit(solution)/shard_map/ppermute | solution.py:25
  7.5 1.5 %collective-permute-start.2 = (bf16[1,16,3584]{2,1,0:T(8,128)(2,1)S(1)}, bf16[1,16,3584]{2,1,0:T(8,128)(2,1)S(1)}, u32[]{:S(2)}, u32[]{:S(2)}) collective-permute-start(bf16[1,16,3584]{2,1,0:T(8,128)(2,1)S(1)} %bitcast.47), channel_id=1, source_target_pairs={{0,2},{1,3},{2,0},{3,1},{4,6},{5,7},{6,4},{7,5},{8,10},{9,11},{10,... | collective-permute-start | bytes 344072 | tf_op jit(solution)/shard_map/ppermute | solution.py:25
  9.0 1.5 %collective-permute-start = (f32[2,224,128]{2,1,0:T(8,128)}, f32[2,224,128]{2,1,0:T(8,128)S(1)}, u32[]{:S(2)}, u32[]{:S(2)}) collective-permute-start(f32[2,224,128]{2,1,0:T(8,128)} %bitcast.39), channel_id=1, source_target_pairs={{0,16},{16,0},{1,17},{17,1},{2,18},{18,2},{3,19},{19,3},{4,20},{20... | collective-permute-start | bytes 688136 | tf_op jit(solution)/shard_map/ppermute | solution.py:25
  10.5 0.0 collective-permute-done.3
  10.5 2.4 %collective-permute-done.1.refs_0_ = bf16[1,16,3584]{2,1,0:T(8,128)(2,1)S(1)} collective-permute-done((bf16[1,16,3584]{2,1,0:T(8,128)(2,1)S(1)}, bf16[1,16,3584]{2,1,0:T(8,128)(2,1)S(1)}, u32[]{:S(2)}, u32[]{:S(2)}) %collective-permute-start.1) | collective-permute-done | bytes 114720 | tf_op jit(solution)/shard_map/ppermute | solution.py:25
  12.9 0.0 copy-start.2
  12.9 1.6 %collective-permute-start.5 = (bf16[2,16,3584]{2,1,0:T(8,128)(2,1)S(1)}, bf16[2,16,3584]{2,1,0:T(8,128)(2,1)S(1)}, u32[]{:S(2)}, u32[]{:S(2)}) collective-permute-start(bf16[2,16,3584]{2,1,0:T(8,128)(2,1)S(1)} %pad_maximum_fusion.1), channel_id=1, source_target_pairs={{0,2},{1,3},{2,0},{3,1},{4,6},{5,7},{6,4},{7,5},{8,10},{9,11},{10,... | collective-permute-start | bytes 688136 | tf_op jit(solution)/shard_map/ppermute | solution.py:25
  14.5 0.4 collective-permute-start.4
  15.0 0.0 collective-permute-done.2
  15.0 0.1 pad_maximum_fusion.refs_3_
  15.0 0.0 copy-done
  15.0 0.5 shard_map.104.refs_2_
  15.5 3.8 %collective-permute-done.4 = bf16[1,16,3584]{2,1,0:T(8,128)(2,1)S(1)} collective-permute-done((bf16[1,16,3584]{2,1,0:T(8,128)(2,1)S(1)}, bf16[1,16,3584]{2,1,0:T(8,128)(2,1)S(1)}, u32[]{:S(2)}, u32[]{:S(2)}) %collective-permute-start.4) | collective-permute-done | bytes 114720 | tf_op jit(solution)/shard_map/ppermute | solution.py:25
  19.3 0.5 collective-permute-start.6
  19.8 0.0 collective-permute-done.other
  19.8 0.0 collective-permute-start.7
  19.8 0.0 collective-permute-done.5
  19.9 4.2 %collective-permute-done.6 = bf16[1,16,3584]{2,1,0:T(8,128)(2,1)S(1)} collective-permute-done((bf16[1,16,3584]{2,1,0:T(8,128)(2,1)S(1)}, bf16[1,16,3584]{2,1,0:T(8,128)(2,1)S(1)}, u32[]{:S(2)}, u32[]{:S(2)}) %collective-permute-start.6) | collective-permute-done | bytes 114720 | tf_op jit(solution)/shard_map/ppermute | solution.py:25
  24.1 0.1 collective-permute-start.8
  24.2 0.0 collective-permute-done.7.refs_5_
  24.2 1.8 %collective-permute-done.8.refs_6_ = bf16[4,16,3584]{2,1,0:T(8,128)(2,1)S(1)} collective-permute-done((bf16[4,16,3584]{2,1,0:T(8,128)(2,1)S(1)}, bf16[4,16,3584]{2,1,0:T(8,128)(2,1)S(1)}, u32[]{:S(2)}, u32[]{:S(2)}) %collective-permute-start.8) | collective-permute-done | bytes 458784 | tf_op jit(solution)/shard_map/ppermute | solution.py:25
  26.0 0.0 copy-done.2
  26.0 6.5 %shard_map.105 = (bf16[8,16,3584]{2,1,0:T(8,128)(2,1)S(1)}, bf16[8,16,3584]{2,1,0:T(8,128)(2,1)S(1)}) custom-call(bf16[128,7168]{1,0:T(8,128)(2,1)S(1)} %bitcast.38, bf16[128,7168]{1,0:T(8,128)(2,1)S(1)} %bitcast.42, f32[128,128]{1,0:T(8,128)S(1)} %shard_map.104.refs_2_, bf16[4,16,3584]{2,1,0:T(8,128)(2,1)S(1)} %pad_maximum_fusion.refs_3_, ...), custom_call_target="tpu_custom_call" | custom-call | tf_op jit(solution)/shard_map/pallas_call | solution.py:248
  32.5 0.2 collective-permute-start.9
  32.7 2.3 %collective-permute-done.9 = bf16[8,16,3584]{2,1,0:T(8,128)(2,1)S(1)} collective-permute-done((bf16[8,16,3584]{2,1,0:T(8,128)(2,1)S(1)}, bf16[8,16,3584]{2,1,0:T(8,128)(2,1)S(1)}, u32[]{:S(2)}, u32[]{:S(2)}) %collective-permute-start.9) | collective-permute-done | bytes 917536 | tf_op jit(solution)/shard_map/ppermute | solution.py:25
  35.0 0.1 add_convert_fusion
  35.1 0.6 %collective-permute-start.11 = (bf16[16,3584]{1,0:T(8,128)(2,1)S(1)}, bf16[16,3584]{1,0:T(8,128)(2,1)S(1)}, u32[]{:S(2)}, u32[]{:S(2)}) collective-permute-start(bf16[16,3584]{1,0:T(8,128)(2,1)S(1)} %get-tuple-element.21), channel_id=1, source_target_pairs={{0,2},{1,3},{2,0},{3,1},{4,6},{5,7},{6,4},{7,5},{8,10},{9,11},{10,... | collective-permute-start | bytes 344072 | tf_op jit(solution)/shard_map/ppermute | solution.py:25
  35.7 0.1 convert_add_fusion
  35.8 0.0 copy-start.7
  35.8 1.6 %collective-permute-start.13 = (bf16[16,3584]{1,0:T(8,128)(2,1)S(1)}, bf16[16,3584]{1,0:T(8,128)(2,1)S(1)}, u32[]{:S(2)}, u32[]{:S(2)}) collective-permute-start(bf16[16,3584]{1,0:T(8,128)(2,1)S(1)} %get-tuple-element.22), channel_id=1, source_target_pairs={{0,2},{1,3},{2,0},{3,1},{4,6},{5,7},{6,4},{7,5},{8,10},{9,11},{10,... | collective-permute-start | bytes 344072 | tf_op jit(solution)/shard_map/ppermute | solution.py:25
  37.4 3.8 %collective-permute-done.11 = bf16[16,3584]{1,0:T(8,128)(2,1)S(1)} collective-permute-done((bf16[16,3584]{1,0:T(8,128)(2,1)S(1)}, bf16[16,3584]{1,0:T(8,128)(2,1)S(1)}, u32[]{:S(2)}, u32[]{:S(2)}) %collective-permute-start.11) | collective-permute-done | bytes 114720 | tf_op jit(solution)/shard_map/ppermute | solution.py:25
  41.2 0.0 copy-start.5
  41.2 0.0 copy-start.6
  41.2 0.5 collective-permute-start.12
  42.4 0.0 copy-done.1
  42.5 0.6 %collective-permute-start.10 = (bf16[2,16,3584]{2,1,0:T(8,128)(2,1)S(1)}, bf16[2,16,3584]{2,1,0:T(8,128)(2,1)S(1)}, u32[]{:S(2)}, u32[]{:S(2)}) collective-permute-start(bf16[2,16,3584]{2,1,0:T(8,128)(2,1)S(1)} %slice.53), channel_id=1, source_target_pairs={{0,2},{1,3},{2,0},{3,1},{4,6},{5,7},{6,4},{7,5},{8,10},{9,11},{10,... | collective-permute-start | bytes 688136 | tf_op jit(solution)/shard_map/ppermute | solution.py:25
  43.1 0.0 collective-permute-done.13
  43.1 3.0 %collective-permute-done.12 = bf16[16,3584]{1,0:T(8,128)(2,1)S(1)} collective-permute-done((bf16[16,3584]{1,0:T(8,128)(2,1)S(1)}, bf16[16,3584]{1,0:T(8,128)(2,1)S(1)}, u32[]{:S(2)}, u32[]{:S(2)}) %collective-permute-start.12) | collective-permute-done | bytes 114720 | tf_op jit(solution)/shard_map/ppermute | solution.py:25
  46.2 1.1 %collective-permute-start.14 = (bf16[16,3584]{1,0:T(8,128)(2,1)S(1)}, bf16[16,3584]{1,0:T(8,128)(2,1)S(1)}, u32[]{:S(2)}, u32[]{:S(2)}) collective-permute-start(bf16[16,3584]{1,0:T(8,128)(2,1)S(1)} %fusion.3), channel_id=1, source_target_pairs={{0,8},{1,9},{2,10},{3,11},{4,12},{5,13},{6,14},{7,15},{8,0},{9,1},... | collective-permute-start | bytes 344072 | tf_op jit(solution)/shard_map/ppermute | solution.py:25
  47.2 1.3 %collective-permute-done.10 = bf16[2,16,3584]{2,1,0:T(8,128)(2,1)S(1)} collective-permute-done((bf16[2,16,3584]{2,1,0:T(8,128)(2,1)S(1)}, bf16[2,16,3584]{2,1,0:T(8,128)(2,1)S(1)}, u32[]{:S(2)}, u32[]{:S(2)}) %collective-permute-start.10) | collective-permute-done | bytes 229408 | tf_op jit(solution)/shard_map/ppermute | solution.py:25
  48.6 1.7 %collective-permute-start.15 = (bf16[16,3584]{1,0:T(8,128)(2,1)S(1)}, bf16[16,3584]{1,0:T(8,128)(2,1)S(1)}, u32[]{:S(2)}, u32[]{:S(2)}) collective-permute-start(bf16[16,3584]{1,0:T(8,128)(2,1)S(1)} %get-tuple-element.19), channel_id=1, source_target_pairs={{0,4},{1,5},{2,6},{3,7},{4,0},{5,1},{6,2},{7,3},{8,12},{9,13},{10,... | collective-permute-start | bytes 344072 | tf_op jit(solution)/shard_map/ppermute | solution.py:25
  50.3 0.7 %multiply_subtract_fusion = (f32[224,128]{1,0:T(8,128)S(1)}, f32[224,128]{1,0:T(8,128)}) fusion(f32[224,128]{1,0:T(8,128)S(1)} %copy-done.4, f32[224,128]{1,0:T(8,128)S(1)} %shard_map.103, f32[224,128]{1,0:T(8,128)S(1)} %copy-done.7), kind=kLoop, calls=%fused_computation.18 | loop fusion | flops 200704 | bytes 573440 | tf_op jit(solution)/shard_map/sub | solution.py:377
  51.0 2.1 %collective-permute-done.14.refs_7_ = bf16[16,3584]{1,0:T(8,128)(2,1)S(1)} collective-permute-done((bf16[16,3584]{1,0:T(8,128)(2,1)S(1)}, bf16[16,3584]{1,0:T(8,128)(2,1)S(1)}, u32[]{:S(2)}, u32[]{:S(2)}) %collective-permute-start.14) | collective-permute-done | bytes 114720 | tf_op jit(solution)/shard_map/ppermute | solution.py:25
  53.1 0.8 %collective-permute-done.15.refs_8_ = bf16[16,3584]{1,0:T(8,128)(2,1)S(1)} collective-permute-done((bf16[16,3584]{1,0:T(8,128)(2,1)S(1)}, bf16[16,3584]{1,0:T(8,128)(2,1)S(1)}, u32[]{:S(2)}, u32[]{:S(2)}) %collective-permute-start.15) | collective-permute-done | bytes 114720 | tf_op jit(solution)/shard_map/ppermute | solution.py:25
  53.9 1.0 %shard_map.106 = f32[2,224,128]{2,1,0:T(8,128)} custom-call(s32[1]{0:T(128)S(6)} %copy.16.fragment.refs_0_, f32[2,224,128]{2,1,0:T(8,128)S(1)} %bitcast.41, f32[2,224,128]{2,1,0:T(8,128)S(1)} %bitcast.43, f32[2,224,128]{2,1,0:T(8,128)S(1)} %bitcast.44, f32[224,128]{1,0:T(8,128)S(1)} %get-tuple-element.17.refs_4_, f32[16,3584]{1,0:T(8,128)S(1)} %get-tuple-element.20.refs_5_, ...), custom_call_target="tpu_custom_call" | custom-call | tf_op jit(solution)/shard_map/pallas_call | solution.py:317
  (21 shorter events, 0.3 us)
Async XLA Ops:
  0.6 14.4 %copy-start = (bf16[1,128,7168]{2,1,0:T(8,128)(2,1)S(1)}, bf16[1,128,7168]{2,1,0:T(8,128)(2,1)}, u32[]{:S(2)}) copy-start(bf16[1,128,7168]{2,1,0:T(8,128)(2,1)} %param.8) | copy-start | bytes 5505028
  1.8 8.7 %collective-permute-start.3 = (bf16[1,16,3584]{2,1,0:T(8,128)(2,1)S(1)}, bf16[1,16,3584]{2,1,0:T(8,128)(2,1)S(1)}, u32[]{:S(2)}, u32[]{:S(2)}) collective-permute-start(bf16[1,16,3584]{2,1,0:T(8,128)(2,1)S(1)} %bitcast.45), channel_id=1, source_target_pairs={{0,4},{1,5},{2,6},{3,7},{4,0},{5,1},{6,2},{7,3},{8,12},{9,13},{10,... | collective-permute-start | bytes 344072 | tf_op jit(solution)/shard_map/ppermute | solution.py:25
  4.9 8.0 %collective-permute-start.1 = (bf16[1,16,3584]{2,1,0:T(8,128)(2,1)S(1)}, bf16[1,16,3584]{2,1,0:T(8,128)(2,1)S(1)}, u32[]{:S(2)}, u32[]{:S(2)}) collective-permute-start(bf16[1,16,3584]{2,1,0:T(8,128)(2,1)S(1)} %bitcast.46), channel_id=1, source_target_pairs={{0,8},{1,9},{2,10},{3,11},{4,12},{5,13},{6,14},{7,15},{8,0},{9,1},... | collective-permute-start | bytes 344072 | tf_op jit(solution)/shard_map/ppermute | solution.py:25
  7.5 7.5 %collective-permute-start.2 = (bf16[1,16,3584]{2,1,0:T(8,128)(2,1)S(1)}, bf16[1,16,3584]{2,1,0:T(8,128)(2,1)S(1)}, u32[]{:S(2)}, u32[]{:S(2)}) collective-permute-start(bf16[1,16,3584]{2,1,0:T(8,128)(2,1)S(1)} %bitcast.47), channel_id=1, source_target_pairs={{0,2},{1,3},{2,0},{3,1},{4,6},{5,7},{6,4},{7,5},{8,10},{9,11},{10,... | collective-permute-start | bytes 344072 | tf_op jit(solution)/shard_map/ppermute | solution.py:25
  9.0 10.8 %collective-permute-start = (f32[2,224,128]{2,1,0:T(8,128)}, f32[2,224,128]{2,1,0:T(8,128)S(1)}, u32[]{:S(2)}, u32[]{:S(2)}) collective-permute-start(f32[2,224,128]{2,1,0:T(8,128)} %bitcast.39), channel_id=1, source_target_pairs={{0,16},{16,0},{1,17},{17,1},{2,18},{18,2},{3,19},{19,3},{4,20},{20... | collective-permute-start | bytes 688136 | tf_op jit(solution)/shard_map/ppermute | solution.py:25
  12.9 13.1 %copy-start.2 = (bf16[1,128,7168]{2,1,0:T(8,128)(2,1)S(1)}, bf16[1,128,7168]{2,1,0:T(8,128)(2,1)}, u32[]{:S(2)}) copy-start(bf16[1,128,7168]{2,1,0:T(8,128)(2,1)} %param.9) | copy-start | bytes 5505028
  12.9 6.9 %collective-permute-start.5 = (bf16[2,16,3584]{2,1,0:T(8,128)(2,1)S(1)}, bf16[2,16,3584]{2,1,0:T(8,128)(2,1)S(1)}, u32[]{:S(2)}, u32[]{:S(2)}) collective-permute-start(bf16[2,16,3584]{2,1,0:T(8,128)(2,1)S(1)} %pad_maximum_fusion.1), channel_id=1, source_target_pairs={{0,2},{1,3},{2,0},{3,1},{4,6},{5,7},{6,4},{7,5},{8,10},{9,11},{10,... | collective-permute-start | bytes 688136 | tf_op jit(solution)/shard_map/ppermute | solution.py:25
  14.5 4.8 %collective-permute-start.4 = (bf16[1,16,3584]{2,1,0:T(8,128)(2,1)S(1)}, bf16[1,16,3584]{2,1,0:T(8,128)(2,1)S(1)}, u32[]{:S(2)}, u32[]{:S(2)}) collective-permute-start(bf16[1,16,3584]{2,1,0:T(8,128)(2,1)S(1)} %collective-permute-done.1.refs_0_), channel_id=1, source_target_pairs={{0,4},{1,5},{2,6},{3,7},{4,0},{5,1},{6,2},{7,3},{8,12},{9,13},{10,... | collective-permute-start | bytes 344072 | tf_op jit(solution)/shard_map/ppermute | solution.py:25
  19.3 4.8 %collective-permute-start.6 = (bf16[1,16,3584]{2,1,0:T(8,128)(2,1)S(1)}, bf16[1,16,3584]{2,1,0:T(8,128)(2,1)S(1)}, u32[]{:S(2)}, u32[]{:S(2)}) collective-permute-start(bf16[1,16,3584]{2,1,0:T(8,128)(2,1)S(1)} %collective-permute-done.4), channel_id=1, source_target_pairs={{0,2},{1,3},{2,0},{3,1},{4,6},{5,7},{6,4},{7,5},{8,10},{9,11},{10,... | collective-permute-start | bytes 344072 | tf_op jit(solution)/shard_map/ppermute | solution.py:25
  19.8 4.4 %collective-permute-start.7 = (bf16[4,16,3584]{2,1,0:T(8,128)(2,1)S(1)}, bf16[4,16,3584]{2,1,0:T(8,128)(2,1)S(1)}, u32[]{:S(2)}, u32[]{:S(2)}) collective-permute-start(bf16[4,16,3584]{2,1,0:T(8,128)(2,1)S(1)} %pad_maximum_fusion.refs_3_), channel_id=1, source_target_pairs={{0,1},{1,0},{2,3},{3,2},{4,5},{5,4},{6,7},{7,6},{8,9},{9,8},{10,11... | collective-permute-start | bytes 1376264 | tf_op jit(solution)/shard_map/ppermute | solution.py:25
  24.1 1.9 %collective-permute-start.8 = (bf16[4,16,3584]{2,1,0:T(8,128)(2,1)S(1)}, bf16[4,16,3584]{2,1,0:T(8,128)(2,1)S(1)}, u32[]{:S(2)}, u32[]{:S(2)}) collective-permute-start(bf16[4,16,3584]{2,1,0:T(8,128)(2,1)S(1)} %constant_dynamic-update-slice_fusion.refs_4_), channel_id=1, source_target_pairs={{0,1},{1,0},{2,3},{3,2},{4,5},{5,4},{6,7},{7,6},{8,9},{9,8},{10,11... | collective-permute-start | bytes 1376264 | tf_op jit(solution)/shard_map/ppermute | solution.py:25
  32.5 2.5 %collective-permute-start.9 = (bf16[8,16,3584]{2,1,0:T(8,128)(2,1)S(1)}, bf16[8,16,3584]{2,1,0:T(8,128)(2,1)S(1)}, u32[]{:S(2)}, u32[]{:S(2)}) collective-permute-start(bf16[8,16,3584]{2,1,0:T(8,128)(2,1)S(1)} %get-tuple-element.13), channel_id=1, source_target_pairs={{0,1},{1,0},{2,3},{3,2},{4,5},{5,4},{6,7},{7,6},{8,9},{9,8},{10,11... | collective-permute-start | bytes 2752520 | tf_op jit(solution)/shard_map/ppermute | solution.py:25
  35.0 7.4 %copy-start.1 = (f32[1,2,224,128]{3,2,1,0:T(8,128)S(1)}, f32[1,2,224,128]{3,2,1,0:T(8,128)}, u32[]{:S(2)}) copy-start(f32[1,2,224,128]{3,2,1,0:T(8,128)} %param.10) | copy-start | bytes 688132
  35.0 7.4 %copy-start.4 = (f32[224,128]{1,0:T(8,128)S(1)}, f32[224,128]{1,0:T(8,128)}, u32[]{:S(2)}) copy-start(f32[224,128]{1,0:T(8,128)} %anchor.1) | copy-start | bytes 344068
  35.1 6.1 %collective-permute-start.11 = (bf16[16,3584]{1,0:T(8,128)(2,1)S(1)}, bf16[16,3584]{1,0:T(8,128)(2,1)S(1)}, u32[]{:S(2)}, u32[]{:S(2)}) collective-permute-start(bf16[16,3584]{1,0:T(8,128)(2,1)S(1)} %get-tuple-element.21), channel_id=1, source_target_pairs={{0,2},{1,3},{2,0},{3,1},{4,6},{5,7},{6,4},{7,5},{8,10},{9,11},{10,... | collective-permute-start | bytes 344072 | tf_op jit(solution)/shard_map/ppermute | solution.py:25
  35.8 14.5 %copy-start.7 = (f32[224,128]{1,0:T(8,128)S(1)}, f32[224,128]{1,0:T(8,128)}, u32[]{:S(2)}) copy-start(f32[224,128]{1,0:T(8,128)} %param.14) | copy-start | bytes 344068
  35.8 7.2 %collective-permute-start.13 = (bf16[16,3584]{1,0:T(8,128)(2,1)S(1)}, bf16[16,3584]{1,0:T(8,128)(2,1)S(1)}, u32[]{:S(2)}, u32[]{:S(2)}) collective-permute-start(bf16[16,3584]{1,0:T(8,128)(2,1)S(1)} %get-tuple-element.22), channel_id=1, source_target_pairs={{0,2},{1,3},{2,0},{3,1},{4,6},{5,7},{6,4},{7,5},{8,10},{9,11},{10,... | collective-permute-start | bytes 344072 | tf_op jit(solution)/shard_map/ppermute | solution.py:25
  41.2 12.7 %copy-start.5 = (f32[1,2,224,128]{3,2,1,0:T(8,128)S(1)}, f32[1,2,224,128]{3,2,1,0:T(8,128)}, u32[]{:S(2)}) copy-start(f32[1,2,224,128]{3,2,1,0:T(8,128)} %param.11) | copy-start | bytes 688132
  41.2 12.7 %copy-start.6 = (f32[1,2,224,128]{3,2,1,0:T(8,128)S(1)}, f32[1,2,224,128]{3,2,1,0:T(8,128)}, u32[]{:S(2)}) copy-start(f32[1,2,224,128]{3,2,1,0:T(8,128)} %param.12) | copy-start | bytes 688132
  41.2 4.9 %collective-permute-start.12 = (bf16[16,3584]{1,0:T(8,128)(2,1)S(1)}, bf16[16,3584]{1,0:T(8,128)(2,1)S(1)}, u32[]{:S(2)}, u32[]{:S(2)}) collective-permute-start(bf16[16,3584]{1,0:T(8,128)(2,1)S(1)} %fusion.5), channel_id=1, source_target_pairs={{0,4},{1,5},{2,6},{3,7},{4,0},{5,1},{6,2},{7,3},{8,12},{9,13},{10,... | collective-permute-start | bytes 344072 | tf_op jit(solution)/shard_map/ppermute | solution.py:25
  42.5 6.1 %collective-permute-start.10 = (bf16[2,16,3584]{2,1,0:T(8,128)(2,1)S(1)}, bf16[2,16,3584]{2,1,0:T(8,128)(2,1)S(1)}, u32[]{:S(2)}, u32[]{:S(2)}) collective-permute-start(bf16[2,16,3584]{2,1,0:T(8,128)(2,1)S(1)} %slice.53), channel_id=1, source_target_pairs={{0,2},{1,3},{2,0},{3,1},{4,6},{5,7},{6,4},{7,5},{8,10},{9,11},{10,... | collective-permute-start | bytes 688136 | tf_op jit(solution)/shard_map/ppermute | solution.py:25
  46.2 6.9 %collective-permute-start.14 = (bf16[16,3584]{1,0:T(8,128)(2,1)S(1)}, bf16[16,3584]{1,0:T(8,128)(2,1)S(1)}, u32[]{:S(2)}, u32[]{:S(2)}) collective-permute-start(bf16[16,3584]{1,0:T(8,128)(2,1)S(1)} %fusion.3), channel_id=1, source_target_pairs={{0,8},{1,9},{2,10},{3,11},{4,12},{5,13},{6,14},{7,15},{8,0},{9,1},... | collective-permute-start | bytes 344072 | tf_op jit(solution)/shard_map/ppermute | solution.py:25
  48.6 5.3 %collective-permute-start.15 = (bf16[16,3584]{1,0:T(8,128)(2,1)S(1)}, bf16[16,3584]{1,0:T(8,128)(2,1)S(1)}, u32[]{:S(2)}, u32[]{:S(2)}) collective-permute-start(bf16[16,3584]{1,0:T(8,128)(2,1)S(1)} %get-tuple-element.19), channel_id=1, source_target_pairs={{0,4},{1,5},{2,6},{3,7},{4,0},{5,1},{6,2},{7,3},{8,12},{9,13},{10,... | collective-permute-start | bytes 344072 | tf_op jit(solution)/shard_map/ppermute | solution.py:25
  51.0 3.9 %copy-start.3 = (f32[224,128]{1,0:T(8,128)}, f32[224,128]{1,0:T(8,128)S(1)}, u32[]{:S(2)}) copy-start(f32[224,128]{1,0:T(8,128)S(1)} %get-tuple-element.17.refs_4_) | copy-start | bytes 344068

commit v6 on v5

--- a/solution.py
+++ b/solution.py
@@ -66,28 +66,25 @@
 def reduce_blocks(odd, even, axis):
     size = lax.axis_size(axis)
     tops = list(range(size - 4, -1, -4))
-    half = len(tops) // 2
     came = swap(odd, axis, 1)
     sums = add_f32(even[: len(tops)], came[: len(tops)]).astype(jnp.bfloat16)
-    near = [swap(sums[at], axis, 2) for at in range(half)]
-    rest = swap(sums[half:], axis, 2)
     came = after(came, sums)
     kept = add_f32(even[len(tops) :], came[len(tops) :])
-    parts = []
-    left = {}
-    for at, k in enumerate(tops):
-        if at == half:
-            rest = after(rest, part)
-        arrived = near[at] if at < half else rest[at - half]
-        if k:
-            left[k] = left.get(k, 0.0) + kept[at] + arrived.astype(jnp.float32)
-            part = left[k].astype(jnp.bfloat16)
-            moved = swap(part, axis, k & -k)
-            if k & (k - 1):
-                left[k & (k - 1)] = left.get(k & (k - 1), 0.0) + moved.astype(jnp.float32)
-            else:
-                parts.append(moved)
-    return [kept[-1], rest[-1]] + parts
+    near = [swap(sums[0], axis, 2)]
+    middle = swap(after(sums[1:-1], near[0]), axis, 2)
+    near += [middle[at] for at in range(len(tops) - 2)]
+    left, parts = {}, []
+    for at, k in enumerate(tops[:-1]):
+        arrived = after(near[at], part) if at > 1 else near[at]
+        part = (left.get(k, 0.0) + kept[at] + arrived.astype(jnp.float32)).astype(jnp.bfloat16)
+        moved = swap(part, axis, k & -k)
+        if k & (k - 1):
+            left[k & (k - 1)] = left.get(k & (k - 1), 0.0) + moved.astype(jnp.float32)
+        else:
+            parts.append(moved)
+        if at == len(tops) - 3:
+            last = swap(after(sums[-1], part), axis, 2)
+    return [kept[-1], last] + parts
 
 
 def dot_nt(left, right):
@@ -372,7 +369,7 @@
     while step < replicas:
         total = total + swap(total, "rep", step)
         step *= 2
-    mean_delta = after(total, parts[1]) / replicas
+    mean_delta = after(total, parts[-1]) / replicas
     new_velocity = outer_beta * momentum + mean_delta
     new_global = anchor - outer_rate * (mean_delta + outer_beta * new_velocity)
     scales = (model_width ** (-0.5), hidden ** (-0.5))

time: 55.1 us -> 56.5 us (1.025)
  waiting for transfers between devices: 25.7 us -> 27.8 us
  starting transfers between devices: 17.5 us -> 16.7 us
    ppermute x16, waiting for transfers between devices: 25.7 us -> 27.8 us  [swap(): return lax.ppermute(value, axis, [(i, i ^ mask) for i in range(size)])]
    ppermute x16, starting transfers between devices: 17.5 us -> 16.7 us  [swap(): return lax.ppermute(value, axis, [(i, i ^ mask) for i in range(size)])]
  transfers between devices with their start and end apart: 16 -> 16, of which waited for: 10 -> 9; matrix products, arithmetic and copies ran while one was open for 2% -> 2% of each run, Pallas kernels for 1% -> 1%
where the time goes in v6:
time: 56.5 us; the launch traced here: 56.3 us
  waiting for transfers between devices  27.8 us (49%)
  starting transfers between devices  16.7 us (30%)
  Pallas kernels  7.97 us (14%)
  other arithmetic  2.13 us (4%)
  between operations  1.5 us (3%)
    ppermute x16, waiting for transfers between devices, swap(): return lax.ppermute(value, axis, [(i, i ^ mask) for i in range(size)])  27.8 us
    ppermute x16, starting transfers between devices, swap(): return lax.ppermute(value, axis, [(i, i ^ mask) for i in range(size)])  16.7 us
    pallas_call x1, Pallas kernels, adapter_grads(): pl.pallas_call(functools.partial(adapter_kernel, len(arrays), sources, pl...  6.48 us
  transfers between devices with their start and end apart: 16, of which 9 were waited for; matrix products, arithmetic and copies ran while one was open for 2% of the time, Pallas kernels for 1%

profile of v6, /device:TPU:0, one launch (start us, length us, event | category | flops | bytes accessed | tf_op | source)
XLA Modules:
  0.0 56.3 jit_solution(288909607761479007)
XLA Ops:
  0.6 0.0 copy-start
  0.6 1.1 %convert_element_type.46 = bf16[1,2,224,128]{3,2,1,0:T(8,128)(2,1)S(1)} convert(f32[1,2,224,128]{3,2,1,0:T(8,128)} %param.10) | non-fusion elementwise | flops 57344 | bytes 344064 | tf_op jit(solution)/shard_map/convert_element_type | solution.py:339
  1.8 3.1 %collective-permute-start.3 = (bf16[1,16,3584]{2,1,0:T(8,128)(2,1)S(1)}, bf16[1,16,3584]{2,1,0:T(8,128)(2,1)S(1)}, u32[]{:S(2)}, u32[]{:S(2)}) collective-permute-start(bf16[1,16,3584]{2,1,0:T(8,128)(2,1)S(1)} %bitcast.54), channel_id=1, source_target_pairs={{0,4},{1,5},{2,6},{3,7},{4,0},{5,1},{6,2},{7,3},{8,12},{9,13},{10,... | collective-permute-start | bytes 344072 | tf_op jit(solution)/shard_map/ppermute | solution.py:25
  4.9 2.6 %collective-permute-start.1 = (bf16[1,16,3584]{2,1,0:T(8,128)(2,1)S(1)}, bf16[1,16,3584]{2,1,0:T(8,128)(2,1)S(1)}, u32[]{:S(2)}, u32[]{:S(2)}) collective-permute-start(bf16[1,16,3584]{2,1,0:T(8,128)(2,1)S(1)} %bitcast.55), channel_id=1, source_target_pairs={{0,8},{1,9},{2,10},{3,11},{4,12},{5,13},{6,14},{7,15},{8,0},{9,1},... | collective-permute-start | bytes 344072 | tf_op jit(solution)/shard_map/ppermute | solution.py:25
  7.5 1.5 %collective-permute-start.2 = (bf16[1,16,3584]{2,1,0:T(8,128)(2,1)S(1)}, bf16[1,16,3584]{2,1,0:T(8,128)(2,1)S(1)}, u32[]{:S(2)}, u32[]{:S(2)}) collective-permute-start(bf16[1,16,3584]{2,1,0:T(8,128)(2,1)S(1)} %bitcast.56), channel_id=1, source_target_pairs={{0,2},{1,3},{2,0},{3,1},{4,6},{5,7},{6,4},{7,5},{8,10},{9,11},{10,... | collective-permute-start | bytes 344072 | tf_op jit(solution)/shard_map/ppermute | solution.py:25
  9.0 1.5 %collective-permute-start = (f32[2,224,128]{2,1,0:T(8,128)}, f32[2,224,128]{2,1,0:T(8,128)S(1)}, u32[]{:S(2)}, u32[]{:S(2)}) collective-permute-start(f32[2,224,128]{2,1,0:T(8,128)} %bitcast.48), channel_id=1, source_target_pairs={{0,16},{16,0},{1,17},{17,1},{2,18},{18,2},{3,19},{19,3},{4,20},{20... | collective-permute-start | bytes 688136 | tf_op jit(solution)/shard_map/ppermute | solution.py:25
  10.5 0.0 collective-permute-done.3
  10.5 2.4 %collective-permute-done.1.refs_0_ = bf16[1,16,3584]{2,1,0:T(8,128)(2,1)S(1)} collective-permute-done((bf16[1,16,3584]{2,1,0:T(8,128)(2,1)S(1)}, bf16[1,16,3584]{2,1,0:T(8,128)(2,1)S(1)}, u32[]{:S(2)}, u32[]{:S(2)}) %collective-permute-start.1) | collective-permute-done | bytes 114720 | tf_op jit(solution)/shard_map/ppermute | solution.py:25
  12.9 0.0 copy-start.2
  12.9 1.6 %collective-permute-start.5 = (bf16[2,16,3584]{2,1,0:T(8,128)(2,1)S(1)}, bf16[2,16,3584]{2,1,0:T(8,128)(2,1)S(1)}, u32[]{:S(2)}, u32[]{:S(2)}) collective-permute-start(bf16[2,16,3584]{2,1,0:T(8,128)(2,1)S(1)} %pad_maximum_fusion.1), channel_id=1, source_target_pairs={{0,2},{1,3},{2,0},{3,1},{4,6},{5,7},{6,4},{7,5},{8,10},{9,11},{10,... | collective-permute-start | bytes 688136 | tf_op jit(solution)/shard_map/ppermute | solution.py:25
  14.5 0.4 collective-permute-start.4
  15.0 0.0 collective-permute-done.2
  15.0 0.1 pad_maximum_fusion.refs_3_
  15.0 0.5 shard_map.104.refs_2_
  15.5 3.8 %collective-permute-done.4 = bf16[1,16,3584]{2,1,0:T(8,128)(2,1)S(1)} collective-permute-done((bf16[1,16,3584]{2,1,0:T(8,128)(2,1)S(1)}, bf16[1,16,3584]{2,1,0:T(8,128)(2,1)S(1)}, u32[]{:S(2)}, u32[]{:S(2)}) %collective-permute-start.4) | collective-permute-done | bytes 114720 | tf_op jit(solution)/shard_map/ppermute | solution.py:25
  19.3 0.5 collective-permute-start.6
  19.8 0.0 collective-permute-done.other
  19.8 0.0 collective-permute-start.7
  19.8 0.0 collective-permute-done.5
  19.9 4.2 %collective-permute-done.6 = bf16[1,16,3584]{2,1,0:T(8,128)(2,1)S(1)} collective-permute-done((bf16[1,16,3584]{2,1,0:T(8,128)(2,1)S(1)}, bf16[1,16,3584]{2,1,0:T(8,128)(2,1)S(1)}, u32[]{:S(2)}, u32[]{:S(2)}) %collective-permute-start.6) | collective-permute-done | bytes 114720 | tf_op jit(solution)/shard_map/ppermute | solution.py:25
  24.1 0.1 collective-permute-start.8
  24.2 0.0 collective-permute-done.7.refs_5_
  24.2 1.8 %collective-permute-done.8.refs_6_ = bf16[4,16,3584]{2,1,0:T(8,128)(2,1)S(1)} collective-permute-done((bf16[4,16,3584]{2,1,0:T(8,128)(2,1)S(1)}, bf16[4,16,3584]{2,1,0:T(8,128)(2,1)S(1)}, u32[]{:S(2)}, u32[]{:S(2)}) %collective-permute-start.8) | collective-permute-done | bytes 458784 | tf_op jit(solution)/shard_map/ppermute | solution.py:25
  26.0 0.0 copy-done.2
  26.0 6.5 %shard_map.105 = (bf16[8,16,3584]{2,1,0:T(8,128)(2,1)S(1)}, bf16[8,16,3584]{2,1,0:T(8,128)(2,1)S(1)}) custom-call(bf16[128,7168]{1,0:T(8,128)(2,1)S(1)} %bitcast.47, bf16[128,7168]{1,0:T(8,128)(2,1)S(1)} %bitcast.51, f32[128,128]{1,0:T(8,128)S(1)} %shard_map.104.refs_2_, bf16[4,16,3584]{2,1,0:T(8,128)(2,1)S(1)} %pad_maximum_fusion.refs_3_, ...), custom_call_target="tpu_custom_call" | custom-call | tf_op jit(solution)/shard_map/pallas_call | solution.py:245
  32.5 0.2 collective-permute-start.9
  33.3 0.0 copy-done.1
  33.3 0.0 copy-done.4
  33.4 1.6 %collective-permute-done.9 = bf16[8,16,3584]{2,1,0:T(8,128)(2,1)S(1)} collective-permute-done((bf16[8,16,3584]{2,1,0:T(8,128)(2,1)S(1)}, bf16[8,16,3584]{2,1,0:T(8,128)(2,1)S(1)}, u32[]{:S(2)}, u32[]{:S(2)}) %collective-permute-start.9) | collective-permute-done | bytes 917536 | tf_op jit(solution)/shard_map/ppermute | solution.py:25
  35.0 0.1 add_convert_fusion
  35.2 0.0 copy-start.7
  35.2 0.6 collective-permute-start.10
  35.7 0.1 convert_add_fusion
  35.8 0.0 copy-start.5
  35.8 0.0 copy-start.6
  35.9 4.6 %collective-permute-done.10 = bf16[16,3584]{1,0:T(8,128)(2,1)S(1)} collective-permute-done((bf16[16,3584]{1,0:T(8,128)(2,1)S(1)}, bf16[16,3584]{1,0:T(8,128)(2,1)S(1)}, u32[]{:S(2)}, u32[]{:S(2)}) %collective-permute-start.10) | collective-permute-done | bytes 114720 | tf_op jit(solution)/shard_map/ppermute | solution.py:25
  40.4 0.5 collective-permute-start.11
  40.9 0.5 collective-permute-start.12
  41.5 5.8 %collective-permute-done.11 = bf16[2,16,3584]{2,1,0:T(8,128)(2,1)S(1)} collective-permute-done((bf16[2,16,3584]{2,1,0:T(8,128)(2,1)S(1)}, bf16[2,16,3584]{2,1,0:T(8,128)(2,1)S(1)}, u32[]{:S(2)}, u32[]{:S(2)}) %collective-permute-start.11) | collective-permute-done | bytes 229408 | tf_op jit(solution)/shard_map/ppermute | solution.py:25
  47.3 0.0 collective-permute-done.12
  47.3 0.5 collective-permute-start.13
  47.9 2.6 %collective-permute-start.15 = (bf16[16,3584]{1,0:T(8,128)(2,1)S(1)}, bf16[16,3584]{1,0:T(8,128)(2,1)S(1)}, u32[]{:S(2)}, u32[]{:S(2)}) collective-permute-start(bf16[16,3584]{1,0:T(8,128)(2,1)S(1)} %fusion.2), channel_id=1, source_target_pairs={{0,8},{1,9},{2,10},{3,11},{4,12},{5,13},{6,14},{7,15},{8,0},{9,1},... | collective-permute-start | bytes 344072 | tf_op jit(solution)/shard_map/ppermute | solution.py:25
  50.5 0.5 collective-permute-start.14
  51.0 1.3 %collective-permute-done.13.refs_8_ = bf16[16,3584]{1,0:T(8,128)(2,1)S(1)} collective-permute-done((bf16[16,3584]{1,0:T(8,128)(2,1)S(1)}, bf16[16,3584]{1,0:T(8,128)(2,1)S(1)}, u32[]{:S(2)}, u32[]{:S(2)}) %collective-permute-start.13) | collective-permute-done | bytes 114720 | tf_op jit(solution)/shard_map/ppermute | solution.py:25
  52.3 0.7 %multiply_subtract_fusion = (f32[224,128]{1,0:T(8,128)S(1)}, f32[224,128]{1,0:T(8,128)}) fusion(f32[224,128]{1,0:T(8,128)S(1)} %copy-done.4, f32[224,128]{1,0:T(8,128)S(1)} %shard_map.103, f32[224,128]{1,0:T(8,128)S(1)} %copy-done.7), kind=kLoop, calls=%fused_computation.20 | loop fusion | flops 200704 | bytes 573440 | tf_op jit(solution)/shard_map/sub | solution.py:374
  53.0 2.3 %collective-permute-done.14.refs_6_ = bf16[16,3584]{1,0:T(8,128)(2,1)S(1)} collective-permute-done((bf16[16,3584]{1,0:T(8,128)(2,1)S(1)}, bf16[16,3584]{1,0:T(8,128)(2,1)S(1)}, u32[]{:S(2)}, u32[]{:S(2)}) %collective-permute-start.14) | collective-permute-done | bytes 114720 | tf_op jit(solution)/shard_map/ppermute | solution.py:25
  55.3 0.0 collective-permute-done.15.refs_7_
  55.3 1.0 %shard_map.106 = f32[2,224,128]{2,1,0:T(8,128)} custom-call(s32[1]{0:T(128)S(6)} %copy.16.fragment.refs_0_, f32[2,224,128]{2,1,0:T(8,128)S(1)} %bitcast.50, f32[2,224,128]{2,1,0:T(8,128)S(1)} %bitcast.52, f32[2,224,128]{2,1,0:T(8,128)S(1)} %bitcast.53, f32[224,128]{1,0:T(8,128)S(1)} %get-tuple-element.21.refs_4_, f32[16,3584]{1,0:T(8,128)S(1)} %slice_bitcast_fusion.refs_5_, ...), custom_call_target="tpu_custom_call" | custom-call | tf_op jit(solution)/shard_map/pallas_call | solution.py:314
  (22 shorter events, 0.3 us)
Async XLA Ops:
  0.6 14.4 %copy-start = (bf16[1,128,7168]{2,1,0:T(8,128)(2,1)S(1)}, bf16[1,128,7168]{2,1,0:T(8,128)(2,1)}, u32[]{:S(2)}) copy-start(bf16[1,128,7168]{2,1,0:T(8,128)(2,1)} %param.8) | copy-start | bytes 5505028
  1.8 8.7 %collective-permute-start.3 = (bf16[1,16,3584]{2,1,0:T(8,128)(2,1)S(1)}, bf16[1,16,3584]{2,1,0:T(8,128)(2,1)S(1)}, u32[]{:S(2)}, u32[]{:S(2)}) collective-permute-start(bf16[1,16,3584]{2,1,0:T(8,128)(2,1)S(1)} %bitcast.54), channel_id=1, source_target_pairs={{0,4},{1,5},{2,6},{3,7},{4,0},{5,1},{6,2},{7,3},{8,12},{9,13},{10,... | collective-permute-start | bytes 344072 | tf_op jit(solution)/shard_map/ppermute | solution.py:25
  4.9 8.0 %collective-permute-start.1 = (bf16[1,16,3584]{2,1,0:T(8,128)(2,1)S(1)}, bf16[1,16,3584]{2,1,0:T(8,128)(2,1)S(1)}, u32[]{:S(2)}, u32[]{:S(2)}) collective-permute-start(bf16[1,16,3584]{2,1,0:T(8,128)(2,1)S(1)} %bitcast.55), channel_id=1, source_target_pairs={{0,8},{1,9},{2,10},{3,11},{4,12},{5,13},{6,14},{7,15},{8,0},{9,1},... | collective-permute-start | bytes 344072 | tf_op jit(solution)/shard_map/ppermute | solution.py:25
  7.5 7.5 %collective-permute-start.2 = (bf16[1,16,3584]{2,1,0:T(8,128)(2,1)S(1)}, bf16[1,16,3584]{2,1,0:T(8,128)(2,1)S(1)}, u32[]{:S(2)}, u32[]{:S(2)}) collective-permute-start(bf16[1,16,3584]{2,1,0:T(8,128)(2,1)S(1)} %bitcast.56), channel_id=1, source_target_pairs={{0,2},{1,3},{2,0},{3,1},{4,6},{5,7},{6,4},{7,5},{8,10},{9,11},{10,... | collective-permute-start | bytes 344072 | tf_op jit(solution)/shard_map/ppermute | solution.py:25
  9.0 10.8 %collective-permute-start = (f32[2,224,128]{2,1,0:T(8,128)}, f32[2,224,128]{2,1,0:T(8,128)S(1)}, u32[]{:S(2)}, u32[]{:S(2)}) collective-permute-start(f32[2,224,128]{2,1,0:T(8,128)} %bitcast.48), channel_id=1, source_target_pairs={{0,16},{16,0},{1,17},{17,1},{2,18},{18,2},{3,19},{19,3},{4,20},{20... | collective-permute-start | bytes 688136 | tf_op jit(solution)/shard_map/ppermute | solution.py:25
  12.9 13.1 %copy-start.2 = (bf16[1,128,7168]{2,1,0:T(8,128)(2,1)S(1)}, bf16[1,128,7168]{2,1,0:T(8,128)(2,1)}, u32[]{:S(2)}) copy-start(bf16[1,128,7168]{2,1,0:T(8,128)(2,1)} %param.9) | copy-start | bytes 5505028
  12.9 6.9 %collective-permute-start.5 = (bf16[2,16,3584]{2,1,0:T(8,128)(2,1)S(1)}, bf16[2,16,3584]{2,1,0:T(8,128)(2,1)S(1)}, u32[]{:S(2)}, u32[]{:S(2)}) collective-permute-start(bf16[2,16,3584]{2,1,0:T(8,128)(2,1)S(1)} %pad_maximum_fusion.1), channel_id=1, source_target_pairs={{0,2},{1,3},{2,0},{3,1},{4,6},{5,7},{6,4},{7,5},{8,10},{9,11},{10,... | collective-permute-start | bytes 688136 | tf_op jit(solution)/shard_map/ppermute | solution.py:25
  14.5 4.8 %collective-permute-start.4 = (bf16[1,16,3584]{2,1,0:T(8,128)(2,1)S(1)}, bf16[1,16,3584]{2,1,0:T(8,128)(2,1)S(1)}, u32[]{:S(2)}, u32[]{:S(2)}) collective-permute-start(bf16[1,16,3584]{2,1,0:T(8,128)(2,1)S(1)} %collective-permute-done.1.refs_0_), channel_id=1, source_target_pairs={{0,4},{1,5},{2,6},{3,7},{4,0},{5,1},{6,2},{7,3},{8,12},{9,13},{10,... | collective-permute-start | bytes 344072 | tf_op jit(solution)/shard_map/ppermute | solution.py:25
  19.3 4.8 %collective-permute-start.6 = (bf16[1,16,3584]{2,1,0:T(8,128)(2,1)S(1)}, bf16[1,16,3584]{2,1,0:T(8,128)(2,1)S(1)}, u32[]{:S(2)}, u32[]{:S(2)}) collective-permute-start(bf16[1,16,3584]{2,1,0:T(8,128)(2,1)S(1)} %collective-permute-done.4), channel_id=1, source_target_pairs={{0,2},{1,3},{2,0},{3,1},{4,6},{5,7},{6,4},{7,5},{8,10},{9,11},{10,... | collective-permute-start | bytes 344072 | tf_op jit(solution)/shard_map/ppermute | solution.py:25
  19.8 4.4 %collective-permute-start.7 = (bf16[4,16,3584]{2,1,0:T(8,128)(2,1)S(1)}, bf16[4,16,3584]{2,1,0:T(8,128)(2,1)S(1)}, u32[]{:S(2)}, u32[]{:S(2)}) collective-permute-start(bf16[4,16,3584]{2,1,0:T(8,128)(2,1)S(1)} %pad_maximum_fusion.refs_3_), channel_id=1, source_target_pairs={{0,1},{1,0},{2,3},{3,2},{4,5},{5,4},{6,7},{7,6},{8,9},{9,8},{10,11... | collective-permute-start | bytes 1376264 | tf_op jit(solution)/shard_map/ppermute | solution.py:25
  24.1 1.9 %collective-permute-start.8 = (bf16[4,16,3584]{2,1,0:T(8,128)(2,1)S(1)}, bf16[4,16,3584]{2,1,0:T(8,128)(2,1)S(1)}, u32[]{:S(2)}, u32[]{:S(2)}) collective-permute-start(bf16[4,16,3584]{2,1,0:T(8,128)(2,1)S(1)} %constant_dynamic-update-slice_fusion.refs_4_), channel_id=1, source_target_pairs={{0,1},{1,0},{2,3},{3,2},{4,5},{5,4},{6,7},{7,6},{8,9},{9,8},{10,11... | collective-permute-start | bytes 1376264 | tf_op jit(solution)/shard_map/ppermute | solution.py:25
  26.0 7.3 %copy-start.1 = (f32[1,2,224,128]{3,2,1,0:T(8,128)S(1)}, f32[1,2,224,128]{3,2,1,0:T(8,128)}, u32[]{:S(2)}) copy-start(f32[1,2,224,128]{3,2,1,0:T(8,128)} %param.10) | copy-start | bytes 688132
  26.0 7.3 %copy-start.4 = (f32[224,128]{1,0:T(8,128)S(1)}, f32[224,128]{1,0:T(8,128)}, u32[]{:S(2)}) copy-start(f32[224,128]{1,0:T(8,128)} %anchor.1) | copy-start | bytes 344068
  32.5 2.5 %collective-permute-start.9 = (bf16[8,16,3584]{2,1,0:T(8,128)(2,1)S(1)}, bf16[8,16,3584]{2,1,0:T(8,128)(2,1)S(1)}, u32[]{:S(2)}, u32[]{:S(2)}) collective-permute-start(bf16[8,16,3584]{2,1,0:T(8,128)(2,1)S(1)} %get-tuple-element.15), channel_id=1, source_target_pairs={{0,1},{1,0},{2,3},{3,2},{4,5},{5,4},{6,7},{7,6},{8,9},{9,8},{10,11... | collective-permute-start | bytes 2752520 | tf_op jit(solution)/shard_map/ppermute | solution.py:25
  35.2 17.2 %copy-start.7 = (f32[224,128]{1,0:T(8,128)S(1)}, f32[224,128]{1,0:T(8,128)}, u32[]{:S(2)}) copy-start(f32[224,128]{1,0:T(8,128)} %param.14) | copy-start | bytes 344068
  35.2 5.3 %collective-permute-start.10 = (bf16[16,3584]{1,0:T(8,128)(2,1)S(1)}, bf16[16,3584]{1,0:T(8,128)(2,1)S(1)}, u32[]{:S(2)}, u32[]{:S(2)}) collective-permute-start(bf16[16,3584]{1,0:T(8,128)(2,1)S(1)} %get-tuple-element.24), channel_id=1, source_target_pairs={{0,2},{1,3},{2,0},{3,1},{4,6},{5,7},{6,4},{7,5},{8,10},{9,11},{10,... | collective-permute-start | bytes 344072 | tf_op jit(solution)/shard_map/ppermute | solution.py:25
  35.8 19.5 %copy-start.5 = (f32[1,2,224,128]{3,2,1,0:T(8,128)S(1)}, f32[1,2,224,128]{3,2,1,0:T(8,128)}, u32[]{:S(2)}) copy-start(f32[1,2,224,128]{3,2,1,0:T(8,128)} %param.11) | copy-start | bytes 688132
  35.8 19.5 %copy-start.6 = (f32[1,2,224,128]{3,2,1,0:T(8,128)S(1)}, f32[1,2,224,128]{3,2,1,0:T(8,128)}, u32[]{:S(2)}) copy-start(f32[1,2,224,128]{3,2,1,0:T(8,128)} %param.12) | copy-start | bytes 688132
  40.4 6.8 %collective-permute-start.11 = (bf16[2,16,3584]{2,1,0:T(8,128)(2,1)S(1)}, bf16[2,16,3584]{2,1,0:T(8,128)(2,1)S(1)}, u32[]{:S(2)}, u32[]{:S(2)}) collective-permute-start(bf16[2,16,3584]{2,1,0:T(8,128)(2,1)S(1)} %slice.54), channel_id=1, source_target_pairs={{0,2},{1,3},{2,0},{3,1},{4,6},{5,7},{6,4},{7,5},{8,10},{9,11},{10,... | collective-permute-start | bytes 688136 | tf_op jit(solution)/shard_map/ppermute | solution.py:25
  40.9 6.3 %collective-permute-start.12 = (bf16[16,3584]{1,0:T(8,128)(2,1)S(1)}, bf16[16,3584]{1,0:T(8,128)(2,1)S(1)}, u32[]{:S(2)}, u32[]{:S(2)}) collective-permute-start(bf16[16,3584]{1,0:T(8,128)(2,1)S(1)} %fusion.4), channel_id=1, source_target_pairs={{0,4},{1,5},{2,6},{3,7},{4,0},{5,1},{6,2},{7,3},{8,12},{9,13},{10,... | collective-permute-start | bytes 344072 | tf_op jit(solution)/shard_map/ppermute | solution.py:25
  47.3 5.0 %collective-permute-start.13 = (bf16[16,3584]{1,0:T(8,128)(2,1)S(1)}, bf16[16,3584]{1,0:T(8,128)(2,1)S(1)}, u32[]{:S(2)}, u32[]{:S(2)}) collective-permute-start(bf16[16,3584]{1,0:T(8,128)(2,1)S(1)} %fusion.6), channel_id=1, source_target_pairs={{0,4},{1,5},{2,6},{3,7},{4,0},{5,1},{6,2},{7,3},{8,12},{9,13},{10,... | collective-permute-start | bytes 344072 | tf_op jit(solution)/shard_map/ppermute | solution.py:25
  47.9 7.4 %collective-permute-start.15 = (bf16[16,3584]{1,0:T(8,128)(2,1)S(1)}, bf16[16,3584]{1,0:T(8,128)(2,1)S(1)}, u32[]{:S(2)}, u32[]{:S(2)}) collective-permute-start(bf16[16,3584]{1,0:T(8,128)(2,1)S(1)} %fusion.2), channel_id=1, source_target_pairs={{0,8},{1,9},{2,10},{3,11},{4,12},{5,13},{6,14},{7,15},{8,0},{9,1},... | collective-permute-start | bytes 344072 | tf_op jit(solution)/shard_map/ppermute | solution.py:25
  50.5 4.8 %collective-permute-start.14 = (bf16[16,3584]{1,0:T(8,128)(2,1)S(1)}, bf16[16,3584]{1,0:T(8,128)(2,1)S(1)}, u32[]{:S(2)}, u32[]{:S(2)}) collective-permute-start(bf16[16,3584]{1,0:T(8,128)(2,1)S(1)} %get-tuple-element.20), channel_id=1, source_target_pairs={{0,2},{1,3},{2,0},{3,1},{4,6},{5,7},{6,4},{7,5},{8,10},{9,11},{10,... | collective-permute-start | bytes 344072 | tf_op jit(solution)/shard_map/ppermute | solution.py:25
  53.0 3.3 %copy-start.3 = (f32[224,128]{1,0:T(8,128)}, f32[224,128]{1,0:T(8,128)S(1)}, u32[]{:S(2)}) copy-start(f32[224,128]{1,0:T(8,128)S(1)} %get-tuple-element.21.refs_4_) | copy-start | bytes 344068

commit v7 on v5

--- a/solution.py
+++ b/solution.py
@@ -59,35 +59,35 @@
 
 def output_sets(size):
     tops = list(range(size - 4, -1, -4))
-    even = [k + 2 for k in tops] + tops
-    return [[k + 1 for k in even], even]
-
-
-def reduce_blocks(odd, even, axis):
+    half = len(tops) // 2
+    parts = [[k + 2 for k in tops[:half]], [k + 2 for k in tops[half:]], tops]
+    return [[k + 1 for k in ks] for ks in parts] + parts
+
+
+def reduce_blocks(outs, axis):
     size = lax.axis_size(axis)
     tops = list(range(size - 4, -1, -4))
     half = len(tops) // 2
+    came = swap(outs[0], axis, 1)
+    sums = add_f32(outs[3], came).astype(jnp.bfloat16)
+    near = [swap(sums[at], axis, 2) for at in range(half)]
+    odd, last_odd, sums = lax.optimization_barrier((outs[1], outs[2], sums))
     came = swap(odd, axis, 1)
-    sums = add_f32(even[: len(tops)], came[: len(tops)]).astype(jnp.bfloat16)
-    near = [swap(sums[at], axis, 2) for at in range(half)]
-    rest = swap(sums[half:], axis, 2)
-    came = after(came, sums)
-    kept = add_f32(even[len(tops) :], came[len(tops) :])
-    parts = []
+    sums = add_f32(outs[4], came).astype(jnp.bfloat16)
+    rest = swap(sums, axis, 2)
+    near[0] = after(near[0], sums)
+    kept = add_f32(outs[5], swap(last_odd, axis, 1))
     left = {}
     for at, k in enumerate(tops):
         if at == half:
             rest = after(rest, part)
         arrived = near[at] if at < half else rest[at - half]
+        left[k] = left.get(k, 0.0) + kept[at] + arrived.astype(jnp.float32)
         if k:
-            left[k] = left.get(k, 0.0) + kept[at] + arrived.astype(jnp.float32)
             part = left[k].astype(jnp.bfloat16)
-            moved = swap(part, axis, k & -k)
-            if k & (k - 1):
-                left[k & (k - 1)] = left.get(k & (k - 1), 0.0) + moved.astype(jnp.float32)
-            else:
-                parts.append(moved)
-    return [kept[-1], rest[-1]] + parts
+            moved = swap(part, axis, k & -k).astype(jnp.float32)
+            left[k & (k - 1)] = left.get(k & (k - 1), 0.0) + moved
+    return left[0]
 
 
 def dot_nt(left, right):
@@ -353,7 +353,7 @@
 
     sets = output_sets(groups)
     if piece == ROWS:
-        odd, even = adapter_grads(tokens, upstream, squares, gathered, units, sets)
+        outs = adapter_grads(tokens, upstream, squares, gathered, units, sets)
     else:
         merged = ROWS // piece
         blocks = {k: array[place] for ks, array in gathered for place, k in enumerate(ks)}
@@ -364,20 +364,20 @@
         (both,) = adapter_grads(tokens, upstream, squares, [(every, blocks)], units, [every])
         both = both.reshape(groups // merged, 2, merged, piece, model_width // 2)
         both = both.transpose(0, 2, 1, 3, 4).reshape(groups, 2 * piece, model_width // 2)
-        odd, even = [jnp.stack([both[k] for k in ks]) for ks in sets]
-    parts = reduce_blocks(odd, even, "fsdp")
+        outs = [jnp.stack([both[k] for k in ks]) for ks in sets]
+    summed = reduce_blocks(outs, "fsdp")
 
     total = fragment_delta(fragment, params, other, anchor)
     step = 2
     while step < replicas:
         total = total + swap(total, "rep", step)
         step *= 2
-    mean_delta = after(total, parts[1]) / replicas
+    mean_delta = total / replicas
     new_velocity = outer_beta * momentum + mean_delta
     new_global = anchor - outer_rate * (mean_delta + outer_beta * new_velocity)
     scales = (model_width ** (-0.5), hidden ** (-0.5))
     merged = adam_step(
-        fragment, params, first_moment[0], second_moment[0], new_global, parts, tokens.shape[0] * groups, scales
+        fragment, params, first_moment[0], second_moment[0], new_global, [summed], tokens.shape[0] * groups, scales
     )
     return (merged[None], new_global, new_velocity)
 

time: 55.1 us -> 54 us (0.980)
  waiting for transfers between devices: 25.7 us -> 22.5 us
  starting transfers between devices: 17.5 us -> 19.6 us
    ppermute x16 -> x18, waiting for transfers between devices: 25.7 us -> 22.5 us  [swap(): return lax.ppermute(value, axis, [(i, i ^ mask) for i in range(size)])]
    ppermute x16 -> x18, starting transfers between devices: 17.5 us -> 19.6 us  [swap(): return lax.ppermute(value, axis, [(i, i ^ mask) for i in range(size)])]
  transfers between devices with their start and end apart: 16 -> 18, of which waited for: 10 -> 10; matrix products, arithmetic and copies ran while one was open for 2% -> 2% of each run, Pallas kernels for 1% -> 1%
where the time goes in v7:
time: 54 us; the launch traced here: 53.9 us
  waiting for transfers between devices  22.5 us (42%)
  starting transfers between devices  19.6 us (36%)
  Pallas kernels  7.93 us (15%)
  other arithmetic  2.2 us (4%)
  between operations  1.5 us (3%)
    ppermute x18, waiting for transfers between devices, swap(): return lax.ppermute(value, axis, [(i, i ^ mask) for i in range(size)])  22.5 us
    ppermute x18, starting transfers between devices, swap(): return lax.ppermute(value, axis, [(i, i ^ mask) for i in range(size)])  19.6 us
    pallas_call x1, Pallas kernels, adapter_grads(): pl.pallas_call(functools.partial(adapter_kernel, len(arrays), sources, pl...  6.47 us
    convert_element_type x1, other arithmetic, shards(): compact = params.astype(jnp.bfloat16).reshape(piece, 2, model_width // 2)  1.09 us
  transfers between devices with their start and end apart: 18, of which 10 were waited for; matrix products, arithmetic and copies ran while one was open for 2% of the time, Pallas kernels for 1%

profile of v7, /device:TPU:0, one launch (start us, length us, event | category | flops | bytes accessed | tf_op | source)
XLA Modules:
  0.0 53.9 jit_solution(17993749422474065136)
XLA Ops:
  0.6 1.1 %convert_element_type.68 = bf16[1,2,224,128]{3,2,1,0:T(8,128)(2,1)S(1)} convert(f32[1,2,224,128]{3,2,1,0:T(8,128)} %param.10) | non-fusion elementwise | flops 57344 | bytes 344064 | tf_op jit(solution)/shard_map/convert_element_type | solution.py:342
  1.8 4.1 %collective-permute-start.1 = (bf16[1,16,3584]{2,1,0:T(8,128)(2,1)S(1)}, bf16[1,16,3584]{2,1,0:T(8,128)(2,1)S(1)}, u32[]{:S(2)}, u32[]{:S(2)}) collective-permute-start(bf16[1,16,3584]{2,1,0:T(8,128)(2,1)S(1)} %bitcast.50), channel_id=1, source_target_pairs={{0,8},{1,9},{2,10},{3,11},{4,12},{5,13},{6,14},{7,15},{8,0},{9,1},... | collective-permute-start | bytes 344072 | tf_op jit(solution)/shard_map/ppermute | solution.py:25
  5.9 1.6 %collective-permute-start.3 = (bf16[1,16,3584]{2,1,0:T(8,128)(2,1)S(1)}, bf16[1,16,3584]{2,1,0:T(8,128)(2,1)S(1)}, u32[]{:S(2)}, u32[]{:S(2)}) collective-permute-start(bf16[1,16,3584]{2,1,0:T(8,128)(2,1)S(1)} %bitcast.51), channel_id=1, source_target_pairs={{0,4},{1,5},{2,6},{3,7},{4,0},{5,1},{6,2},{7,3},{8,12},{9,13},{10,... | collective-permute-start | bytes 344072 | tf_op jit(solution)/shard_map/ppermute | solution.py:25
  7.5 1.5 %collective-permute-start.2 = (bf16[1,16,3584]{2,1,0:T(8,128)(2,1)S(1)}, bf16[1,16,3584]{2,1,0:T(8,128)(2,1)S(1)}, u32[]{:S(2)}, u32[]{:S(2)}) collective-permute-start(bf16[1,16,3584]{2,1,0:T(8,128)(2,1)S(1)} %bitcast.52), channel_id=1, source_target_pairs={{0,2},{1,3},{2,0},{3,1},{4,6},{5,7},{6,4},{7,5},{8,10},{9,11},{10,... | collective-permute-start | bytes 344072 | tf_op jit(solution)/shard_map/ppermute | solution.py:25
  9.0 1.5 %collective-permute-start = (f32[2,224,128]{2,1,0:T(8,128)}, f32[2,224,128]{2,1,0:T(8,128)S(1)}, u32[]{:S(2)}, u32[]{:S(2)}) collective-permute-start(f32[2,224,128]{2,1,0:T(8,128)} %bitcast.44), channel_id=1, source_target_pairs={{0,16},{16,0},{1,17},{17,1},{2,18},{18,2},{3,19},{19,3},{4,20},{20... | collective-permute-start | bytes 688136 | tf_op jit(solution)/shard_map/ppermute | solution.py:25
  10.5 1.1 %collective-permute-done.1.refs_0_ = bf16[1,16,3584]{2,1,0:T(8,128)(2,1)S(1)} collective-permute-done((bf16[1,16,3584]{2,1,0:T(8,128)(2,1)S(1)}, bf16[1,16,3584]{2,1,0:T(8,128)(2,1)S(1)}, u32[]{:S(2)}, u32[]{:S(2)}) %collective-permute-start.1) | collective-permute-done | bytes 114720 | tf_op jit(solution)/shard_map/ppermute | solution.py:25
  11.6 0.2 collective-permute-done.3
  11.9 0.0 copy-start.2
  11.9 1.6 %collective-permute-start.5 = (bf16[2,16,3584]{2,1,0:T(8,128)(2,1)S(1)}, bf16[2,16,3584]{2,1,0:T(8,128)(2,1)S(1)}, u32[]{:S(2)}, u32[]{:S(2)}) collective-permute-start(bf16[2,16,3584]{2,1,0:T(8,128)(2,1)S(1)} %pad_maximum_fusion.1), channel_id=1, source_target_pairs={{0,2},{1,3},{2,0},{3,1},{4,6},{5,7},{6,4},{7,5},{8,10},{9,11},{10,... | collective-permute-start | bytes 688136 | tf_op jit(solution)/shard_map/ppermute | solution.py:25
  13.5 1.4 %collective-permute-start.4 = (bf16[1,16,3584]{2,1,0:T(8,128)(2,1)S(1)}, bf16[1,16,3584]{2,1,0:T(8,128)(2,1)S(1)}, u32[]{:S(2)}, u32[]{:S(2)}) collective-permute-start(bf16[1,16,3584]{2,1,0:T(8,128)(2,1)S(1)} %collective-permute-done.1.refs_0_), channel_id=1, source_target_pairs={{0,4},{1,5},{2,6},{3,7},{4,0},{5,1},{6,2},{7,3},{8,12},{9,13},{10,... | collective-permute-start | bytes 344072 | tf_op jit(solution)/shard_map/ppermute | solution.py:25
  14.9 0.0 collective-permute-done.2
  14.9 0.1 pad_maximum_fusion.refs_3_
  14.9 0.5 shard_map.104.refs_2_
  15.4 2.9 %collective-permute-done.4 = bf16[1,16,3584]{2,1,0:T(8,128)(2,1)S(1)} collective-permute-done((bf16[1,16,3584]{2,1,0:T(8,128)(2,1)S(1)}, bf16[1,16,3584]{2,1,0:T(8,128)(2,1)S(1)}, u32[]{:S(2)}, u32[]{:S(2)}) %collective-permute-start.4) | collective-permute-done | bytes 114720 | tf_op jit(solution)/shard_map/ppermute | solution.py:25
  18.3 0.5 collective-permute-start.6
  18.8 0.0 collective-permute-done.other
  18.8 0.0 collective-permute-start.7
  18.8 0.0 collective-permute-done.5
  18.8 4.3 %collective-permute-done.6 = bf16[1,16,3584]{2,1,0:T(8,128)(2,1)S(1)} collective-permute-done((bf16[1,16,3584]{2,1,0:T(8,128)(2,1)S(1)}, bf16[1,16,3584]{2,1,0:T(8,128)(2,1)S(1)}, u32[]{:S(2)}, u32[]{:S(2)}) %collective-permute-start.6) | collective-permute-done | bytes 114720 | tf_op jit(solution)/shard_map/ppermute | solution.py:25
  23.1 0.1 collective-permute-start.8
  23.2 1.8 %collective-permute-done.8.refs_6_ = bf16[4,16,3584]{2,1,0:T(8,128)(2,1)S(1)} collective-permute-done((bf16[4,16,3584]{2,1,0:T(8,128)(2,1)S(1)}, bf16[4,16,3584]{2,1,0:T(8,128)(2,1)S(1)}, u32[]{:S(2)}, u32[]{:S(2)}) %collective-permute-start.8) | collective-permute-done | bytes 458784 | tf_op jit(solution)/shard_map/ppermute | solution.py:25
  25.0 6.5 %shard_map.105 = (bf16[2,16,3584]{2,1,0:T(8,128)(2,1)S(1)}, bf16[2,16,3584]{2,1,0:T(8,128)(2,1)S(1)}, bf16[4,16,3584]{2,1,0:T(8,128)(2,1)S(1)}, bf16[2,16,3584]{...) custom-call(bf16[128,7168]{1,0:T(8,128)(2,1)S(1)} %bitcast.43, ...), custom_call_target="tpu_custom_call" | custom-call | tf_op jit(solution)/shard_map/pallas_call | solution.py:248
  31.4 0.2 collective-permute-start.9
  31.7 1.3 %collective-permute-done.9 = bf16[2,16,3584]{2,1,0:T(8,128)(2,1)S(1)} collective-permute-done((bf16[2,16,3584]{2,1,0:T(8,128)(2,1)S(1)}, bf16[2,16,3584]{2,1,0:T(8,128)(2,1)S(1)}, u32[]{:S(2)}, u32[]{:S(2)}) %collective-permute-start.9) | collective-permute-done | bytes 229408 | tf_op jit(solution)/shard_map/ppermute | solution.py:25
  33.0 0.1 add_convert_fusion.1
  33.1 0.0 copy-start.1
  33.1 0.0 copy-start.4
  33.1 0.2 collective-permute-start.12
  33.3 0.5 %collective-permute-start.11 = (bf16[16,3584]{1,0:T(8,128)(2,1)S(1)}, bf16[16,3584]{1,0:T(8,128)(2,1)S(1)}, u32[]{:S(2)}, u32[]{:S(2)}) collective-permute-start(bf16[16,3584]{1,0:T(8,128)(2,1)S(1)} %get-tuple-element.29), channel_id=1, source_target_pairs={{0,2},{1,3},{2,0},{3,1},{4,6},{5,7},{6,4},{7,5},{8,10},{9,11},{10,... | collective-permute-start | bytes 344072 | tf_op jit(solution)/shard_map/ppermute | solution.py:25
  33.8 0.1 collective-permute-start.10
  33.9 1.6 %collective-permute-start.14 = (bf16[16,3584]{1,0:T(8,128)(2,1)S(1)}, bf16[16,3584]{1,0:T(8,128)(2,1)S(1)}, u32[]{:S(2)}, u32[]{:S(2)}) collective-permute-start(bf16[16,3584]{1,0:T(8,128)(2,1)S(1)} %get-tuple-element.30), channel_id=1, source_target_pairs={{0,2},{1,3},{2,0},{3,1},{4,6},{5,7},{6,4},{7,5},{8,10},{9,11},{10,... | collective-permute-start | bytes 344072 | tf_op jit(solution)/shard_map/ppermute | solution.py:25
  35.5 0.1 add_convert_fusion
  35.6 3.8 %collective-permute-done.11 = bf16[16,3584]{1,0:T(8,128)(2,1)S(1)} collective-permute-done((bf16[16,3584]{1,0:T(8,128)(2,1)S(1)}, bf16[16,3584]{1,0:T(8,128)(2,1)S(1)}, u32[]{:S(2)}, u32[]{:S(2)}) %collective-permute-start.11) | collective-permute-done | bytes 114720 | tf_op jit(solution)/shard_map/ppermute | solution.py:25
  39.4 0.1 convert_add_fusion
  39.5 0.0 copy-start.5
  39.5 0.0 copy-start.6
  39.5 1.4 %collective-permute-start.13 = (bf16[16,3584]{1,0:T(8,128)(2,1)S(1)}, bf16[16,3584]{1,0:T(8,128)(2,1)S(1)}, u32[]{:S(2)}, u32[]{:S(2)}) collective-permute-start(bf16[16,3584]{1,0:T(8,128)(2,1)S(1)} %fusion.7), channel_id=1, source_target_pairs={{0,4},{1,5},{2,6},{3,7},{4,0},{5,1},{6,2},{7,3},{8,12},{9,13},{10,... | collective-permute-start | bytes 344072 | tf_op jit(solution)/shard_map/ppermute | solution.py:25
  41.7 0.6 %collective-permute-start.16 = (bf16[2,16,3584]{2,1,0:T(8,128)(2,1)S(1)}, bf16[2,16,3584]{2,1,0:T(8,128)(2,1)S(1)}, u32[]{:S(2)}, u32[]{:S(2)}) collective-permute-start(bf16[2,16,3584]{2,1,0:T(8,128)(2,1)S(1)} %add_convert_fusion), channel_id=1, source_target_pairs={{0,2},{1,3},{2,0},{3,1},{4,6},{5,7},{6,4},{7,5},{8,10},{9,11},{10,... | collective-permute-start | bytes 688136 | tf_op jit(solution)/shard_map/ppermute | solution.py:25
  42.2 0.0 collective-permute-done.14
  42.2 2.1 %collective-permute-done.13 = bf16[16,3584]{1,0:T(8,128)(2,1)S(1)} collective-permute-done((bf16[16,3584]{1,0:T(8,128)(2,1)S(1)}, bf16[16,3584]{1,0:T(8,128)(2,1)S(1)}, u32[]{:S(2)}, u32[]{:S(2)}) %collective-permute-start.13) | collective-permute-done | bytes 114720 | tf_op jit(solution)/shard_map/ppermute | solution.py:25
  44.4 2.1 %collective-permute-start.15 = (bf16[16,3584]{1,0:T(8,128)(2,1)S(1)}, bf16[16,3584]{1,0:T(8,128)(2,1)S(1)}, u32[]{:S(2)}, u32[]{:S(2)}) collective-permute-start(bf16[16,3584]{1,0:T(8,128)(2,1)S(1)} %fusion.5), channel_id=1, source_target_pairs={{0,8},{1,9},{2,10},{3,11},{4,12},{5,13},{6,14},{7,15},{8,0},{9,1},... | collective-permute-start | bytes 344072 | tf_op jit(solution)/shard_map/ppermute | solution.py:25
  46.5 1.5 %collective-permute-done.16 = bf16[2,16,3584]{2,1,0:T(8,128)(2,1)S(1)} collective-permute-done((bf16[2,16,3584]{2,1,0:T(8,128)(2,1)S(1)}, bf16[2,16,3584]{2,1,0:T(8,128)(2,1)S(1)}, u32[]{:S(2)}, u32[]{:S(2)}) %collective-permute-start.16) | collective-permute-done | bytes 229408 | tf_op jit(solution)/shard_map/ppermute | solution.py:25
  48.0 0.7 %collective-permute-start.17 = (bf16[16,3584]{1,0:T(8,128)(2,1)S(1)}, bf16[16,3584]{1,0:T(8,128)(2,1)S(1)}, u32[]{:S(2)}, u32[]{:S(2)}) collective-permute-start(bf16[16,3584]{1,0:T(8,128)(2,1)S(1)} %fusion.8), channel_id=1, source_target_pairs={{0,4},{1,5},{2,6},{3,7},{4,0},{5,1},{6,2},{7,3},{8,12},{9,13},{10,... | collective-permute-start | bytes 344072 | tf_op jit(solution)/shard_map/ppermute | solution.py:25
  48.7 0.7 %multiply_subtract_fusion = (f32[224,128]{1,0:T(8,128)S(1)}, f32[224,128]{1,0:T(8,128)}) fusion(f32[224,128]{1,0:T(8,128)S(1)} %copy-done.4, f32[224,128]{1,0:T(8,128)S(1)} %shard_map.103, f32[224,128]{1,0:T(8,128)S(1)} %copy-done.7), kind=kLoop, calls=%fused_computation.21 | loop fusion | flops 200704 | bytes 573440 | tf_op jit(solution)/shard_map/sub | solution.py:377
  49.4 3.4 %collective-permute-done.17 = bf16[16,3584]{1,0:T(8,128)(2,1)S(1)} collective-permute-done((bf16[16,3584]{1,0:T(8,128)(2,1)S(1)}, bf16[16,3584]{1,0:T(8,128)(2,1)S(1)}, u32[]{:S(2)}, u32[]{:S(2)}) %collective-permute-start.17) | collective-permute-done | bytes 114720 | tf_op jit(solution)/shard_map/ppermute | solution.py:25
  52.8 0.0 collective-permute-done.15
  52.8 0.1 fusion.1.refs_5_
  52.9 1.0 %shard_map.106 = f32[2,224,128]{2,1,0:T(8,128)} custom-call(s32[1]{0:T(128)S(6)} %copy.16.fragment.refs_0_, f32[2,224,128]{2,1,0:T(8,128)S(1)} %bitcast.46, f32[2,224,128]{2,1,0:T(8,128)S(1)} %bitcast.48, f32[2,224,128]{2,1,0:T(8,128)S(1)} %bitcast.49, f32[224,128]{1,0:T(8,128)S(1)} %get-tuple-element.27.refs_4_, f32[16,3584]{1,0:T(8,128)S(1)} %fusion.1.refs_5_), custom_call_target="tpu_custom_call" | custom-call | tf_op jit(solution)/shard_map/pallas_call | solution.py:317
  (25 shorter events, 0.3 us)
Async XLA Ops:
  0.6 14.3 %copy-start = (bf16[1,128,7168]{2,1,0:T(8,128)(2,1)S(1)}, bf16[1,128,7168]{2,1,0:T(8,128)(2,1)}, u32[]{:S(2)}) copy-start(bf16[1,128,7168]{2,1,0:T(8,128)(2,1)} %param.8) | copy-start | bytes 5505028
  1.8 9.8 %collective-permute-start.1 = (bf16[1,16,3584]{2,1,0:T(8,128)(2,1)S(1)}, bf16[1,16,3584]{2,1,0:T(8,128)(2,1)S(1)}, u32[]{:S(2)}, u32[]{:S(2)}) collective-permute-start(bf16[1,16,3584]{2,1,0:T(8,128)(2,1)S(1)} %bitcast.50), channel_id=1, source_target_pairs={{0,8},{1,9},{2,10},{3,11},{4,12},{5,13},{6,14},{7,15},{8,0},{9,1},... | collective-permute-start | bytes 344072 | tf_op jit(solution)/shard_map/ppermute | solution.py:25
  5.9 5.9 %collective-permute-start.3 = (bf16[1,16,3584]{2,1,0:T(8,128)(2,1)S(1)}, bf16[1,16,3584]{2,1,0:T(8,128)(2,1)S(1)}, u32[]{:S(2)}, u32[]{:S(2)}) collective-permute-start(bf16[1,16,3584]{2,1,0:T(8,128)(2,1)S(1)} %bitcast.51), channel_id=1, source_target_pairs={{0,4},{1,5},{2,6},{3,7},{4,0},{5,1},{6,2},{7,3},{8,12},{9,13},{10,... | collective-permute-start | bytes 344072 | tf_op jit(solution)/shard_map/ppermute | solution.py:25
  7.5 7.4 %collective-permute-start.2 = (bf16[1,16,3584]{2,1,0:T(8,128)(2,1)S(1)}, bf16[1,16,3584]{2,1,0:T(8,128)(2,1)S(1)}, u32[]{:S(2)}, u32[]{:S(2)}) collective-permute-start(bf16[1,16,3584]{2,1,0:T(8,128)(2,1)S(1)} %bitcast.52), channel_id=1, source_target_pairs={{0,2},{1,3},{2,0},{3,1},{4,6},{5,7},{6,4},{7,5},{8,10},{9,11},{10,... | collective-permute-start | bytes 344072 | tf_op jit(solution)/shard_map/ppermute | solution.py:25
  9.0 9.8 %collective-permute-start = (f32[2,224,128]{2,1,0:T(8,128)}, f32[2,224,128]{2,1,0:T(8,128)S(1)}, u32[]{:S(2)}, u32[]{:S(2)}) collective-permute-start(f32[2,224,128]{2,1,0:T(8,128)} %bitcast.44), channel_id=1, source_target_pairs={{0,16},{16,0},{1,17},{17,1},{2,18},{18,2},{3,19},{19,3},{4,20},{20... | collective-permute-start | bytes 688136 | tf_op jit(solution)/shard_map/ppermute | solution.py:25
  11.9 13.1 %copy-start.2 = (bf16[1,128,7168]{2,1,0:T(8,128)(2,1)S(1)}, bf16[1,128,7168]{2,1,0:T(8,128)(2,1)}, u32[]{:S(2)}) copy-start(bf16[1,128,7168]{2,1,0:T(8,128)(2,1)} %param.9) | copy-start | bytes 5505028
  11.9 6.9 %collective-permute-start.5 = (bf16[2,16,3584]{2,1,0:T(8,128)(2,1)S(1)}, bf16[2,16,3584]{2,1,0:T(8,128)(2,1)S(1)}, u32[]{:S(2)}, u32[]{:S(2)}) collective-permute-start(bf16[2,16,3584]{2,1,0:T(8,128)(2,1)S(1)} %pad_maximum_fusion.1), channel_id=1, source_target_pairs={{0,2},{1,3},{2,0},{3,1},{4,6},{5,7},{6,4},{7,5},{8,10},{9,11},{10,... | collective-permute-start | bytes 688136 | tf_op jit(solution)/shard_map/ppermute | solution.py:25
  13.5 4.8 %collective-permute-start.4 = (bf16[1,16,3584]{2,1,0:T(8,128)(2,1)S(1)}, bf16[1,16,3584]{2,1,0:T(8,128)(2,1)S(1)}, u32[]{:S(2)}, u32[]{:S(2)}) collective-permute-start(bf16[1,16,3584]{2,1,0:T(8,128)(2,1)S(1)} %collective-permute-done.1.refs_0_), channel_id=1, source_target_pairs={{0,4},{1,5},{2,6},{3,7},{4,0},{5,1},{6,2},{7,3},{8,12},{9,13},{10,... | collective-permute-start | bytes 344072 | tf_op jit(solution)/shard_map/ppermute | solution.py:25
  18.3 4.8 %collective-permute-start.6 = (bf16[1,16,3584]{2,1,0:T(8,128)(2,1)S(1)}, bf16[1,16,3584]{2,1,0:T(8,128)(2,1)S(1)}, u32[]{:S(2)}, u32[]{:S(2)}) collective-permute-start(bf16[1,16,3584]{2,1,0:T(8,128)(2,1)S(1)} %collective-permute-done.4), channel_id=1, source_target_pairs={{0,2},{1,3},{2,0},{3,1},{4,6},{5,7},{6,4},{7,5},{8,10},{9,11},{10,... | collective-permute-start | bytes 344072 | tf_op jit(solution)/shard_map/ppermute | solution.py:25
  18.8 4.4 %collective-permute-start.7 = (bf16[4,16,3584]{2,1,0:T(8,128)(2,1)S(1)}, bf16[4,16,3584]{2,1,0:T(8,128)(2,1)S(1)}, u32[]{:S(2)}, u32[]{:S(2)}) collective-permute-start(bf16[4,16,3584]{2,1,0:T(8,128)(2,1)S(1)} %pad_maximum_fusion.refs_3_), channel_id=1, source_target_pairs={{0,1},{1,0},{2,3},{3,2},{4,5},{5,4},{6,7},{7,6},{8,9},{9,8},{10,11... | collective-permute-start | bytes 1376264 | tf_op jit(solution)/shard_map/ppermute | solution.py:25
  23.1 1.9 %collective-permute-start.8 = (bf16[4,16,3584]{2,1,0:T(8,128)(2,1)S(1)}, bf16[4,16,3584]{2,1,0:T(8,128)(2,1)S(1)}, u32[]{:S(2)}, u32[]{:S(2)}) collective-permute-start(bf16[4,16,3584]{2,1,0:T(8,128)(2,1)S(1)} %constant_dynamic-update-slice_fusion.refs_4_), channel_id=1, source_target_pairs={{0,1},{1,0},{2,3},{3,2},{4,5},{5,4},{6,7},{7,6},{8,9},{9,8},{10,11... | collective-permute-start | bytes 1376264 | tf_op jit(solution)/shard_map/ppermute | solution.py:25
  31.4 1.6 %collective-permute-start.9 = (bf16[2,16,3584]{2,1,0:T(8,128)(2,1)S(1)}, bf16[2,16,3584]{2,1,0:T(8,128)(2,1)S(1)}, u32[]{:S(2)}, u32[]{:S(2)}) collective-permute-start(bf16[2,16,3584]{2,1,0:T(8,128)(2,1)S(1)} %get-tuple-element.21), channel_id=1, source_target_pairs={{0,1},{1,0},{2,3},{3,2},{4,5},{5,4},{6,7},{7,6},{8,9},{9,8},{10,11... | collective-permute-start | bytes 688136 | tf_op jit(solution)/shard_map/ppermute | solution.py:25
  33.1 8.5 %copy-start.1 = (f32[1,2,224,128]{3,2,1,0:T(8,128)S(1)}, f32[1,2,224,128]{3,2,1,0:T(8,128)}, u32[]{:S(2)}) copy-start(f32[1,2,224,128]{3,2,1,0:T(8,128)} %param.10) | copy-start | bytes 688132
  33.1 8.5 %copy-start.4 = (f32[224,128]{1,0:T(8,128)S(1)}, f32[224,128]{1,0:T(8,128)}, u32[]{:S(2)}) copy-start(f32[224,128]{1,0:T(8,128)} %anchor.1) | copy-start | bytes 344068
  33.1 2.4 %collective-permute-start.12 = (bf16[2,16,3584]{2,1,0:T(8,128)(2,1)S(1)}, bf16[2,16,3584]{2,1,0:T(8,128)(2,1)S(1)}, u32[]{:S(2)}, u32[]{:S(2)}) collective-permute-start(bf16[2,16,3584]{2,1,0:T(8,128)(2,1)S(1)} %get-tuple-element.24), channel_id=1, source_target_pairs={{0,1},{1,0},{2,3},{3,2},{4,5},{5,4},{6,7},{7,6},{8,9},{9,8},{10,11... | collective-permute-start | bytes 688136 | tf_op jit(solution)/shard_map/ppermute | solution.py:25
  33.3 6.0 %collective-permute-start.11 = (bf16[16,3584]{1,0:T(8,128)(2,1)S(1)}, bf16[16,3584]{1,0:T(8,128)(2,1)S(1)}, u32[]{:S(2)}, u32[]{:S(2)}) collective-permute-start(bf16[16,3584]{1,0:T(8,128)(2,1)S(1)} %get-tuple-element.29), channel_id=1, source_target_pairs={{0,2},{1,3},{2,0},{3,1},{4,6},{5,7},{6,4},{7,5},{8,10},{9,11},{10,... | collective-permute-start | bytes 344072 | tf_op jit(solution)/shard_map/ppermute | solution.py:25
  33.8 5.5 %collective-permute-start.10 = (bf16[4,16,3584]{2,1,0:T(8,128)(2,1)S(1)}, bf16[4,16,3584]{2,1,0:T(8,128)(2,1)S(1)}, u32[]{:S(2)}, u32[]{:S(2)}) collective-permute-start(bf16[4,16,3584]{2,1,0:T(8,128)(2,1)S(1)} %get-tuple-element.22), channel_id=1, source_target_pairs={{0,1},{1,0},{2,3},{3,2},{4,5},{5,4},{6,7},{7,6},{8,9},{9,8},{10,11... | collective-permute-start | bytes 1376264 | tf_op jit(solution)/shard_map/ppermute | solution.py:25
  33.9 8.3 %collective-permute-start.14 = (bf16[16,3584]{1,0:T(8,128)(2,1)S(1)}, bf16[16,3584]{1,0:T(8,128)(2,1)S(1)}, u32[]{:S(2)}, u32[]{:S(2)}) collective-permute-start(bf16[16,3584]{1,0:T(8,128)(2,1)S(1)} %get-tuple-element.30), channel_id=1, source_target_pairs={{0,2},{1,3},{2,0},{3,1},{4,6},{5,7},{6,4},{7,5},{8,10},{9,11},{10,... | collective-permute-start | bytes 344072 | tf_op jit(solution)/shard_map/ppermute | solution.py:25
  39.4 9.3 %copy-start.7 = (f32[224,128]{1,0:T(8,128)S(1)}, f32[224,128]{1,0:T(8,128)}, u32[]{:S(2)}) copy-start(f32[224,128]{1,0:T(8,128)} %param.14) | copy-start | bytes 344068
  39.5 13.4 %copy-start.5 = (f32[1,2,224,128]{3,2,1,0:T(8,128)S(1)}, f32[1,2,224,128]{3,2,1,0:T(8,128)}, u32[]{:S(2)}) copy-start(f32[1,2,224,128]{3,2,1,0:T(8,128)} %param.11) | copy-start | bytes 688132
  39.5 13.4 %copy-start.6 = (f32[1,2,224,128]{3,2,1,0:T(8,128)S(1)}, f32[1,2,224,128]{3,2,1,0:T(8,128)}, u32[]{:S(2)}) copy-start(f32[1,2,224,128]{3,2,1,0:T(8,128)} %param.12) | copy-start | bytes 688132
  39.5 4.9 %collective-permute-start.13 = (bf16[16,3584]{1,0:T(8,128)(2,1)S(1)}, bf16[16,3584]{1,0:T(8,128)(2,1)S(1)}, u32[]{:S(2)}, u32[]{:S(2)}) collective-permute-start(bf16[16,3584]{1,0:T(8,128)(2,1)S(1)} %fusion.7), channel_id=1, source_target_pairs={{0,4},{1,5},{2,6},{3,7},{4,0},{5,1},{6,2},{7,3},{8,12},{9,13},{10,... | collective-permute-start | bytes 344072 | tf_op jit(solution)/shard_map/ppermute | solution.py:25
  41.7 6.3 %collective-permute-start.16 = (bf16[2,16,3584]{2,1,0:T(8,128)(2,1)S(1)}, bf16[2,16,3584]{2,1,0:T(8,128)(2,1)S(1)}, u32[]{:S(2)}, u32[]{:S(2)}) collective-permute-start(bf16[2,16,3584]{2,1,0:T(8,128)(2,1)S(1)} %add_convert_fusion), channel_id=1, source_target_pairs={{0,2},{1,3},{2,0},{3,1},{4,6},{5,7},{6,4},{7,5},{8,10},{9,11},{10,... | collective-permute-start | bytes 688136 | tf_op jit(solution)/shard_map/ppermute | solution.py:25
  44.4 8.4 %collective-permute-start.15 = (bf16[16,3584]{1,0:T(8,128)(2,1)S(1)}, bf16[16,3584]{1,0:T(8,128)(2,1)S(1)}, u32[]{:S(2)}, u32[]{:S(2)}) collective-permute-start(bf16[16,3584]{1,0:T(8,128)(2,1)S(1)} %fusion.5), channel_id=1, source_target_pairs={{0,8},{1,9},{2,10},{3,11},{4,12},{5,13},{6,14},{7,15},{8,0},{9,1},... | collective-permute-start | bytes 344072 | tf_op jit(solution)/shard_map/ppermute | solution.py:25
  48.0 4.9 %collective-permute-start.17 = (bf16[16,3584]{1,0:T(8,128)(2,1)S(1)}, bf16[16,3584]{1,0:T(8,128)(2,1)S(1)}, u32[]{:S(2)}, u32[]{:S(2)}) collective-permute-start(bf16[16,3584]{1,0:T(8,128)(2,1)S(1)} %fusion.8), channel_id=1, source_target_pairs={{0,4},{1,5},{2,6},{3,7},{4,0},{5,1},{6,2},{7,3},{8,12},{9,13},{10,... | collective-permute-start | bytes 344072 | tf_op jit(solution)/shard_map/ppermute | solution.py:25
  49.4 4.5 %copy-start.3 = (f32[224,128]{1,0:T(8,128)}, f32[224,128]{1,0:T(8,128)S(1)}, u32[]{:S(2)}) copy-start(f32[224,128]{1,0:T(8,128)S(1)} %get-tuple-element.27.refs_4_) | copy-start | bytes 344068

commit v8 on v7

--- a/solution.py
+++ b/solution.py
@@ -87,7 +87,7 @@
             part = left[k].astype(jnp.bfloat16)
             moved = swap(part, axis, k & -k).astype(jnp.float32)
             left[k & (k - 1)] = left.get(k & (k - 1), 0.0) + moved
-    return left[0]
+    return left[0], rest
 
 
 def dot_nt(left, right):
@@ -365,9 +365,9 @@
         both = both.reshape(groups // merged, 2, merged, piece, model_width // 2)
         both = both.transpose(0, 2, 1, 3, 4).reshape(groups, 2 * piece, model_width // 2)
         outs = [jnp.stack([both[k] for k in ks]) for ks in sets]
-    summed = reduce_blocks(outs, "fsdp")
-
-    total = fragment_delta(fragment, params, other, anchor)
+    summed, late = reduce_blocks(outs, "fsdp")
+
+    total = fragment_delta(fragment, params, after(other, late), anchor)
     step = 2
     while step < replicas:
         total = total + swap(total, "rep", step)

time: 54 us -> 53.9 us (level)
  no operation moved by 1% of the time
where the time goes in v8:
time: 53.9 us; the launch traced here: 53.8 us
  waiting for transfers between devices  22.4 us (42%)
  starting transfers between devices  19.6 us (36%)
  Pallas kernels  7.92 us (15%)
  other arithmetic  2.2 us (4%)
  between operations  1.49 us (3%)
    ppermute x18, waiting for transfers between devices, swap(): return lax.ppermute(value, axis, [(i, i ^ mask) for i in range(size)])  22.4 us
    ppermute x18, starting transfers between devices, swap(): return lax.ppermute(value, axis, [(i, i ^ mask) for i in range(size)])  19.6 us
    pallas_call x1, Pallas kernels, adapter_grads(): pl.pallas_call(functools.partial(adapter_kernel, len(arrays), sources, pl...  6.47 us
    convert_element_type x1, other arithmetic, shards(): compact = params.astype(jnp.bfloat16).reshape(piece, 2, model_width // 2)  1.09 us
  transfers between devices with their start and end apart: 18, of which 10 were waited for; matrix products, arithmetic and copies ran while one was open for 2% of the time, Pallas kernels for 1%

profile of v8, /device:TPU:0, one launch (start us, length us, event | category | flops | bytes accessed | tf_op | source)
XLA Modules:
  0.0 53.8 jit_solution(16871887392450692570)
XLA Ops:
  0.6 1.1 %convert_element_type.68 = bf16[1,2,224,128]{3,2,1,0:T(8,128)(2,1)S(1)} convert(f32[1,2,224,128]{3,2,1,0:T(8,128)} %param.10) | non-fusion elementwise | flops 57344 | bytes 344064 | tf_op jit(solution)/shard_map/convert_element_type | solution.py:342
  1.8 4.1 %collective-permute-start.1 = (bf16[1,16,3584]{2,1,0:T(8,128)(2,1)S(1)}, bf16[1,16,3584]{2,1,0:T(8,128)(2,1)S(1)}, u32[]{:S(2)}, u32[]{:S(2)}) collective-permute-start(bf16[1,16,3584]{2,1,0:T(8,128)(2,1)S(1)} %bitcast.50), channel_id=1, source_target_pairs={{0,8},{1,9},{2,10},{3,11},{4,12},{5,13},{6,14},{7,15},{8,0},{9,1},... | collective-permute-start | bytes 344072 | tf_op jit(solution)/shard_map/ppermute | solution.py:25
  5.9 1.6 %collective-permute-start.3 = (bf16[1,16,3584]{2,1,0:T(8,128)(2,1)S(1)}, bf16[1,16,3584]{2,1,0:T(8,128)(2,1)S(1)}, u32[]{:S(2)}, u32[]{:S(2)}) collective-permute-start(bf16[1,16,3584]{2,1,0:T(8,128)(2,1)S(1)} %bitcast.51), channel_id=1, source_target_pairs={{0,4},{1,5},{2,6},{3,7},{4,0},{5,1},{6,2},{7,3},{8,12},{9,13},{10,... | collective-permute-start | bytes 344072 | tf_op jit(solution)/shard_map/ppermute | solution.py:25
  7.5 1.5 %collective-permute-start.2 = (bf16[1,16,3584]{2,1,0:T(8,128)(2,1)S(1)}, bf16[1,16,3584]{2,1,0:T(8,128)(2,1)S(1)}, u32[]{:S(2)}, u32[]{:S(2)}) collective-permute-start(bf16[1,16,3584]{2,1,0:T(8,128)(2,1)S(1)} %bitcast.52), channel_id=1, source_target_pairs={{0,2},{1,3},{2,0},{3,1},{4,6},{5,7},{6,4},{7,5},{8,10},{9,11},{10,... | collective-permute-start | bytes 344072 | tf_op jit(solution)/shard_map/ppermute | solution.py:25
  9.0 1.5 %collective-permute-start = (f32[2,224,128]{2,1,0:T(8,128)}, f32[2,224,128]{2,1,0:T(8,128)S(1)}, u32[]{:S(2)}, u32[]{:S(2)}) collective-permute-start(f32[2,224,128]{2,1,0:T(8,128)} %bitcast.44), channel_id=1, source_target_pairs={{0,16},{16,0},{1,17},{17,1},{2,18},{18,2},{3,19},{19,3},{4,20},{20... | collective-permute-start | bytes 688136 | tf_op jit(solution)/shard_map/ppermute | solution.py:25
  10.5 1.1 %collective-permute-done.1.refs_0_ = bf16[1,16,3584]{2,1,0:T(8,128)(2,1)S(1)} collective-permute-done((bf16[1,16,3584]{2,1,0:T(8,128)(2,1)S(1)}, bf16[1,16,3584]{2,1,0:T(8,128)(2,1)S(1)}, u32[]{:S(2)}, u32[]{:S(2)}) %collective-permute-start.1) | collective-permute-done | bytes 114720 | tf_op jit(solution)/shard_map/ppermute | solution.py:25
  11.6 0.2 collective-permute-done.3
  11.9 0.0 copy-start.2
  11.9 1.6 %collective-permute-start.5 = (bf16[2,16,3584]{2,1,0:T(8,128)(2,1)S(1)}, bf16[2,16,3584]{2,1,0:T(8,128)(2,1)S(1)}, u32[]{:S(2)}, u32[]{:S(2)}) collective-permute-start(bf16[2,16,3584]{2,1,0:T(8,128)(2,1)S(1)} %pad_maximum_fusion.1), channel_id=1, source_target_pairs={{0,2},{1,3},{2,0},{3,1},{4,6},{5,7},{6,4},{7,5},{8,10},{9,11},{10,... | collective-permute-start | bytes 688136 | tf_op jit(solution)/shard_map/ppermute | solution.py:25
  13.5 1.4 %collective-permute-start.4 = (bf16[1,16,3584]{2,1,0:T(8,128)(2,1)S(1)}, bf16[1,16,3584]{2,1,0:T(8,128)(2,1)S(1)}, u32[]{:S(2)}, u32[]{:S(2)}) collective-permute-start(bf16[1,16,3584]{2,1,0:T(8,128)(2,1)S(1)} %collective-permute-done.1.refs_0_), channel_id=1, source_target_pairs={{0,4},{1,5},{2,6},{3,7},{4,0},{5,1},{6,2},{7,3},{8,12},{9,13},{10,... | collective-permute-start | bytes 344072 | tf_op jit(solution)/shard_map/ppermute | solution.py:25
  14.9 0.0 collective-permute-done.2
  14.9 0.1 pad_maximum_fusion.refs_3_
  14.9 0.5 shard_map.103.refs_2_
  15.4 2.9 %collective-permute-done.4 = bf16[1,16,3584]{2,1,0:T(8,128)(2,1)S(1)} collective-permute-done((bf16[1,16,3584]{2,1,0:T(8,128)(2,1)S(1)}, bf16[1,16,3584]{2,1,0:T(8,128)(2,1)S(1)}, u32[]{:S(2)}, u32[]{:S(2)}) %collective-permute-start.4) | collective-permute-done | bytes 114720 | tf_op jit(solution)/shard_map/ppermute | solution.py:25
  18.3 0.5 collective-permute-start.6
  18.8 0.0 collective-permute-done.other
  18.8 4.3 %collective-permute-done.6 = bf16[1,16,3584]{2,1,0:T(8,128)(2,1)S(1)} collective-permute-done((bf16[1,16,3584]{2,1,0:T(8,128)(2,1)S(1)}, bf16[1,16,3584]{2,1,0:T(8,128)(2,1)S(1)}, u32[]{:S(2)}, u32[]{:S(2)}) %collective-permute-start.6) | collective-permute-done | bytes 114720 | tf_op jit(solution)/shard_map/ppermute | solution.py:25
  23.1 0.1 collective-permute-start.8
  23.2 1.8 %collective-permute-done.8.refs_6_ = bf16[4,16,3584]{2,1,0:T(8,128)(2,1)S(1)} collective-permute-done((bf16[4,16,3584]{2,1,0:T(8,128)(2,1)S(1)}, bf16[4,16,3584]{2,1,0:T(8,128)(2,1)S(1)}, u32[]{:S(2)}, u32[]{:S(2)}) %collective-permute-start.8) | collective-permute-done | bytes 458784 | tf_op jit(solution)/shard_map/ppermute | solution.py:25
  25.0 6.5 %shard_map.104 = (bf16[2,16,3584]{2,1,0:T(8,128)(2,1)S(1)}, bf16[2,16,3584]{2,1,0:T(8,128)(2,1)S(1)}, bf16[4,16,3584]{2,1,0:T(8,128)(2,1)S(1)}, bf16[2,16,3584]{...) custom-call(bf16[128,7168]{1,0:T(8,128)(2,1)S(1)} %bitcast.43, ...), custom_call_target="tpu_custom_call" | custom-call | tf_op jit(solution)/shard_map/pallas_call | solution.py:248
  31.4 0.2 collective-permute-start.9
  31.7 1.3 %collective-permute-done.9 = bf16[2,16,3584]{2,1,0:T(8,128)(2,1)S(1)} collective-permute-done((bf16[2,16,3584]{2,1,0:T(8,128)(2,1)S(1)}, bf16[2,16,3584]{2,1,0:T(8,128)(2,1)S(1)}, u32[]{:S(2)}, u32[]{:S(2)}) %collective-permute-start.9) | collective-permute-done | bytes 229408 | tf_op jit(solution)/shard_map/ppermute | solution.py:25
  33.0 0.1 add_convert_fusion.1
  33.1 0.2 collective-permute-start.10
  33.3 0.5 %collective-permute-start.13 = (bf16[16,3584]{1,0:T(8,128)(2,1)S(1)}, bf16[16,3584]{1,0:T(8,128)(2,1)S(1)}, u32[]{:S(2)}, u32[]{:S(2)}) collective-permute-start(bf16[16,3584]{1,0:T(8,128)(2,1)S(1)} %get-tuple-element.31), channel_id=1, source_target_pairs={{0,2},{1,3},{2,0},{3,1},{4,6},{5,7},{6,4},{7,5},{8,10},{9,11},{10,... | collective-permute-start | bytes 344072 | tf_op jit(solution)/shard_map/ppermute | solution.py:25
  33.8 0.1 collective-permute-start.12
  33.9 1.6 %collective-permute-start.15 = (bf16[16,3584]{1,0:T(8,128)(2,1)S(1)}, bf16[16,3584]{1,0:T(8,128)(2,1)S(1)}, u32[]{:S(2)}, u32[]{:S(2)}) collective-permute-start(bf16[16,3584]{1,0:T(8,128)(2,1)S(1)} %get-tuple-element.32), channel_id=1, source_target_pairs={{0,2},{1,3},{2,0},{3,1},{4,6},{5,7},{6,4},{7,5},{8,10},{9,11},{10,... | collective-permute-start | bytes 344072 | tf_op jit(solution)/shard_map/ppermute | solution.py:25
  35.5 0.0 collective-permute-done.10
  35.5 0.1 add_convert_fusion
  35.5 0.0 copy-start.1
  35.5 0.0 copy-start.4
  35.6 3.8 %collective-permute-done.13 = bf16[16,3584]{1,0:T(8,128)(2,1)S(1)} collective-permute-done((bf16[16,3584]{1,0:T(8,128)(2,1)S(1)}, bf16[16,3584]{1,0:T(8,128)(2,1)S(1)}, u32[]{:S(2)}, u32[]{:S(2)}) %collective-permute-start.13) | collective-permute-done | bytes 114720 | tf_op jit(solution)/shard_map/ppermute | solution.py:25
  39.3 0.0 collective-permute-done.12
  39.3 0.1 convert_add_fusion
  39.4 0.0 copy-start.5
  39.4 0.0 copy-start.6
  39.5 1.4 %collective-permute-start.14 = (bf16[16,3584]{1,0:T(8,128)(2,1)S(1)}, bf16[16,3584]{1,0:T(8,128)(2,1)S(1)}, u32[]{:S(2)}, u32[]{:S(2)}) collective-permute-start(bf16[16,3584]{1,0:T(8,128)(2,1)S(1)} %fusion.7), channel_id=1, source_target_pairs={{0,4},{1,5},{2,6},{3,7},{4,0},{5,1},{6,2},{7,3},{8,12},{9,13},{10,... | collective-permute-start | bytes 344072 | tf_op jit(solution)/shard_map/ppermute | solution.py:25
  41.6 0.6 %collective-permute-start.11 = (bf16[2,16,3584]{2,1,0:T(8,128)(2,1)S(1)}, bf16[2,16,3584]{2,1,0:T(8,128)(2,1)S(1)}, u32[]{:S(2)}, u32[]{:S(2)}) collective-permute-start(bf16[2,16,3584]{2,1,0:T(8,128)(2,1)S(1)} %add_convert_fusion), channel_id=1, source_target_pairs={{0,2},{1,3},{2,0},{3,1},{4,6},{5,7},{6,4},{7,5},{8,10},{9,11},{10,... | collective-permute-start | bytes 688136 | tf_op jit(solution)/shard_map/ppermute | solution.py:25
  42.2 0.0 collective-permute-done.15
  42.2 2.2 %collective-permute-done.14 = bf16[16,3584]{1,0:T(8,128)(2,1)S(1)} collective-permute-done((bf16[16,3584]{1,0:T(8,128)(2,1)S(1)}, bf16[16,3584]{1,0:T(8,128)(2,1)S(1)}, u32[]{:S(2)}, u32[]{:S(2)}) %collective-permute-start.14) | collective-permute-done | bytes 114720 | tf_op jit(solution)/shard_map/ppermute | solution.py:25
  44.4 2.1 %collective-permute-start.16 = (bf16[16,3584]{1,0:T(8,128)(2,1)S(1)}, bf16[16,3584]{1,0:T(8,128)(2,1)S(1)}, u32[]{:S(2)}, u32[]{:S(2)}) collective-permute-start(bf16[16,3584]{1,0:T(8,128)(2,1)S(1)} %fusion.5), channel_id=1, source_target_pairs={{0,8},{1,9},{2,10},{3,11},{4,12},{5,13},{6,14},{7,15},{8,0},{9,1},... | collective-permute-start | bytes 344072 | tf_op jit(solution)/shard_map/ppermute | solution.py:25
  46.4 1.4 %collective-permute-done.11 = bf16[2,16,3584]{2,1,0:T(8,128)(2,1)S(1)} collective-permute-done((bf16[2,16,3584]{2,1,0:T(8,128)(2,1)S(1)}, bf16[2,16,3584]{2,1,0:T(8,128)(2,1)S(1)}, u32[]{:S(2)}, u32[]{:S(2)}) %collective-permute-start.11) | collective-permute-done | bytes 229408 | tf_op jit(solution)/shard_map/ppermute | solution.py:25
  47.9 0.7 %collective-permute-start.17 = (bf16[16,3584]{1,0:T(8,128)(2,1)S(1)}, bf16[16,3584]{1,0:T(8,128)(2,1)S(1)}, u32[]{:S(2)}, u32[]{:S(2)}) collective-permute-start(bf16[16,3584]{1,0:T(8,128)(2,1)S(1)} %fusion.8), channel_id=1, source_target_pairs={{0,4},{1,5},{2,6},{3,7},{4,0},{5,1},{6,2},{7,3},{8,12},{9,13},{10,... | collective-permute-start | bytes 344072 | tf_op jit(solution)/shard_map/ppermute | solution.py:25
  48.7 0.7 %multiply_subtract_fusion = (f32[224,128]{1,0:T(8,128)S(1)}, f32[224,128]{1,0:T(8,128)}) fusion(f32[224,128]{1,0:T(8,128)S(1)} %copy-done.4, f32[224,128]{1,0:T(8,128)S(1)} %shard_map.105, f32[224,128]{1,0:T(8,128)S(1)} %copy-done.7), kind=kLoop, calls=%fused_computation.21 | loop fusion | flops 200704 | bytes 573440 | tf_op jit(solution)/shard_map/sub | solution.py:377
  49.3 3.4 %collective-permute-done.17 = bf16[16,3584]{1,0:T(8,128)(2,1)S(1)} collective-permute-done((bf16[16,3584]{1,0:T(8,128)(2,1)S(1)}, bf16[16,3584]{1,0:T(8,128)(2,1)S(1)}, u32[]{:S(2)}, u32[]{:S(2)}) %collective-permute-start.17) | collective-permute-done | bytes 114720 | tf_op jit(solution)/shard_map/ppermute | solution.py:25
  52.7 0.0 collective-permute-done.16
  52.7 0.1 fusion.1.refs_5_
  52.8 1.0 %shard_map.106 = f32[2,224,128]{2,1,0:T(8,128)} custom-call(s32[1]{0:T(128)S(6)} %copy.16.fragment.refs_0_, f32[2,224,128]{2,1,0:T(8,128)S(1)} %bitcast.46, f32[2,224,128]{2,1,0:T(8,128)S(1)} %bitcast.48, f32[2,224,128]{2,1,0:T(8,128)S(1)} %bitcast.49, f32[224,128]{1,0:T(8,128)S(1)} %get-tuple-element.29.refs_4_, f32[16,3584]{1,0:T(8,128)S(1)} %fusion.1.refs_5_), custom_call_target="tpu_custom_call" | custom-call | tf_op jit(solution)/shard_map/pallas_call | solution.py:317
  (25 shorter events, 0.3 us)
Async XLA Ops:
  0.6 14.3 %copy-start = (bf16[1,128,7168]{2,1,0:T(8,128)(2,1)S(1)}, bf16[1,128,7168]{2,1,0:T(8,128)(2,1)}, u32[]{:S(2)}) copy-start(bf16[1,128,7168]{2,1,0:T(8,128)(2,1)} %param.8) | copy-start | bytes 5505028
  1.8 9.8 %collective-permute-start.1 = (bf16[1,16,3584]{2,1,0:T(8,128)(2,1)S(1)}, bf16[1,16,3584]{2,1,0:T(8,128)(2,1)S(1)}, u32[]{:S(2)}, u32[]{:S(2)}) collective-permute-start(bf16[1,16,3584]{2,1,0:T(8,128)(2,1)S(1)} %bitcast.50), channel_id=1, source_target_pairs={{0,8},{1,9},{2,10},{3,11},{4,12},{5,13},{6,14},{7,15},{8,0},{9,1},... | collective-permute-start | bytes 344072 | tf_op jit(solution)/shard_map/ppermute | solution.py:25
  5.9 5.9 %collective-permute-start.3 = (bf16[1,16,3584]{2,1,0:T(8,128)(2,1)S(1)}, bf16[1,16,3584]{2,1,0:T(8,128)(2,1)S(1)}, u32[]{:S(2)}, u32[]{:S(2)}) collective-permute-start(bf16[1,16,3584]{2,1,0:T(8,128)(2,1)S(1)} %bitcast.51), channel_id=1, source_target_pairs={{0,4},{1,5},{2,6},{3,7},{4,0},{5,1},{6,2},{7,3},{8,12},{9,13},{10,... | collective-permute-start | bytes 344072 | tf_op jit(solution)/shard_map/ppermute | solution.py:25
  7.5 7.4 %collective-permute-start.2 = (bf16[1,16,3584]{2,1,0:T(8,128)(2,1)S(1)}, bf16[1,16,3584]{2,1,0:T(8,128)(2,1)S(1)}, u32[]{:S(2)}, u32[]{:S(2)}) collective-permute-start(bf16[1,16,3584]{2,1,0:T(8,128)(2,1)S(1)} %bitcast.52), channel_id=1, source_target_pairs={{0,2},{1,3},{2,0},{3,1},{4,6},{5,7},{6,4},{7,5},{8,10},{9,11},{10,... | collective-permute-start | bytes 344072 | tf_op jit(solution)/shard_map/ppermute | solution.py:25
  9.0 9.8 %collective-permute-start = (f32[2,224,128]{2,1,0:T(8,128)}, f32[2,224,128]{2,1,0:T(8,128)S(1)}, u32[]{:S(2)}, u32[]{:S(2)}) collective-permute-start(f32[2,224,128]{2,1,0:T(8,128)} %bitcast.44), channel_id=1, source_target_pairs={{0,16},{16,0},{1,17},{17,1},{2,18},{18,2},{3,19},{19,3},{4,20},{20... | collective-permute-start | bytes 688136 | tf_op jit(solution)/shard_map/ppermute | solution.py:25
  11.9 13.1 %copy-start.2 = (bf16[1,128,7168]{2,1,0:T(8,128)(2,1)S(1)}, bf16[1,128,7168]{2,1,0:T(8,128)(2,1)}, u32[]{:S(2)}) copy-start(bf16[1,128,7168]{2,1,0:T(8,128)(2,1)} %param.9) | copy-start | bytes 5505028
  11.9 6.9 %collective-permute-start.5 = (bf16[2,16,3584]{2,1,0:T(8,128)(2,1)S(1)}, bf16[2,16,3584]{2,1,0:T(8,128)(2,1)S(1)}, u32[]{:S(2)}, u32[]{:S(2)}) collective-permute-start(bf16[2,16,3584]{2,1,0:T(8,128)(2,1)S(1)} %pad_maximum_fusion.1), channel_id=1, source_target_pairs={{0,2},{1,3},{2,0},{3,1},{4,6},{5,7},{6,4},{7,5},{8,10},{9,11},{10,... | collective-permute-start | bytes 688136 | tf_op jit(solution)/shard_map/ppermute | solution.py:25
  13.5 4.8 %collective-permute-start.4 = (bf16[1,16,3584]{2,1,0:T(8,128)(2,1)S(1)}, bf16[1,16,3584]{2,1,0:T(8,128)(2,1)S(1)}, u32[]{:S(2)}, u32[]{:S(2)}) collective-permute-start(bf16[1,16,3584]{2,1,0:T(8,128)(2,1)S(1)} %collective-permute-done.1.refs_0_), channel_id=1, source_target_pairs={{0,4},{1,5},{2,6},{3,7},{4,0},{5,1},{6,2},{7,3},{8,12},{9,13},{10,... | collective-permute-start | bytes 344072 | tf_op jit(solution)/shard_map/ppermute | solution.py:25
  18.3 4.8 %collective-permute-start.6 = (bf16[1,16,3584]{2,1,0:T(8,128)(2,1)S(1)}, bf16[1,16,3584]{2,1,0:T(8,128)(2,1)S(1)}, u32[]{:S(2)}, u32[]{:S(2)}) collective-permute-start(bf16[1,16,3584]{2,1,0:T(8,128)(2,1)S(1)} %collective-permute-done.4), channel_id=1, source_target_pairs={{0,2},{1,3},{2,0},{3,1},{4,6},{5,7},{6,4},{7,5},{8,10},{9,11},{10,... | collective-permute-start | bytes 344072 | tf_op jit(solution)/shard_map/ppermute | solution.py:25
  18.8 4.4 %collective-permute-start.7 = (bf16[4,16,3584]{2,1,0:T(8,128)(2,1)S(1)}, bf16[4,16,3584]{2,1,0:T(8,128)(2,1)S(1)}, u32[]{:S(2)}, u32[]{:S(2)}) collective-permute-start(bf16[4,16,3584]{2,1,0:T(8,128)(2,1)S(1)} %pad_maximum_fusion.refs_3_), channel_id=1, source_target_pairs={{0,1},{1,0},{2,3},{3,2},{4,5},{5,4},{6,7},{7,6},{8,9},{9,8},{10,11... | collective-permute-start | bytes 1376264 | tf_op jit(solution)/shard_map/ppermute | solution.py:25
  23.1 1.9 %collective-permute-start.8 = (bf16[4,16,3584]{2,1,0:T(8,128)(2,1)S(1)}, bf16[4,16,3584]{2,1,0:T(8,128)(2,1)S(1)}, u32[]{:S(2)}, u32[]{:S(2)}) collective-permute-start(bf16[4,16,3584]{2,1,0:T(8,128)(2,1)S(1)} %constant_dynamic-update-slice_fusion.refs_4_), channel_id=1, source_target_pairs={{0,1},{1,0},{2,3},{3,2},{4,5},{5,4},{6,7},{7,6},{8,9},{9,8},{10,11... | collective-permute-start | bytes 1376264 | tf_op jit(solution)/shard_map/ppermute | solution.py:25
  31.4 1.6 %collective-permute-start.9 = (bf16[2,16,3584]{2,1,0:T(8,128)(2,1)S(1)}, bf16[2,16,3584]{2,1,0:T(8,128)(2,1)S(1)}, u32[]{:S(2)}, u32[]{:S(2)}) collective-permute-start(bf16[2,16,3584]{2,1,0:T(8,128)(2,1)S(1)} %get-tuple-element.22), channel_id=1, source_target_pairs={{0,1},{1,0},{2,3},{3,2},{4,5},{5,4},{6,7},{7,6},{8,9},{9,8},{10,11... | collective-permute-start | bytes 688136 | tf_op jit(solution)/shard_map/ppermute | solution.py:25
  33.1 2.4 %collective-permute-start.10 = (bf16[2,16,3584]{2,1,0:T(8,128)(2,1)S(1)}, bf16[2,16,3584]{2,1,0:T(8,128)(2,1)S(1)}, u32[]{:S(2)}, u32[]{:S(2)}) collective-permute-start(bf16[2,16,3584]{2,1,0:T(8,128)(2,1)S(1)} %get-tuple-element.23), channel_id=1, source_target_pairs={{0,1},{1,0},{2,3},{3,2},{4,5},{5,4},{6,7},{7,6},{8,9},{9,8},{10,11... | collective-permute-start | bytes 688136 | tf_op jit(solution)/shard_map/ppermute | solution.py:25
  33.3 6.0 %collective-permute-start.13 = (bf16[16,3584]{1,0:T(8,128)(2,1)S(1)}, bf16[16,3584]{1,0:T(8,128)(2,1)S(1)}, u32[]{:S(2)}, u32[]{:S(2)}) collective-permute-start(bf16[16,3584]{1,0:T(8,128)(2,1)S(1)} %get-tuple-element.31), channel_id=1, source_target_pairs={{0,2},{1,3},{2,0},{3,1},{4,6},{5,7},{6,4},{7,5},{8,10},{9,11},{10,... | collective-permute-start | bytes 344072 | tf_op jit(solution)/shard_map/ppermute | solution.py:25
  33.8 5.5 %collective-permute-start.12 = (bf16[4,16,3584]{2,1,0:T(8,128)(2,1)S(1)}, bf16[4,16,3584]{2,1,0:T(8,128)(2,1)S(1)}, u32[]{:S(2)}, u32[]{:S(2)}) collective-permute-start(bf16[4,16,3584]{2,1,0:T(8,128)(2,1)S(1)} %get-tuple-element.25), channel_id=1, source_target_pairs={{0,1},{1,0},{2,3},{3,2},{4,5},{5,4},{6,7},{7,6},{8,9},{9,8},{10,11... | collective-permute-start | bytes 1376264 | tf_op jit(solution)/shard_map/ppermute | solution.py:25
  33.9 8.3 %collective-permute-start.15 = (bf16[16,3584]{1,0:T(8,128)(2,1)S(1)}, bf16[16,3584]{1,0:T(8,128)(2,1)S(1)}, u32[]{:S(2)}, u32[]{:S(2)}) collective-permute-start(bf16[16,3584]{1,0:T(8,128)(2,1)S(1)} %get-tuple-element.32), channel_id=1, source_target_pairs={{0,2},{1,3},{2,0},{3,1},{4,6},{5,7},{6,4},{7,5},{8,10},{9,11},{10,... | collective-permute-start | bytes 344072 | tf_op jit(solution)/shard_map/ppermute | solution.py:25
  35.5 13.1 %copy-start.1 = (f32[1,2,224,128]{3,2,1,0:T(8,128)S(1)}, f32[1,2,224,128]{3,2,1,0:T(8,128)}, u32[]{:S(2)}) copy-start(f32[1,2,224,128]{3,2,1,0:T(8,128)} %param.10) | copy-start | bytes 688132
  35.5 13.1 %copy-start.4 = (f32[224,128]{1,0:T(8,128)S(1)}, f32[224,128]{1,0:T(8,128)}, u32[]{:S(2)}) copy-start(f32[224,128]{1,0:T(8,128)} %anchor.1) | copy-start | bytes 344068
  39.3 9.3 %copy-start.7 = (f32[224,128]{1,0:T(8,128)S(1)}, f32[224,128]{1,0:T(8,128)}, u32[]{:S(2)}) copy-start(f32[224,128]{1,0:T(8,128)} %param.14) | copy-start | bytes 344068
  39.4 13.4 %copy-start.5 = (f32[1,2,224,128]{3,2,1,0:T(8,128)S(1)}, f32[1,2,224,128]{3,2,1,0:T(8,128)}, u32[]{:S(2)}) copy-start(f32[1,2,224,128]{3,2,1,0:T(8,128)} %param.11) | copy-start | bytes 688132
  39.4 13.4 %copy-start.6 = (f32[1,2,224,128]{3,2,1,0:T(8,128)S(1)}, f32[1,2,224,128]{3,2,1,0:T(8,128)}, u32[]{:S(2)}) copy-start(f32[1,2,224,128]{3,2,1,0:T(8,128)} %param.12) | copy-start | bytes 688132
  39.5 4.9 %collective-permute-start.14 = (bf16[16,3584]{1,0:T(8,128)(2,1)S(1)}, bf16[16,3584]{1,0:T(8,128)(2,1)S(1)}, u32[]{:S(2)}, u32[]{:S(2)}) collective-permute-start(bf16[16,3584]{1,0:T(8,128)(2,1)S(1)} %fusion.7), channel_id=1, source_target_pairs={{0,4},{1,5},{2,6},{3,7},{4,0},{5,1},{6,2},{7,3},{8,12},{9,13},{10,... | collective-permute-start | bytes 344072 | tf_op jit(solution)/shard_map/ppermute | solution.py:25
  41.6 6.3 %collective-permute-start.11 = (bf16[2,16,3584]{2,1,0:T(8,128)(2,1)S(1)}, bf16[2,16,3584]{2,1,0:T(8,128)(2,1)S(1)}, u32[]{:S(2)}, u32[]{:S(2)}) collective-permute-start(bf16[2,16,3584]{2,1,0:T(8,128)(2,1)S(1)} %add_convert_fusion), channel_id=1, source_target_pairs={{0,2},{1,3},{2,0},{3,1},{4,6},{5,7},{6,4},{7,5},{8,10},{9,11},{10,... | collective-permute-start | bytes 688136 | tf_op jit(solution)/shard_map/ppermute | solution.py:25
  44.4 8.4 %collective-permute-start.16 = (bf16[16,3584]{1,0:T(8,128)(2,1)S(1)}, bf16[16,3584]{1,0:T(8,128)(2,1)S(1)}, u32[]{:S(2)}, u32[]{:S(2)}) collective-permute-start(bf16[16,3584]{1,0:T(8,128)(2,1)S(1)} %fusion.5), channel_id=1, source_target_pairs={{0,8},{1,9},{2,10},{3,11},{4,12},{5,13},{6,14},{7,15},{8,0},{9,1},... | collective-permute-start | bytes 344072 | tf_op jit(solution)/shard_map/ppermute | solution.py:25
  47.9 4.9 %collective-permute-start.17 = (bf16[16,3584]{1,0:T(8,128)(2,1)S(1)}, bf16[16,3584]{1,0:T(8,128)(2,1)S(1)}, u32[]{:S(2)}, u32[]{:S(2)}) collective-permute-start(bf16[16,3584]{1,0:T(8,128)(2,1)S(1)} %fusion.8), channel_id=1, source_target_pairs={{0,4},{1,5},{2,6},{3,7},{4,0},{5,1},{6,2},{7,3},{8,12},{9,13},{10,... | collective-permute-start | bytes 344072 | tf_op jit(solution)/shard_map/ppermute | solution.py:25
  49.3 4.5 %copy-start.3 = (f32[224,128]{1,0:T(8,128)}, f32[224,128]{1,0:T(8,128)S(1)}, u32[]{:S(2)}) copy-start(f32[224,128]{1,0:T(8,128)S(1)} %get-tuple-element.29.refs_4_) | copy-start | bytes 344068
